TPU v7x, 32 devices: a whole 2x2x4 slice. The times are simulated.
32 devices in a mesh: groups: 2 (over x), rows: 16 (over z, y, core).
Axes of the slice: x: 2, y: 2, z: 4, core: 2. Of those that a mesh axis runs over, the one named last changes fastest.
Arguments:
- points: bfloat16 [64, 32768], P(None, ('groups', 'rows')), parts along dimension 1, may hold values from -12 to 12
- landmarks: bfloat16 [64, 2048], P(None, 'groups'), parts along dimension 1, may hold values from -12 to 12
- chol: float32 [2048, 1024], P('groups'), parts along dimension 0
- ridge: float32 [2], P('groups'), parts along dimension 0, may hold values from 0.5 to 2
- solution: float32 [8, 32768], P(None, ('groups', 'rows')), parts along dimension 1, may hold values from -6 to 6
- residual: float32 [8, 32768], P(None, ('groups', 'rows')), parts along dimension 1, may hold values from -6 to 6
- direction: float32 [8, 32768], P(None, ('groups', 'rows')), parts along dimension 1, may hold values from -6 to 6
- rz_prev: float32 [16], P('groups'), parts along dimension 0, may hold values from 8192 to 32768
Outputs:
- solution_new: float32 [8, 32768], P(None, ('groups', 'rows')), parts along dimension 1
- residual_new: float32 [8, 32768], P(None, ('groups', 'rows')), parts along dimension 1
- direction_new: float32 [8, 32768], P(None, ('groups', 'rows')), parts along dimension 1
- inner_new: float32 [16], P('groups'), parts along dimension 0
There are 2 independent parts, one for each index of `groups`. A program takes and returns all parts, laid end to end along the dimension named above; each array names one. Nothing has to cross between parts.
All inputs are finite; a program needn't handle non-finite values.
Results may differ from a plain program's by a relative error of at most 0.0064.
Values may be sent and summed in bfloat16 or wider, within the bound.
No kernel may reach another device: no remote copies, remote signals or barrier semaphores. Data moves between devices by JAX's collectives and lax.ppermute only.
A program may use at most 64 MiB of HBM per device.

v0:
```python
import math

import jax
import jax.numpy as jnp
from jax import lax
from jax.sharding import PartitionSpec as P


def square_norms(features):
    wide = features.astype(jnp.float32)
    return jnp.sum(wide * wide, axis=0)


def kernel_block(row_points, row_norms, col_points, col_norms):
    scale = 0.5 / row_points.shape[0]
    cross = lax.dot_general(
        row_points, col_points, (((0,), (0,)), ((), ())), preferred_element_type=jnp.float32
    )
    dist = row_norms[:, None] + col_norms[None, :] - 2.0 * cross
    return jnp.exp(-scale * dist)


def split_blocks(values, block_len):
    blocks = values.shape[-1] // block_len
    return jnp.moveaxis(values.reshape(values.shape[:-1] + (blocks, block_len)), -2, 0)


def row_products(own_points, own_norms, col_points, col_dirs):
    block_len = math.gcd(col_points.shape[1], 4096)
    point_blocks = split_blocks(col_points, block_len)
    dir_blocks = split_blocks(col_dirs, block_len)

    def step_block(running, inputs):
        block_points, block_dirs = inputs
        kernel_tile = kernel_block(
            own_points, own_norms, block_points, square_norms(block_points)
        ).astype(jnp.bfloat16)
        added = lax.dot_general(
            block_dirs, kernel_tile, (((1,), (1,)), ((), ())), preferred_element_type=jnp.float32
        )
        return (running + added, None)

    start_value = jnp.zeros((col_dirs.shape[0], own_points.shape[1]), jnp.float32)
    summed, _ = lax.scan(step_block, start_value, (point_blocks, dir_blocks))
    return summed


def precondition(residual, landmark_kernel, projection, chol, ridge_value):
    coeffs = jax.scipy.linalg.cho_solve((chol, True), projection.T)
    precond = (
        residual - jnp.dot(coeffs.T, landmark_kernel.T, precision=lax.Precision.HIGHEST)
    ) / ridge_value
    return (coeffs, precond)


def local(points, landmarks, chol, ridge, solution, residual, direction, rz_prev):
    ridge_value = ridge[0]
    norms = square_norms(points)
    landmark_kernel = kernel_block(points, norms, landmarks, square_norms(landmarks))
    partial_proj = jnp.dot(residual, landmark_kernel, precision=lax.Precision.HIGHEST)
    projection = lax.psum(partial_proj, "rows")
    coeffs, precond = precondition(residual, landmark_kernel, projection, chol, ridge_value)
    inner_new = lax.psum(jnp.sum(precond * residual, axis=1), "rows")
    direction_new = precond + (inner_new / rz_prev)[:, None] * direction
    direction_low = direction_new.astype(jnp.bfloat16)
    kernel_part = row_products(
        points,
        norms,
        lax.all_gather(points, "rows", axis=1, tiled=True),
        lax.all_gather(direction_low, "rows", axis=1, tiled=True),
    )
    image = kernel_part + ridge_value * direction_new
    curvature = lax.psum(jnp.sum(direction_new * image, axis=1), "rows")
    alpha = inner_new / curvature
    solution_new = solution + alpha[:, None] * direction_new
    residual_new = residual - alpha[:, None] * image
    return (solution_new, residual_new, direction_new, inner_new)


def solution(mesh):
    in_specs = (
        P(None, ("groups", "rows")),
        P(None, "groups"),
        P("groups", None),
        P("groups"),
        P(None, ("groups", "rows")),
        P(None, ("groups", "rows")),
        P(None, ("groups", "rows")),
        P("groups"),
    )
    out_specs = (
        P(None, ("groups", "rows")),
        P(None, ("groups", "rows")),
        P(None, ("groups", "rows")),
        P("groups"),
    )
    return jax.shard_map(local, mesh=mesh, in_specs=in_specs, out_specs=out_specs, check_vma=False)
```

profile of v0, /device:TPU:0, one launch (start us, length us, event | category | flops | bytes accessed | tf_op | source)
XLA Modules:
  0.0 328.2 jit_solution(10841898238312821311)
XLA Ops:
  9.0 3.8 %fusion.100 = f32[1024,1024]{1,0:T(8,128)} fusion(bf16[64,1024]{1,0:T(8,128)(2,1)} %param.10, bf16[64,1024]{1,0:T(8,128)(2,1)} %param.11), kind=kOutput, calls=%fused_computation.178 | convolution fusion | flops 134217728 | bytes 4456448 | tf_op jit(solution)/shard_map/dot_general | solution.py:16
  12.9 2.4 fusion.15
  15.4 23.2 %while.12 = (s32[]{:T(128)}, f32[1024,1024]{1,0:T(8,128)}, s32[8,2]{0,1:T(2,128)S(1)}, f32[8,128,128]{2,1,0:T(8,128)S(1)}, s32[]{:T(128)}) while((s32[]{:T(128)}, f32[1024,1024]{1,0:T(8,128)}, s32[8,2]{0,1:T(2,128)S(1)}, f32[8,128,128]{2,1,0:T(8,128)S(1)}, s32[]{:T(128)}) %tuple.65), condition=%wide.while_cond, body=%wide.while_body.sunk | while | flops 2 | bytes 131181 | solution.py:49
  16.0 2.3 bitcast_dynamic-update-slice_fusion.2
  18.9 2.3 bitcast_dynamic-update-slice_fusion.2
  21.8 2.3 bitcast_dynamic-update-slice_fusion.2
  24.7 2.3 bitcast_dynamic-update-slice_fusion.2
  27.6 2.3 bitcast_dynamic-update-slice_fusion.2
  30.5 2.3 bitcast_dynamic-update-slice_fusion.2
  33.4 2.3 bitcast_dynamic-update-slice_fusion.2
  38.6 78.6 %custom-call.7 = f32[8,128,128]{1,2,0:T(8,128)S(1)} custom-call(f32[8,128,128]{2,1,0:T(8,128)S(1)} %get-tuple-element.44), custom_call_target="InvertDiagBlocksLowerTriangular" | custom-call | tf_op jit(solution)/shard_map/jit(_cho_solve)/triangular_solve | solution.py:49
  117.2 5.3 %fusion.17 = f32[1024,8]{0,1:T(8,128)S(1)} fusion(f32[8,1024]{1,0:T(8,128)S(1)} %copy-done.6, f32[1024,1024]{1,0:T(8,128)} %fusion.100, f32[1024]{0:T(1024)S(1)} %multiply_reduce_fusion.1, f32[1024]{0:T(1024)S(1)} %multiply_reduce_fusion.2), kind=kOutput, calls=%fused_computation.20 | convolution fusion | flops 104857600 | bytes 4268032 | tf_op jit(solution)/shard_map/dot_general | solution.py:60
  122.5 63.0 %psum.21 = f32[1024,8]{0,1:T(8,128)S(1)} all-reduce(f32[1024,8]{0,1:T(8,128)S(1)} %fusion.17), channel_id=1, replica_groups=mesh['groups'=2,'rows'=16] {'rows'}, use_global_device_ids=true, to_apply=%region_2.0 | all-reduce | flops 8192 | bytes 65536 | tf_op jit(solution)/shard_map/psum | solution.py:61
  207.3 4.2 %multiply_reduce_fusion.4 = (f32[8]{0:T(128)S(1)}, f32[8,1024]{1,0:T(8,128)S(1)}) fusion(f32[8,1024]{1,0:T(8,128)S(1)} %copy-done.6, f32[]{:T(128)} %bitcast.125, f32[1024,8]{0,1:T(8,128)S(1)} %constant_dynamic-update-slice_fusion.36, f32[1024,1024]{1,0:T(8,128)S(1)} %copy-done.1, f32[1024]{0:T(1024)S(1)} %multiply_reduce_fusion.1, ...), kind=kOutput, calls=%fused_computation.133 | convolution fusion | flops 104890360 | bytes 4300836 | tf_op jit(solution)/shard_map/dot_general | solution.py:51
  211.5 29.5 %psum.22 = f32[8]{0:T(128)S(1)} all-reduce(f32[8]{0:T(128)S(1)} %get-tuple-element.129), channel_id=1, replica_groups=mesh['groups'=2,'rows'=16] {'rows'}, use_global_device_ids=true, to_apply=%region_4.5 | all-reduce | flops 8 | bytes 64 | tf_op jit(solution)/shard_map/psum | solution.py:63
  241.1 18.1 %all_gather.6 = bf16[8,16384]{1,0:T(8,128)(2,1)S(1)} all-gather(bf16[8,1024]{1,0:T(8,128)(2,1)S(1)} %get-tuple-element.92), channel_id=1, replica_groups=mesh['groups'=2,'rows'=16] {'rows'}, dimensions={1}, use_global_device_ids=true | all-gather | bytes 278528 | tf_op jit(solution)/shard_map/all_gather | solution.py:70
  259.3 4.5 %reshape.69 = bf16[64,4,4096]{2,1,0:T(4,128)(2,1)} reshape(bf16[64,16384]{1,0:T(8,128)(2,1)} %all-gather.2.cloned.1.call-done) | data formatting | bytes 4194304 | tf_op jit(solution)/shard_map/reshape | solution.py:25
  263.8 2.7 copy.12
  266.6 22.5 %while.13 = (s32[]{:T(128)}, f32[8,1024]{1,0:T(8,128)S(1)}, bf16[4,8,4096]{2,1,0:T(8,128)(2,1)S(1)}, f32[1024]{0:T(1024)S(1)}, bf16[4,64,4096]{2,1,0:T(8,128)(2,...) while((s32[]{:T(128)}, f32[8,1024]{1,0:T(8,128)S(1)}, ...), condition=%wide.region_7.8_spmd.clone, body=%wide.region_5.7_spmd.clone.sunk | while | flops 625750016 | bytes 1348707 | solution.py:44
  266.7 5.5 %fusion.138 = f32[8,1024]{1,0:T(8,128)S(1)} fusion(bf16[64,1024]{1,0:T(8,128)(2,1)S(1)} %get-tuple-element.233, f32[4096]{0:T(1024)S(1)} %multiply_reduce_fusion.6, f32[1024]{0:T(1024)S(1)} %get-tuple-element.231, bf16[4,64,4096]{2,1,0:T(8,128)(2,1)S(1)} %get-tuple-element.232, s32[]{:T(128)} %get-tuple-element.220, ...), kind=kOutput, calls=%fused_computation.7.clone.1 | convolution fusion | flops 624967680 | bytes 807937 | tf_op jit(solution)/shard_map/while/body/eval_jaxpr/dot_general | solution.py:38
  272.3 5.5 %fusion.138 = f32[8,1024]{1,0:T(8,128)S(1)} fusion(bf16[64,1024]{1,0:T(8,128)(2,1)S(1)} %get-tuple-element.233, f32[4096]{0:T(1024)S(1)} %multiply_reduce_fusion.6, f32[1024]{0:T(1024)S(1)} %get-tuple-element.231, bf16[4,64,4096]{2,1,0:T(8,128)(2,1)S(1)} %get-tuple-element.232, s32[]{:T(128)} %get-tuple-element.220, ...), kind=kOutput, calls=%fused_computation.7.clone.1 | convolution fusion | flops 624967680 | bytes 807937 | tf_op jit(solution)/shard_map/while/body/eval_jaxpr/dot_general | solution.py:38
  278.0 5.5 %fusion.138 = f32[8,1024]{1,0:T(8,128)S(1)} fusion(bf16[64,1024]{1,0:T(8,128)(2,1)S(1)} %get-tuple-element.233, f32[4096]{0:T(1024)S(1)} %multiply_reduce_fusion.6, f32[1024]{0:T(1024)S(1)} %get-tuple-element.231, bf16[4,64,4096]{2,1,0:T(8,128)(2,1)S(1)} %get-tuple-element.232, s32[]{:T(128)} %get-tuple-element.220, ...), kind=kOutput, calls=%fused_computation.7.clone.1 | convolution fusion | flops 624967680 | bytes 807937 | tf_op jit(solution)/shard_map/while/body/eval_jaxpr/dot_general | solution.py:38
  283.6 5.5 %fusion.138 = f32[8,1024]{1,0:T(8,128)S(1)} fusion(bf16[64,1024]{1,0:T(8,128)(2,1)S(1)} %get-tuple-element.233, f32[4096]{0:T(1024)S(1)} %multiply_reduce_fusion.6, f32[1024]{0:T(1024)S(1)} %get-tuple-element.231, bf16[4,64,4096]{2,1,0:T(8,128)(2,1)S(1)} %get-tuple-element.232, s32[]{:T(128)} %get-tuple-element.220, ...), kind=kOutput, calls=%fused_computation.7.clone.1 | convolution fusion | flops 624967680 | bytes 807937 | tf_op jit(solution)/shard_map/while/body/eval_jaxpr/dot_general | solution.py:38
  289.2 31.4 %psum.23 = f32[8]{0:T(128)S(1)} all-reduce(f32[8]{0:T(128)S(1)} %multiply_reduce_fusion.3), channel_id=1, replica_groups=mesh['groups'=2,'rows'=16] {'rows'}, use_global_device_ids=true, to_apply=%region_9.10 | all-reduce | flops 8 | bytes 64 | tf_op jit(solution)/shard_map/psum | solution.py:73
  (107 shorter events, 31.5 us)
Async XLA Ops:
  7.2 5.7 %copy-start.3 = (bf16[64,1024]{1,0:T(8,128)(2,1)S(1)}, bf16[64,1024]{1,0:T(8,128)(2,1)}, u32[]{:S(2)}) copy-start(bf16[64,1024]{1,0:T(8,128)(2,1)} %param.11) | copy-start | bytes 393220
  7.2 252.1 %all-gather.2.cloned.1.call-start = ((), (), s32[]{:S(2)}) async-start(), calls=%async_computation | async-start | bytes 2228224 | tf_op jit(solution)/shard_map/all_gather | solution.py:69
  7.9 5.0 %copy-start = (f32[1024,1024]{1,0:T(8,128)S(1)}, f32[1024,1024]{1,0:T(8,128)}, u32[]{:S(2)}) copy-start(f32[1024,1024]{1,0:T(8,128)} %param.12) | copy-start | bytes 12582916
  12.9 104.3 %copy-start.6 = (f32[8,1024]{1,0:T(8,128)S(1)}, f32[8,1024]{1,0:T(8,128)}, u32[]{:S(2)}) copy-start(f32[8,1024]{1,0:T(8,128)} %param.15) | copy-start | bytes 98308
  185.5 21.8 %copy-start.1 = (f32[1024,1024]{1,0:T(8,128)S(1)}, f32[1024,1024]{1,0:T(8,128)}, u32[]{:S(2)}) copy-start(f32[1024,1024]{1,0:T(8,128)} %fusion.100) | copy-start | bytes 12582916
  195.9 45.1 %copy-start.8 = (f32[8]{0:T(128)S(1)}, f32[8]{0:T(128)}, u32[]{:S(2)}) copy-start(f32[8]{0:T(128)} %param.17) | copy-start | bytes 100
  195.9 45.1 %copy-start.5 = (f32[8,1024]{1,0:T(8,128)S(1)}, f32[8,1024]{1,0:T(8,128)}, u32[]{:S(2)}) copy-start(f32[8,1024]{1,0:T(8,128)} %param.16) | copy-start | bytes 98308
  241.0 79.6 %copy-start.9 = (f32[8]{0:T(128)}, f32[8]{0:T(128)S(1)}, u32[]{:S(2)}) copy-start(f32[8]{0:T(128)S(1)} %psum.22) | copy-start | bytes 100
  241.1 79.5 %copy-start.4 = (f32[8,1024]{1,0:T(8,128)}, f32[8,1024]{1,0:T(8,128)S(1)}, u32[]{:S(2)}) copy-start(f32[8,1024]{1,0:T(8,128)S(1)} %get-tuple-element.93) | copy-start | bytes 98308
  259.3 7.3 %copy-start.2 = (bf16[64,1024]{1,0:T(8,128)(2,1)S(1)}, bf16[64,1024]{1,0:T(8,128)(2,1)}, u32[]{:S(2)}) copy-start(bf16[64,1024]{1,0:T(8,128)(2,1)} %param.10) | copy-start | bytes 393220
  266.5 54.1 %copy-start.7 = (f32[8,1024]{1,0:T(8,128)S(1)}, f32[8,1024]{1,0:T(8,128)}, u32[]{:S(2)}) copy-start(f32[8,1024]{1,0:T(8,128)} %param.14) | copy-start | bytes 98308
Sparse Core Ops, SparseCore 0:
  10.2 44.1 all-gather.1
where the time goes:
time: 329 us; the launch traced here: 328 us
  blocking collectives  142 us (43%)
  other arithmetic  83.7 us (25%)
  matrix products  56 us (17%)
  local copies, waits for them, and re-layouts  30.6 us (9%)
  between operations  15 us (5%)
    another operation x3, other arithmetic, precondition(): coeffs = jax.scipy.linalg.cho_solve((chol, True), projection.T)  81 us
    psum x1, blocking collectives, local(): projection = lax.psum(partial_proj, 'rows')  63 us
    psum x1, blocking collectives, local(): curvature = lax.psum(jnp.sum(direction_new * image, axis=1), 'rows')  31.4 us
    psum x1, blocking collectives, local(): inner_new = lax.psum(jnp.sum(precond * residual, axis=1), 'rows')  29.5 us
    another operation x24, local copies, waits for them, and re-layouts  23.1 us
    dot_general x4, matrix products, step_block(): lax.dot_general(block_dirs, kernel_tile, (((1,), (1,)), ((), ())), prefer...  21.8 us
    another operation x30, matrix products, precondition(): coeffs = jax.scipy.linalg.cho_solve((chol, True), projection.T)  20.8 us
    all_gather x1, blocking collectives, local(): lax.all_gather(direction_low, 'rows', axis=1, tiled=True)  18.1 us
  transfers between devices with their start and end apart: 1, of which 0 were waited for; matrix products, arithmetic and copies ran while one was open for 43% of the time, Pallas kernels for 0%

commit v1 on v0

v1 whole, which is shorter than its diff:
```python
import functools
import math

import jax
import jax.numpy as jnp
from jax import lax
from jax.experimental import pallas as pl
from jax.experimental.pallas import tpu as pltpu
from jax.sharding import PartitionSpec as P

F32 = jnp.float32
B16 = jnp.bfloat16
LOG2E = 1.4426950408889634
PAD = 10
VMEM = pl.BlockSpec(memory_space=pltpu.VMEM)
SMEM = pl.BlockSpec(memory_space=pltpu.SMEM)
HIGH = lax.Precision.HIGHEST


def dot(a, b, ca, cb, precision=None):
    return lax.dot_general(
        a, b, (((ca,), (cb,)), ((), ())), precision=precision, preferred_element_type=F32
    )


def split3(x):
    hi = x.astype(B16)
    rest = x - hi.astype(F32)
    mid = rest.astype(B16)
    low = (rest - mid.astype(F32)).astype(B16)
    return hi, mid, low


def norm_rows(features):
    wide = features.astype(F32)
    return split3(jnp.sum(wide * wide, axis=0, keepdims=True))


def rows_side(features):
    n = features.shape[1]
    hi, mid, low = norm_rows(features)
    return jnp.concatenate(
        [features, hi, mid, low, jnp.ones((3, n), B16), jnp.zeros((PAD, n), B16)], axis=0
    )


def cols_side(features):
    n = features.shape[1]
    hi, mid, low = norm_rows(features)
    return jnp.concatenate(
        [features * 2, -jnp.ones((3, n), B16), -hi, -mid, -low, jnp.zeros((PAD, n), B16)], axis=0
    )


def gauss(exponent, features):
    return jnp.exp2(exponent * (0.5 * LOG2E / features))


def cross_kernel(pts_ref, marks_ref, res_ref, cross_ref, proj_ref):
    feat = pts_ref.shape[0]
    land = marks_ref.shape[1]
    exponent = dot(rows_side(pts_ref[...]), cols_side(marks_ref[...]), 0, 0)
    cross = gauss(exponent, feat)
    cross_ref[...] = cross
    res = res_ref[...]
    proj_ref[:, :land] = dot(res, cross, 1, 0, HIGH)
    squares = jnp.sum(res * res, axis=1, keepdims=True)
    proj_ref[:, land:] = jnp.broadcast_to(squares, (res.shape[0], proj_ref.shape[1] - land))


def inverse_kernel(chol_ref, inv_ref):
    size = chol_ref.shape[0]
    base = math.gcd(size, 128)
    row = lax.broadcasted_iota(jnp.int32, (base, base), 0)
    col = lax.broadcasted_iota(jnp.int32, (base, base), 1)
    eye = row == col
    count = size // base
    inv_ref[...] = jnp.zeros((size, size), F32)
    blocks, inverses = [], []
    for b in range(count):
        lo = b * base
        block = chol_ref[lo : lo + base, lo : lo + base]
        diag = jnp.where(eye, block, 0.0)
        inv_col = 1.0 / jnp.sum(diag, axis=1, keepdims=True)
        inv_row = 1.0 / jnp.sum(diag, axis=0, keepdims=True)
        pair = (row // 2 == col // 2) & (row > col)
        scaled = inv_col * inv_row
        x = jnp.where(eye, inv_col, 0.0) - jnp.where(pair, block * scaled, 0.0)
        blocks.append(block)
        inverses.append(x)
    step = 2
    while step < base:
        mask = (row // (2 * step) == col // (2 * step)) & (row // step > col // step)
        tmp = [dot(jnp.where(mask, blocks[b], 0.0), inverses[b], 1, 0, HIGH) for b in range(count)]
        inverses = [inverses[b] - dot(inverses[b], tmp[b], 1, 0, HIGH) for b in range(count)]
        step *= 2
    for b in range(count):
        lo = b * base
        inv_ref[lo : lo + base, lo : lo + base] = inverses[b]
    step = base
    while step < size:
        tmp = []
        for lo in range(0, size, 2 * step):
            mid, end = lo + step, lo + 2 * step
            tmp.append(dot(chol_ref[mid:end, lo:mid], inv_ref[lo:mid, lo:mid], 1, 0, HIGH))
        for i, lo in enumerate(range(0, size, 2 * step)):
            mid, end = lo + step, lo + 2 * step
            inv_ref[mid:end, lo:mid] = -dot(inv_ref[mid:end, mid:end], tmp[i], 1, 0, HIGH)
        step *= 2


def direction_kernel(ridge_ref, rz_ref, proj_ref, inv_ref, cross_ref, res_ref, dir_ref, new_ref, low_ref, inner_ref):
    land = cross_ref.shape[1]
    ridge = ridge_ref[0]
    proj = proj_ref[:, :land]
    squares = proj_ref[:, land : land + 1]
    half = dot(proj, inv_ref[...], 1, 1, HIGH)
    coeffs = dot(half, inv_ref[...], 1, 0, HIGH)
    inner = (squares - jnp.sum(proj * coeffs, axis=1, keepdims=True)) / ridge
    precond = (res_ref[...] - dot(coeffs, cross_ref[...], 1, 1, HIGH)) / ridge
    new = precond + (inner / rz_ref[...]) * dir_ref[...]
    new_ref[...] = new
    low_ref[...] = new.astype(B16)
    inner_ref[...] = inner


def image_kernel(points_at, ridge_ref, own_ref, pts_ref, low_ref, new_ref, image_ref, curv_ref, lhs_ref):
    feat, width = own_ref.shape
    blocks = len(points_at)
    group = math.gcd(blocks, 4)
    lhs_ref[...] = cols_side(own_ref[...])
    total = jnp.zeros(image_ref.shape, F32)
    for first in range(0, blocks, group):
        pts = jnp.concatenate(
            [pts_ref[:, points_at[b] * width : (points_at[b] + 1) * width] for b in range(first, first + group)],
            axis=1,
        )
        kernel = gauss(dot(rows_side(pts), lhs_ref[...], 0, 0), feat).astype(B16)
        total = total + dot(low_ref[:, first * width : (first + group) * width], kernel, 1, 0)
    new = new_ref[...]
    image = total + ridge_ref[0] * new
    image_ref[...] = image
    curv = jnp.sum(new * image, axis=1, keepdims=True)
    curv_ref[...] = jnp.broadcast_to(curv, curv_ref.shape)


def exchange(x, mask, count):
    return lax.ppermute(x, "rows", [(i, i ^ mask) for i in range(count)])


def stages(count):
    out, bit = [], 1
    while bit < count:
        if 2 * bit < count:
            out.append([bit, 2 * bit, 3 * bit])
            bit *= 4
        else:
            out.append([bit])
            bit *= 2
    return out


def all_sum(x, count):
    for masks in stages(count):
        parts = [x] + [exchange(x, m, count) for m in masks]
        while len(parts) > 1:
            parts = [parts[i] + parts[i + 1] for i in range(0, len(parts), 2)]
        x = parts[0]
    return x


def gather(x, stage_list, count):
    order = [0]
    for masks in stage_list:
        x = jnp.concatenate([x] + [exchange(x, m, count) for m in masks], axis=1)
        order = order + [m ^ o for m in masks for o in order]
    return x, order


def call(kernel, out, *args, smem=(), scratch=(), name=None, **cost):
    return pl.pallas_call(
        kernel,
        out_shape=out,
        in_specs=[SMEM if i in smem else VMEM for i in range(len(args))],
        out_specs=jax.tree.map(lambda _: VMEM, out),
        scratch_shapes=list(scratch),
        compiler_params=pltpu.CompilerParams(vmem_limit_bytes=56 * 2**20),
        name=name,
    )(*args)


def local(count, points, landmarks, chol, ridge, solution, residual, direction, rz_prev):
    outs, width = residual.shape
    land = landmarks.shape[1]
    shape = jax.ShapeDtypeStruct
    *lower, top = stages(count)
    point_stages = [top] + [[masks[i]] for masks in reversed(lower) for i in range(len(masks) // 2, -1, -1)]
    all_points, point_order = gather(points, point_stages, count)
    cross, partial = call(
        cross_kernel,
        (shape((width, land), F32), shape((outs, land + 128), F32)),
        points, landmarks, residual, name="cross",
    )
    inverse = call(inverse_kernel, shape((land, land), F32), chol, name="inverse")
    proj = all_sum(partial, count)
    new, low, inner = call(
        direction_kernel,
        (shape((outs, width), F32), shape((outs, width), B16), shape((outs, 1), F32)),
        ridge, rz_prev[:, None], proj, inverse, cross, residual, direction, smem=(0,), name="direction",
    )
    all_low, low_order = gather(low, stages(count), count)
    points_at = [point_order.index(m) for m in low_order]
    image, curv = call(
        functools.partial(image_kernel, points_at),
        (shape((outs, width), F32), shape((outs, 128), F32)),
        ridge, points, all_points, all_low, new, smem=(0,),
        scratch=(pltpu.VMEM((points.shape[0] + 6 + PAD, width), B16),), name="image",
    )
    curv = all_sum(curv, count)
    inner_new = inner[:, 0]
    alpha = inner / curv[:, :1]
    return (solution + alpha * new, residual - alpha * image, new, inner_new)


def solution(mesh):
    count = mesh.shape["rows"]
    vec = P(None, ("groups", "rows"))
    in_specs = (vec, P(None, "groups"), P("groups", None), P("groups"), vec, vec, vec, P("groups"))
    out_specs = (vec, vec, vec, P("groups"))
    return jax.shard_map(
        functools.partial(local, count), mesh=mesh, in_specs=in_specs, out_specs=out_specs, check_vma=False
    )
```

time: 329 us -> 104 us (0.32)
  blocking collectives: 142 us -> 0 us
  other arithmetic: 83.7 us -> 4.22 us
  matrix products: 56 us -> 0 us
  Pallas kernels: 0 us -> 47.9 us
  starting transfers between devices: 0.04 us -> 28.1 us
  local copies, waits for them, and re-layouts: 30.6 us -> 4.62 us
  waiting for transfers between devices: 0.68 us -> 17.1 us
  between operations: 15 us -> 1.48 us
    psum x3 -> x0, blocking collectives: 124 us -> none  [the longest x1 63 us: local(): projection = lax.psum(partial_proj, 'rows')]
    another operation x3 -> x0, other arithmetic: 81 us -> none  [precondition(): coeffs = jax.scipy.linalg.cho_solve((chol, True), projection.T)]
    pallas_call x0 -> x4, Pallas kernels: none -> 47.9 us  [call(): pl.pallas_call(kernel, out_shape=out, in_specs=[SMEM if i in smem else VM...]
    dot_general x7 -> x0, matrix products: 35.2 us -> none  [the longest x4 21.8 us: step_block(): lax.dot_general(block_dirs, kernel_tile, (((1,), (1,)), ((), ())), prefer...]
    ppermute x0 -> x23, starting transfers between devices: none -> 28.1 us  [exchange(): return lax.ppermute(x, 'rows', [(i, i ^ mask) for i in range(count)])]
    another operation x29 -> x0, local copies, waits for them, and re-layouts: 23.1 us -> none
    another operation x30 -> x0, matrix products: 20.8 us -> none  [precondition(): coeffs = jax.scipy.linalg.cho_solve((chol, True), projection.T)]
    all_gather x1 -> x0, blocking collectives: 18.1 us -> none  [local(): lax.all_gather(direction_low, 'rows', axis=1, tiled=True)]
  transfers between devices with their start and end apart: 1 -> 23, of which waited for: 0 -> 8; matrix products, arithmetic and copies ran while one was open for 43% -> 4% of each run, Pallas kernels for 0% -> 27%
where the time goes in v1:
time: 104 us; the launch traced here: 103 us
  Pallas kernels  47.9 us (46%)
  starting transfers between devices  28.1 us (27%)
  waiting for transfers between devices  17.1 us (16%)
  local copies, waits for them, and re-layouts  4.62 us (4%)
  other arithmetic  4.22 us (4%)
  between operations  1.48 us (1%)
    pallas_call x4, Pallas kernels, call(): pl.pallas_call(kernel, out_shape=out, in_specs=[SMEM if i in smem else VM...  47.9 us
    ppermute x23, starting transfers between devices, exchange(): return lax.ppermute(x, 'rows', [(i, i ^ mask) for i in range(count)])  28.1 us
    ppermute x23, waiting for transfers between devices, exchange(): return lax.ppermute(x, 'rows', [(i, i ^ mask) for i in range(count)])  17.1 us
    unnamed x27, local copies, waits for them, and re-layouts  3.77 us
    add x4, other arithmetic, all_sum(): parts = [parts[i] + parts[i + 1] for i in range(0, len(parts), 2)]  2.1 us
  transfers between devices with their start and end apart: 23, of which 8 were waited for; matrix products, arithmetic and copies ran while one was open for 4% of the time, Pallas kernels for 27%

profile of v1, /device:TPU:0, one launch (start us, length us, event | category | flops | bytes accessed | tf_op | source)
XLA Modules:
  0.0 103.4 jit_solution(16442499225698768008)
XLA Ops:
  0.6 4.2 %cross.1 = (f32[1024,1024]{1,0:T(8,128)}, f32[8,1152]{1,0:T(8,128)}) custom-call(bf16[64,1024]{1,0:T(8,128)(2,1)} %own_ref.1, bf16[64,1024]{1,0:T(8,128)(2,1)} %marks_ref.1, f32[8,1024]{1,0:T(8,128)} %res_ref.3), custom_call_target="tpu_custom_call" | custom-call | tf_op jit(solution)/shard_map/cross/pallas_call | solution.py:181
  5.3 2.5 %collective-permute-start.1 = (f32[8,1152]{1,0:T(8,128)}, f32[8,1152]{1,0:T(8,128)S(1)}, u32[]{:S(2)}, u32[]{:S(2)}) collective-permute-start(f32[8,1152]{1,0:T(8,128)} %get-tuple-element.11), channel_id=1, source_target_pairs={{0,2},{1,3},{2,0},{3,1},{4,6},{5,7},{6,4},{7,5},{8,10},{9,11},{10,... | collective-permute-start | bytes 110600 | tf_op jit(solution)/shard_map/ppermute | solution.py:148
  7.9 1.8 %collective-permute-start.6 = (bf16[64,1024]{1,0:T(8,128)(2,1)}, bf16[64,1024]{1,0:T(8,128)(2,1)S(1)}, u32[]{:S(2)}, u32[]{:S(2)}) collective-permute-start(bf16[64,1024]{1,0:T(8,128)(2,1)} %own_ref.1), channel_id=1, source_target_pairs={{0,4},{1,5},{2,6},{3,7},{4,0},{5,1},{6,2},{7,3},{8,12},{9,13},{10,... | collective-permute-start | bytes 393224 | tf_op jit(solution)/shard_map/ppermute | solution.py:148
  9.7 2.6 %collective-permute-start.7 = (bf16[64,1024]{1,0:T(8,128)(2,1)}, bf16[64,1024]{1,0:T(8,128)(2,1)S(1)}, u32[]{:S(2)}, u32[]{:S(2)}) collective-permute-start(bf16[64,1024]{1,0:T(8,128)(2,1)} %own_ref.1), channel_id=1, source_target_pairs={{0,8},{1,9},{2,10},{3,11},{4,12},{5,13},{6,14},{7,15},{8,0},{9,1},... | collective-permute-start | bytes 393224 | tf_op jit(solution)/shard_map/ppermute | solution.py:148
  13.8 2.6 %collective-permute-start.4 = (f32[8,1152]{1,0:T(8,128)S(1)}, f32[8,1152]{1,0:T(8,128)S(1)}, u32[]{:S(2)}, u32[]{:S(2)}) collective-permute-start(f32[8,1152]{1,0:T(8,128)S(1)} %add_add_fusion.1), channel_id=1, source_target_pairs={{0,8},{1,9},{2,10},{3,11},{4,12},{5,13},{6,14},{7,15},{8,0},{9,1},... | collective-permute-start | bytes 110600 | tf_op jit(solution)/shard_map/ppermute | solution.py:148
  16.4 1.1 %collective-permute-start.5 = (f32[8,1152]{1,0:T(8,128)S(1)}, f32[8,1152]{1,0:T(8,128)S(1)}, u32[]{:S(2)}, u32[]{:S(2)}) collective-permute-start(f32[8,1152]{1,0:T(8,128)S(1)} %add_add_fusion.1), channel_id=1, source_target_pairs={{0,12},{1,13},{2,14},{3,15},{4,8},{5,9},{6,10},{7,11},{8,4},{9,5},... | collective-permute-start | bytes 110600 | tf_op jit(solution)/shard_map/ppermute | solution.py:148
  17.5 1.6 %constant_dynamic-update-slice_fusion.4 = (bf16[64,8192]{1,0:T(8,128)(2,1)}, bf16[64,16384]{1,0:T(8,128)(2,1)S(1)}) fusion(bf16[64,1024]{1,0:T(8,128)(2,1)} %own_ref.1), kind=kLoop, calls=%fused_computation.5 | loop fusion | bytes 393216
  19.8 15.1 %inverse.1.inv_ref = f32[1024,1024]{1,0:T(8,128)} custom-call(f32[1024,1024]{1,0:T(8,128)} %chol_ref.1), custom_call_target="tpu_custom_call" | custom-call | tf_op jit(solution)/shard_map/inverse/pallas_call | solution.py:181
  35.6 2.7 %collective-permute-start.8 = (bf16[64,1024]{1,0:T(8,128)(2,1)S(1)}, bf16[64,1024]{1,0:T(8,128)(2,1)S(1)}, u32[]{:S(2)}, u32[]{:S(2)}) collective-permute-start(bf16[64,1024]{1,0:T(8,128)(2,1)S(1)} %copy-done.1), channel_id=1, source_target_pairs={{0,12},{1,13},{2,14},{3,15},{4,8},{5,9},{6,10},{7,11},{8,4},{9,5},... | collective-permute-start | bytes 393224 | tf_op jit(solution)/shard_map/ppermute | solution.py:148
  38.9 12.6 %direction.1 = (f32[8,1024]{1,0:T(8,128)}, bf16[8,1024]{1,0:T(8,128)(2,1)}, f32[8,1]{1,0:T(8,128)}) custom-call(f32[1]{0:T(128)S(6)} %copy.32.ridge_ref, f32[8,1]{1,0:T(8,128)} %copy.13.rz_ref, f32[8,1152]{1,0:T(8,128)} %add_add_fusion.proj_ref, f32[1024,1024]{1,0:T(8,128)} %inverse.1.inv_ref, f32[1024,1024]{1,0:T(8,128)} %get-tuple-element.12.cross_ref, ...), custom_call_target="tpu_custom_call" | custom-call | tf_op jit(solution)/shard_map/direction/pallas_call | solution.py:181
  54.1 1.0 collective-permute-start.9
  55.1 1.0 %collective-permute-done.12 = bf16[8,1024]{1,0:T(8,128)(2,1)S(1)} collective-permute-done((bf16[8,1024]{1,0:T(8,128)(2,1)}, bf16[8,1024]{1,0:T(8,128)(2,1)S(1)}, u32[]{:S(2)}, u32[]{:S(2)}) %collective-permute-start.12) | collective-permute-done | bytes 16416 | tf_op jit(solution)/shard_map/ppermute | solution.py:148
  56.5 2.3 %collective-permute-start.15 = (bf16[8,4096]{1,0:T(8,128)(2,1)S(1)}, bf16[8,4096]{1,0:T(8,128)(2,1)S(1)}, u32[]{:S(2)}, u32[]{:S(2)}) collective-permute-start(bf16[8,4096]{1,0:T(8,128)(2,1)S(1)} %get-tuple-element.30), channel_id=1, source_target_pairs={{0,8},{1,9},{2,10},{3,11},{4,12},{5,13},{6,14},{7,15},{8,0},{9,1},... | collective-permute-start | bytes 196616 | tf_op jit(solution)/shard_map/ppermute | solution.py:148
  58.8 2.1 %collective-permute-start.16 = (bf16[8,4096]{1,0:T(8,128)(2,1)S(1)}, bf16[8,4096]{1,0:T(8,128)(2,1)S(1)}, u32[]{:S(2)}, u32[]{:S(2)}) collective-permute-start(bf16[8,4096]{1,0:T(8,128)(2,1)S(1)} %get-tuple-element.30), channel_id=1, source_target_pairs={{0,12},{1,13},{2,14},{3,15},{4,8},{5,9},{6,10},{7,11},{8,4},{9,5},... | collective-permute-start | bytes 196616 | tf_op jit(solution)/shard_map/ppermute | solution.py:148
  61.0 7.3 %collective-permute-done.9 = bf16[64,4096]{1,0:T(8,128)(2,1)S(1)} collective-permute-done((bf16[64,4096]{1,0:T(8,128)(2,1)S(1)}, bf16[64,4096]{1,0:T(8,128)(2,1)S(1)}, u32[]{:S(2)}, u32[]{:S(2)}) %collective-permute-start.9) | collective-permute-done | bytes 524320 | tf_op jit(solution)/shard_map/ppermute | solution.py:148
  68.6 2.6 %collective-permute-done.10 = bf16[64,8192]{1,0:T(8,128)(2,1)S(1)} collective-permute-done((bf16[64,8192]{1,0:T(8,128)(2,1)S(1)}, bf16[64,8192]{1,0:T(8,128)(2,1)S(1)}, u32[]{:S(2)}, u32[]{:S(2)}) %collective-permute-start.10) | collective-permute-done | bytes 1048608 | tf_op jit(solution)/shard_map/ppermute | solution.py:148
  71.2 1.3 %copy-done = bf16[64,16384]{1,0:T(8,128)(2,1)} copy-done((bf16[64,16384]{1,0:T(8,128)(2,1)}, bf16[64,16384]{1,0:T(8,128)(2,1)S(1)}, u32[]{:S(2)}) %copy-start) | copy-done | bytes 2097176
  72.6 16.0 %image.1 = (f32[8,1024]{1,0:T(8,128)}, f32[8,128]{1,0:T(8,128)}) custom-call(f32[1]{0:T(128)S(6)} %copy.32.ridge_ref, bf16[64,1024]{1,0:T(8,128)(2,1)} %own_ref.1, bf16[64,16384]{1,0:T(8,128)(2,1)} %copy-done, bf16[8,16384]{1,0:T(8,128)(2,1)} %copy-done.2, f32[8,1024]{1,0:T(8,128)} %get-tuple-element.9.new_ref), custom_call_target="tpu_custom_call" | custom-call | tf_op jit(solution)/shard_map/image/pallas_call | solution.py:181
  88.7 1.0 collective-permute-start.18
  90.5 2.1 %collective-permute-done.18 = f32[8,128]{1,0:T(8,128)S(1)} collective-permute-done((f32[8,128]{1,0:T(8,128)}, f32[8,128]{1,0:T(8,128)S(1)}, u32[]{:S(2)}, u32[]{:S(2)}) %collective-permute-start.18) | collective-permute-done | bytes 4128 | tf_op jit(solution)/shard_map/ppermute | solution.py:148
  93.6 2.3 %collective-permute-start.21 = (f32[8,128]{1,0:T(8,128)S(1)}, f32[8,128]{1,0:T(8,128)S(1)}, u32[]{:S(2)}, u32[]{:S(2)}) collective-permute-start(f32[8,128]{1,0:T(8,128)S(1)} %add_add_fusion.3), channel_id=1, source_target_pairs={{0,8},{1,9},{2,10},{3,11},{4,12},{5,13},{6,14},{7,15},{8,0},{9,1},... | collective-permute-start | bytes 12296 | tf_op jit(solution)/shard_map/ppermute | solution.py:148
  95.9 2.1 %collective-permute-start.22 = (f32[8,128]{1,0:T(8,128)S(1)}, f32[8,128]{1,0:T(8,128)S(1)}, u32[]{:S(2)}, u32[]{:S(2)}) collective-permute-start(f32[8,128]{1,0:T(8,128)S(1)} %add_add_fusion.3), channel_id=1, source_target_pairs={{0,12},{1,13},{2,14},{3,15},{4,8},{5,9},{6,10},{7,11},{8,4},{9,5},... | collective-permute-start | bytes 12296 | tf_op jit(solution)/shard_map/ppermute | solution.py:148
  98.1 3.2 %collective-permute-done.22 = f32[8,128]{1,0:T(8,128)S(1)} collective-permute-done((f32[8,128]{1,0:T(8,128)S(1)}, f32[8,128]{1,0:T(8,128)S(1)}, u32[]{:S(2)}, u32[]{:S(2)}) %collective-permute-start.22) | collective-permute-done | bytes 4128 | tf_op jit(solution)/shard_map/ppermute | solution.py:148
  102.0 1.5 %multiply_subtract_fusion = (f32[8,1024]{1,0:T(8,128)}, f32[8,1024]{1,0:T(8,128)}) fusion(f32[8,1024]{1,0:T(8,128)S(1)} %copy-done.3, f32[8,1024]{1,0:T(8,128)} %get-tuple-element.17, f32[8]{0:T(128)S(1)} %get-tuple-element.19, f32[8,1024]{1,0:T(8,128)S(1)} %copy-done.5, f32[8,1024]{1,0:T(8,128)S(1)} %copy-done.4), kind=kLoop, calls=%fused_computation.25 | loop fusion | flops 32768 | bytes 196640 | tf_op jit(solution)/shard_map/sub | solution.py:222
  (65 shorter events, 9.5 us)
Async XLA Ops:
  4.8 7.5 %collective-permute-start = (f32[8,1152]{1,0:T(8,128)}, f32[8,1152]{1,0:T(8,128)S(1)}, u32[]{:S(2)}, u32[]{:S(2)}) collective-permute-start(f32[8,1152]{1,0:T(8,128)} %get-tuple-element.11), channel_id=1, source_target_pairs={{0,1},{1,0},{2,3},{3,2},{4,5},{5,4},{6,7},{7,6},{8,9},{9,8},{10,11... | collective-permute-start | bytes 110600 | tf_op jit(solution)/shard_map/ppermute | solution.py:148
  5.3 7.0 %collective-permute-start.1 = (f32[8,1152]{1,0:T(8,128)}, f32[8,1152]{1,0:T(8,128)S(1)}, u32[]{:S(2)}, u32[]{:S(2)}) collective-permute-start(f32[8,1152]{1,0:T(8,128)} %get-tuple-element.11), channel_id=1, source_target_pairs={{0,2},{1,3},{2,0},{3,1},{4,6},{5,7},{6,4},{7,5},{8,10},{9,11},{10,... | collective-permute-start | bytes 110600 | tf_op jit(solution)/shard_map/ppermute | solution.py:148
  7.8 4.5 %collective-permute-start.2 = (f32[8,1152]{1,0:T(8,128)}, f32[8,1152]{1,0:T(8,128)S(1)}, u32[]{:S(2)}, u32[]{:S(2)}) collective-permute-start(f32[8,1152]{1,0:T(8,128)} %get-tuple-element.11), channel_id=1, source_target_pairs={{0,3},{1,2},{2,1},{3,0},{4,7},{5,6},{6,5},{7,4},{8,11},{9,10},{10,... | collective-permute-start | bytes 110600 | tf_op jit(solution)/shard_map/ppermute | solution.py:148
  7.9 46.2 %collective-permute-start.6 = (bf16[64,1024]{1,0:T(8,128)(2,1)}, bf16[64,1024]{1,0:T(8,128)(2,1)S(1)}, u32[]{:S(2)}, u32[]{:S(2)}) collective-permute-start(bf16[64,1024]{1,0:T(8,128)(2,1)} %own_ref.1), channel_id=1, source_target_pairs={{0,4},{1,5},{2,6},{3,7},{4,0},{5,1},{6,2},{7,3},{8,12},{9,13},{10,... | collective-permute-start | bytes 393224 | tf_op jit(solution)/shard_map/ppermute | solution.py:148
  9.7 44.4 %collective-permute-start.7 = (bf16[64,1024]{1,0:T(8,128)(2,1)}, bf16[64,1024]{1,0:T(8,128)(2,1)S(1)}, u32[]{:S(2)}, u32[]{:S(2)}) collective-permute-start(bf16[64,1024]{1,0:T(8,128)(2,1)} %own_ref.1), channel_id=1, source_target_pairs={{0,8},{1,9},{2,10},{3,11},{4,12},{5,13},{6,14},{7,15},{8,0},{9,1},... | collective-permute-start | bytes 393224 | tf_op jit(solution)/shard_map/ppermute | solution.py:148
  13.1 22.5 %collective-permute-start.3 = (f32[8,1152]{1,0:T(8,128)S(1)}, f32[8,1152]{1,0:T(8,128)S(1)}, u32[]{:S(2)}, u32[]{:S(2)}) collective-permute-start(f32[8,1152]{1,0:T(8,128)S(1)} %add_add_fusion.1), channel_id=1, source_target_pairs={{0,4},{1,5},{2,6},{3,7},{4,0},{5,1},{6,2},{7,3},{8,12},{9,13},{10,... | collective-permute-start | bytes 110600 | tf_op jit(solution)/shard_map/ppermute | solution.py:148
  13.8 24.5 %collective-permute-start.4 = (f32[8,1152]{1,0:T(8,128)S(1)}, f32[8,1152]{1,0:T(8,128)S(1)}, u32[]{:S(2)}, u32[]{:S(2)}) collective-permute-start(f32[8,1152]{1,0:T(8,128)S(1)} %add_add_fusion.1), channel_id=1, source_target_pairs={{0,8},{1,9},{2,10},{3,11},{4,12},{5,13},{6,14},{7,15},{8,0},{9,1},... | collective-permute-start | bytes 110600 | tf_op jit(solution)/shard_map/ppermute | solution.py:148
  16.4 21.9 %collective-permute-start.5 = (f32[8,1152]{1,0:T(8,128)S(1)}, f32[8,1152]{1,0:T(8,128)S(1)}, u32[]{:S(2)}, u32[]{:S(2)}) collective-permute-start(f32[8,1152]{1,0:T(8,128)S(1)} %add_add_fusion.1), channel_id=1, source_target_pairs={{0,12},{1,13},{2,14},{3,15},{4,8},{5,9},{6,10},{7,11},{8,4},{9,5},... | collective-permute-start | bytes 110600 | tf_op jit(solution)/shard_map/ppermute | solution.py:148
  35.6 18.5 %collective-permute-start.8 = (bf16[64,1024]{1,0:T(8,128)(2,1)S(1)}, bf16[64,1024]{1,0:T(8,128)(2,1)S(1)}, u32[]{:S(2)}, u32[]{:S(2)}) collective-permute-start(bf16[64,1024]{1,0:T(8,128)(2,1)S(1)} %copy-done.1), channel_id=1, source_target_pairs={{0,12},{1,13},{2,14},{3,15},{4,8},{5,9},{6,10},{7,11},{8,4},{9,5},... | collective-permute-start | bytes 393224 | tf_op jit(solution)/shard_map/ppermute | solution.py:148
  51.5 1.6 %collective-permute-start.11 = (bf16[8,1024]{1,0:T(8,128)(2,1)}, bf16[8,1024]{1,0:T(8,128)(2,1)S(1)}, u32[]{:S(2)}, u32[]{:S(2)}) collective-permute-start(bf16[8,1024]{1,0:T(8,128)(2,1)} %get-tuple-element.14), channel_id=1, source_target_pairs={{0,1},{1,0},{2,3},{3,2},{4,5},{5,4},{6,7},{7,6},{8,9},{9,8},{10,11... | collective-permute-start | bytes 49160 | tf_op jit(solution)/shard_map/ppermute | solution.py:148
  52.2 3.9 %collective-permute-start.12 = (bf16[8,1024]{1,0:T(8,128)(2,1)}, bf16[8,1024]{1,0:T(8,128)(2,1)S(1)}, u32[]{:S(2)}, u32[]{:S(2)}) collective-permute-start(bf16[8,1024]{1,0:T(8,128)(2,1)} %get-tuple-element.14), channel_id=1, source_target_pairs={{0,2},{1,3},{2,0},{3,1},{4,6},{5,7},{6,4},{7,5},{8,10},{9,11},{10,... | collective-permute-start | bytes 49160 | tf_op jit(solution)/shard_map/ppermute | solution.py:148
  53.1 3.4 %collective-permute-start.13 = (bf16[8,1024]{1,0:T(8,128)(2,1)}, bf16[8,1024]{1,0:T(8,128)(2,1)S(1)}, u32[]{:S(2)}, u32[]{:S(2)}) collective-permute-start(bf16[8,1024]{1,0:T(8,128)(2,1)} %get-tuple-element.14), channel_id=1, source_target_pairs={{0,3},{1,2},{2,1},{3,0},{4,7},{5,6},{6,5},{7,4},{8,11},{9,10},{10,... | collective-permute-start | bytes 49160 | tf_op jit(solution)/shard_map/ppermute | solution.py:148
  54.1 14.2 %collective-permute-start.9 = (bf16[64,4096]{1,0:T(8,128)(2,1)S(1)}, bf16[64,4096]{1,0:T(8,128)(2,1)S(1)}, u32[]{:S(2)}, u32[]{:S(2)}) collective-permute-start(bf16[64,4096]{1,0:T(8,128)(2,1)S(1)} %pad_maximum_fusion), channel_id=1, source_target_pairs={{0,2},{1,3},{2,0},{3,1},{4,6},{5,7},{6,4},{7,5},{8,10},{9,11},{10,... | collective-permute-start | bytes 1572872 | tf_op jit(solution)/shard_map/ppermute | solution.py:148
  56.5 12.0 %collective-permute-start.14 = (bf16[8,4096]{1,0:T(8,128)(2,1)S(1)}, bf16[8,4096]{1,0:T(8,128)(2,1)S(1)}, u32[]{:S(2)}, u32[]{:S(2)}) collective-permute-start(bf16[8,4096]{1,0:T(8,128)(2,1)S(1)} %get-tuple-element.30), channel_id=1, source_target_pairs={{0,4},{1,5},{2,6},{3,7},{4,0},{5,1},{6,2},{7,3},{8,12},{9,13},{10,... | collective-permute-start | bytes 196616 | tf_op jit(solution)/shard_map/ppermute | solution.py:148
  56.5 12.0 %collective-permute-start.15 = (bf16[8,4096]{1,0:T(8,128)(2,1)S(1)}, bf16[8,4096]{1,0:T(8,128)(2,1)S(1)}, u32[]{:S(2)}, u32[]{:S(2)}) collective-permute-start(bf16[8,4096]{1,0:T(8,128)(2,1)S(1)} %get-tuple-element.30), channel_id=1, source_target_pairs={{0,8},{1,9},{2,10},{3,11},{4,12},{5,13},{6,14},{7,15},{8,0},{9,1},... | collective-permute-start | bytes 196616 | tf_op jit(solution)/shard_map/ppermute | solution.py:148
  58.8 9.7 %collective-permute-start.16 = (bf16[8,4096]{1,0:T(8,128)(2,1)S(1)}, bf16[8,4096]{1,0:T(8,128)(2,1)S(1)}, u32[]{:S(2)}, u32[]{:S(2)}) collective-permute-start(bf16[8,4096]{1,0:T(8,128)(2,1)S(1)} %get-tuple-element.30), channel_id=1, source_target_pairs={{0,12},{1,13},{2,14},{3,15},{4,8},{5,9},{6,10},{7,11},{8,4},{9,5},... | collective-permute-start | bytes 196616 | tf_op jit(solution)/shard_map/ppermute | solution.py:148
  68.4 2.7 %collective-permute-start.10 = (bf16[64,8192]{1,0:T(8,128)(2,1)S(1)}, bf16[64,8192]{1,0:T(8,128)(2,1)S(1)}, u32[]{:S(2)}, u32[]{:S(2)}) collective-permute-start(bf16[64,8192]{1,0:T(8,128)(2,1)S(1)} %get-tuple-element.20), channel_id=1, source_target_pairs={{0,1},{1,0},{2,3},{3,2},{4,5},{5,4},{6,7},{7,6},{8,9},{9,8},{10,11... | collective-permute-start | bytes 3145736 | tf_op jit(solution)/shard_map/ppermute | solution.py:148
  71.1 30.8 %copy-start.5 = (f32[8,1024]{1,0:T(8,128)S(1)}, f32[8,1024]{1,0:T(8,128)}, u32[]{:S(2)}) copy-start(f32[8,1024]{1,0:T(8,128)} %param.12) | copy-start | bytes 98308
  88.6 1.9 %collective-permute-start.17 = (f32[8,128]{1,0:T(8,128)}, f32[8,128]{1,0:T(8,128)S(1)}, u32[]{:S(2)}, u32[]{:S(2)}) collective-permute-start(f32[8,128]{1,0:T(8,128)} %get-tuple-element.16), channel_id=1, source_target_pairs={{0,1},{1,0},{2,3},{3,2},{4,5},{5,4},{6,7},{7,6},{8,9},{9,8},{10,11... | collective-permute-start | bytes 12296 | tf_op jit(solution)/shard_map/ppermute | solution.py:148
  88.7 3.8 %collective-permute-start.18 = (f32[8,128]{1,0:T(8,128)}, f32[8,128]{1,0:T(8,128)S(1)}, u32[]{:S(2)}, u32[]{:S(2)}) collective-permute-start(f32[8,128]{1,0:T(8,128)} %get-tuple-element.16), channel_id=1, source_target_pairs={{0,2},{1,3},{2,0},{3,1},{4,6},{5,7},{6,4},{7,5},{8,10},{9,11},{10,... | collective-permute-start | bytes 12296 | tf_op jit(solution)/shard_map/ppermute | solution.py:148
  89.7 3.2 %collective-permute-start.19 = (f32[8,128]{1,0:T(8,128)}, f32[8,128]{1,0:T(8,128)S(1)}, u32[]{:S(2)}, u32[]{:S(2)}) collective-permute-start(f32[8,128]{1,0:T(8,128)} %get-tuple-element.16), channel_id=1, source_target_pairs={{0,3},{1,2},{2,1},{3,0},{4,7},{5,6},{6,5},{7,4},{8,11},{9,10},{10,... | collective-permute-start | bytes 12296 | tf_op jit(solution)/shard_map/ppermute | solution.py:148
  93.6 4.4 %collective-permute-start.20 = (f32[8,128]{1,0:T(8,128)S(1)}, f32[8,128]{1,0:T(8,128)S(1)}, u32[]{:S(2)}, u32[]{:S(2)}) collective-permute-start(f32[8,128]{1,0:T(8,128)S(1)} %add_add_fusion.3), channel_id=1, source_target_pairs={{0,4},{1,5},{2,6},{3,7},{4,0},{5,1},{6,2},{7,3},{8,12},{9,13},{10,... | collective-permute-start | bytes 12296 | tf_op jit(solution)/shard_map/ppermute | solution.py:148
  93.6 4.5 %collective-permute-start.21 = (f32[8,128]{1,0:T(8,128)S(1)}, f32[8,128]{1,0:T(8,128)S(1)}, u32[]{:S(2)}, u32[]{:S(2)}) collective-permute-start(f32[8,128]{1,0:T(8,128)S(1)} %add_add_fusion.3), channel_id=1, source_target_pairs={{0,8},{1,9},{2,10},{3,11},{4,12},{5,13},{6,14},{7,15},{8,0},{9,1},... | collective-permute-start | bytes 12296 | tf_op jit(solution)/shard_map/ppermute | solution.py:148
  95.9 5.4 %collective-permute-start.22 = (f32[8,128]{1,0:T(8,128)S(1)}, f32[8,128]{1,0:T(8,128)S(1)}, u32[]{:S(2)}, u32[]{:S(2)}) collective-permute-start(f32[8,128]{1,0:T(8,128)S(1)} %add_add_fusion.3), channel_id=1, source_target_pairs={{0,12},{1,13},{2,14},{3,15},{4,8},{5,9},{6,10},{7,11},{8,4},{9,5},... | collective-permute-start | bytes 12296 | tf_op jit(solution)/shard_map/ppermute | solution.py:148
  (8 other events, 148.8 us)

commit v2 on v1

v2 whole, which is shorter than its diff:
```python
import functools
import math

import jax
import jax.numpy as jnp
from jax import lax
from jax.experimental import pallas as pl
from jax.experimental.pallas import tpu as pltpu
from jax.sharding import PartitionSpec as P

F32 = jnp.float32
B16 = jnp.bfloat16
LOG2E = 1.4426950408889634
PAD = 10
VMEM = pl.BlockSpec(memory_space=pltpu.VMEM)
ANY = pl.BlockSpec(memory_space=pl.ANY)
SMEM = pl.BlockSpec(memory_space=pltpu.SMEM)
HIGH = lax.Precision.HIGHEST


def dot(a, b, ca, cb, precision=None):
    return lax.dot_general(
        a, b, (((ca,), (cb,)), ((), ())), precision=precision, preferred_element_type=F32
    )


def split3(x):
    hi = x.astype(B16)
    rest = x - hi.astype(F32)
    mid = rest.astype(B16)
    low = (rest - mid.astype(F32)).astype(B16)
    return hi, mid, low


def norm_rows(features):
    wide = features.astype(F32)
    return split3(jnp.sum(wide * wide, axis=0, keepdims=True))


def rows_side(features):
    n = features.shape[1]
    hi, mid, low = norm_rows(features)
    return jnp.concatenate(
        [features, hi, mid, low, jnp.ones((3, n), B16), jnp.zeros((PAD, n), B16)], axis=0
    )


def cols_side(features):
    n = features.shape[1]
    hi, mid, low = norm_rows(features)
    return jnp.concatenate(
        [features * 2, -jnp.ones((3, n), B16), -hi, -mid, -low, jnp.zeros((PAD, n), B16)], axis=0
    )


def gauss(exponent, features):
    return jnp.exp2(exponent * (0.5 * LOG2E / features))


def stacked(x):
    return jnp.concatenate([piece.astype(F32) for piece in split3(x)], axis=0).astype(B16)


def wide_dot(x, pieces, axis):
    rows = x.shape[0]
    stack = stacked(x)
    total = None
    for i, piece in enumerate(pieces):
        count = len(pieces) - i
        part = dot(stack[: count * rows] if rows % 16 == 0 else stack, piece, 1, axis)
        for k in reversed(range(count)):
            term = part[k * rows : (k + 1) * rows]
            total = term if total is None else total + term
    return total


def fine_dot(a, b):
    n = b.shape[1]
    ah, am, al = split3(a)
    bh, bm, bl = split3(b)
    both = jnp.concatenate([bh, bm], axis=1)
    first = dot(jnp.concatenate([ah, am], axis=1), jnp.concatenate([both, both], axis=0), 1, 0)
    second = dot(jnp.concatenate([ah, al], axis=1), jnp.concatenate([bl, bh], axis=0), 1, 0)
    return (second + first[:, n:]) + first[:, :n]


def cross_kernel(pts_ref, marks_ref, res_ref, *refs):
    cross_refs, proj_ref = refs[:-1], refs[-1]
    feat = pts_ref.shape[0]
    land = marks_ref.shape[1]
    exponent = dot(rows_side(pts_ref[...]), cols_side(marks_ref[...]), 0, 0)
    pieces = split3(gauss(exponent, feat))
    for ref, piece in zip(cross_refs, pieces):
        ref[...] = piece
    res = res_ref[...]
    proj_ref[:, :land] = wide_dot(res, pieces, 0)
    squares = jnp.sum(res * res, axis=1, keepdims=True)
    proj_ref[:, land:] = jnp.broadcast_to(squares, (res.shape[0], proj_ref.shape[1] - land))


def inverse_kernel(chol_ref, *inv_refs):
    half = inv_refs[0].shape[1]
    size = chol_ref.shape[0]
    base = math.gcd(half, 128)
    row = lax.broadcasted_iota(jnp.int32, (base, base), 0)
    col = lax.broadcasted_iota(jnp.int32, (base, base), 1)
    eye = row == col
    count = size // base
    blocks, inverses = [], []
    for b in range(count):
        lo = b * base
        block = chol_ref[lo : lo + base, lo : lo + base]
        diag = jnp.where(eye, block, 0.0)
        inv_col = 1.0 / jnp.sum(diag, axis=1, keepdims=True)
        inv_row = 1.0 / jnp.sum(diag, axis=0, keepdims=True)
        pair = (row // 2 == col // 2) & (row > col)
        x = jnp.where(eye, inv_col, 0.0) - jnp.where(pair, block * (inv_col * inv_row), 0.0)
        blocks.append(block)
        inverses.append(x)
    step = 2
    while step < base:
        mask = (row // (2 * step) == col // (2 * step)) & (row // step > col // step)
        tmp = [fine_dot(jnp.where(mask, blocks[b], 0.0), inverses[b]) for b in range(count)]
        inverses = [inverses[b] - fine_dot(inverses[b], tmp[b]) for b in range(count)]
        step *= 2
    while step < half:
        tmp = []
        for i in range(0, count, 2):
            lo = i * step
            tmp.append(fine_dot(chol_ref[lo + step : lo + 2 * step, lo : lo + step], inverses[i]))
        merged = []
        for i in range(0, count, 2):
            low = -fine_dot(inverses[i + 1], tmp[i // 2])
            top = jnp.concatenate([inverses[i], jnp.zeros((step, step), F32)], axis=1)
            merged.append(jnp.concatenate([top, jnp.concatenate([low, inverses[i + 1]], axis=1)], axis=0))
        inverses = merged
        count //= 2
        step *= 2
    for i in range(count):
        for ref, piece in zip(inv_refs, split3(inverses[i])):
            ref[i * half : (i + 1) * half, :] = piece


def direction_kernel(ridge_ref, rz_ref, *refs):
    proj_refs, refs = refs[:4], refs[4:]
    chol_ref, refs = refs[0], refs[1:]
    inv_refs, cross_refs, refs = refs[:3], refs[3:6], refs[6:]
    res_ref, dir_ref, new_ref, low_ref, inner_ref = refs
    land = cross_refs[0].shape[1]
    half = inv_refs[0].shape[1]
    ridge = ridge_ref[0]
    lane = lax.broadcasted_iota(jnp.int32, inner_ref.shape, 0)
    rz = sum(jnp.where(lane == i, rz_ref[i], 0.0) for i in range(inner_ref.shape[0]))
    sums = (proj_refs[0][...] + proj_refs[1][...]) + (proj_refs[2][...] + proj_refs[3][...])
    proj = sums[:, :land]
    squares = sums[:, land : land + 1]
    below = split3(chol_ref[half:, :half])
    upper = [ref[:half] for ref in inv_refs]
    lower = [ref[half:] for ref in inv_refs]
    y0 = wide_dot(proj[:, :half], upper, 1)
    y1 = wide_dot(proj[:, half:] - wide_dot(y0, below, 1), lower, 1)
    x1 = wide_dot(y1, lower, 0)
    x0 = wide_dot(y0 - wide_dot(x1, below, 0), upper, 0)
    coeffs = jnp.concatenate([x0, x1], axis=1)
    inner = (squares - jnp.sum(proj * coeffs, axis=1, keepdims=True)) / ridge
    precond = (res_ref[...] - wide_dot(coeffs, [ref[...] for ref in cross_refs], 1)) / ridge
    new = precond + (inner / rz) * dir_ref[...]
    new_ref[...] = new
    low_ref[...] = new.astype(B16)
    inner_ref[...] = inner


def products(points_at, first, own_lhs, pts_ref, low_ref, total):
    feat, width = pts_ref.shape[0], own_lhs.shape[1]
    group = math.gcd(len(points_at), 4)
    for i in range(0, len(points_at), group):
        pts = jnp.concatenate(
            [pts_ref[:, at * width : (at + 1) * width] for at in points_at[i : i + group]], axis=1
        )
        kernel = gauss(dot(rows_side(pts), own_lhs[...], 0, 0), feat).astype(B16)
        at = (first + i) * width
        total = total + dot(low_ref[:, at : at + group * width], kernel, 1, 0)
    return total


def near_kernel(points_at, own_ref, pts_ref, low_ref, total_ref, lhs_ref):
    lhs_ref[...] = cols_side(own_ref[...])
    total_ref[...] = products(points_at, 0, lhs_ref, pts_ref, low_ref, jnp.zeros(total_ref.shape, F32))


def image_kernel(points_at, first, ridge_ref, own_ref, pts_ref, low_ref, near_ref, new_ref, image_ref, curv_ref, lhs_ref):
    lhs_ref[...] = cols_side(own_ref[...])
    total = products(points_at, first, lhs_ref, pts_ref, low_ref, near_ref[...])
    new = new_ref[...]
    image = total + ridge_ref[0] * new
    image_ref[...] = image
    curv = jnp.sum(new * image, axis=1, keepdims=True)
    curv_ref[...] = jnp.broadcast_to(curv, curv_ref.shape)


def update_kernel(*refs):
    curv_refs, refs = refs[:4], refs[4:]
    inner_ref, sol_ref, res_ref, new_ref, image_ref, sol_out, res_out, inner_out = refs
    curv = (curv_refs[0][...] + curv_refs[1][...]) + (curv_refs[2][...] + curv_refs[3][...])
    inner = inner_ref[...]
    alpha = inner / curv[:, :1]
    n = inner.shape[0]
    eye = lax.broadcasted_iota(jnp.int32, (n, n), 0) == lax.broadcasted_iota(jnp.int32, (n, n), 1)
    inner_out[...] = jnp.sum(jnp.where(eye, inner, 0.0), axis=0, keepdims=True)
    sol_out[...] = sol_ref[...] + alpha * new_ref[...]
    res_out[...] = res_ref[...] - alpha * image_ref[...]


def exchange(x, mask, count):
    return lax.ppermute(x, "rows", [(i, i ^ mask) for i in range(count)])


def stages(count):
    out, bit = [], 1
    while bit < count:
        if 2 * bit < count:
            out.append([bit, 2 * bit, 3 * bit])
            bit *= 4
        else:
            out.append([bit])
            bit *= 2
    return out


def add_kernel(*refs):
    parts = [ref[...] for ref in refs[:-1]]
    while len(parts) > 1:
        parts = [parts[i] + parts[i + 1] for i in range(0, len(parts), 2)]
    refs[-1][...] = parts[0]


def join_kernel(*refs):
    at = 0
    for ref in refs[:-1]:
        refs[-1][:, at : at + ref.shape[1]] = ref[...]
        at += ref.shape[1]


def add_up(parts, after=()):
    return call(add_kernel, jax.ShapeDtypeStruct(parts[0].shape, F32), *parts, name="add", room=1, after=after)


def join(parts, after=()):
    rows, dtype = parts[0].shape[0], parts[0].dtype
    total = sum(part.shape[1] for part in parts)
    return call(join_kernel, jax.ShapeDtypeStruct((rows, total), dtype), *parts, name="join", room=8, after=after)


def all_sum(x, level_list, count, after=()):
    for masks in level_list:
        x = add_up(x, after) if isinstance(x, list) else x
        x = [x] + [exchange(x, m, count) for m in masks]
    return x + [jnp.zeros_like(x[0])] * (4 - len(x))


def gather(x, order, level_list, count, afters=()):
    for i, masks in enumerate(level_list):
        x = join([x] + [exchange(x, m, count) for m in masks], afters[i] if i < len(afters) else ())
        order = order + [m ^ o for m in masks for o in order]
    return x, order


def call(kernel, out, *args, smem=(), scratch=(), name=None, work=0, room=16, after=()):
    body = (lambda *refs: kernel(*refs[len(after) :])) if after else kernel
    smem = [i + len(after) for i in smem]
    args = tuple(after) + args
    return pl.pallas_call(
        body,
        out_shape=out,
        in_specs=[
            ANY if i < len(after) else SMEM if i in smem else VMEM for i in range(len(args))
        ],
        out_specs=jax.tree.map(lambda _: VMEM, out),
        scratch_shapes=list(scratch),
        compiler_params=pltpu.CompilerParams(vmem_limit_bytes=room * 2**20),
        cost_estimate=pl.CostEstimate(flops=2 * work, bytes_accessed=0, transcendentals=0),
        name=name,
    )(*args)


def local(count, points, landmarks, chol, ridge, solution, residual, direction, rz_prev):
    feat = points.shape[0]
    outs, width = residual.shape
    land = landmarks.shape[1]
    shape = jax.ShapeDtypeStruct
    depth = 256
    levels = stages(count)
    side = pltpu.VMEM((feat + 6 + PAD, width), B16)
    *lower, top = levels
    far_stages = [[m] for masks in reversed(lower) for m in masks[1::-1]]
    *cross, partial = call(
        cross_kernel,
        (shape((width, land), B16),) * 3 + (shape((outs, land + 128), F32),),
        points, landmarks, residual, name="cross", room=24, work=5 * width * land * depth,
    )
    inverse = call(
        inverse_kernel, (shape((land, land // 2), B16),) * 3, chol,
        name="inverse", work=width * land * depth, after=(partial,),
    )
    partial = add_up(all_sum(partial, levels[:1], count), inverse[:1])
    near_points, near_order = gather(points, [0], [top], count, [(partial,)])
    proj = all_sum(partial, levels[1:], count)
    new, low, inner = call(
        direction_kernel,
        (shape((outs, width), F32), shape((outs, width), B16), shape((outs, 1), F32)),
        ridge, rz_prev, *proj, chol, *inverse, *cross, residual, direction,
        smem=(0, 1), name="direction", room=24, work=6 * width * land * depth,
    )
    all_points, point_order = gather(near_points, near_order, far_stages, count, [(new,)])
    near_low, low_order = gather(low, [0], [top], count)
    near = call(
        functools.partial(near_kernel, [near_order.index(m) for m in low_order]),
        shape((outs, width), F32),
        points, near_points, near_low, scratch=(side,), name="near", room=32,
        work=2 * len(low_order) * width * width * depth,
    )
    first = len(low_order)
    all_low, low_order = gather(near_low, low_order, lower[::-1], count, [(near,)])
    image, curv = call(
        functools.partial(image_kernel, [point_order.index(m) for m in low_order[first:]], first),
        (shape((outs, width), F32), shape((outs, 128), F32)),
        ridge, points, all_points, all_low, near, new, smem=(0,),
        scratch=(side,), name="image", room=32, work=2 * (count - first) * width * width * depth,
    )
    sol_new, res_new, inner_row = call(
        update_kernel,
        (shape((outs, width), F32),) * 2 + (shape((1, outs), F32),),
        *all_sum(curv, levels, count), inner, solution, residual, new, image, name="update",
    )
    return (sol_new, res_new, new, inner_row.reshape(outs))


def solution(mesh):
    count = mesh.shape["rows"]
    vec = P(None, ("groups", "rows"))
    in_specs = (vec, P(None, "groups"), P("groups", None), P("groups"), vec, vec, vec, P("groups"))
    out_specs = (vec, vec, vec, P("groups"))
    return jax.shard_map(
        functools.partial(local, count), mesh=mesh, in_specs=in_specs, out_specs=out_specs, check_vma=False
    )
```

time: 104 us -> 75.3 us (0.72)
  Pallas kernels: 47.9 us -> 28.3 us
  other arithmetic: 4.22 us -> 0 us
  waiting for transfers between devices: 17.1 us -> 14.7 us
  starting transfers between devices: 28.1 us -> 26.4 us
    pallas_call x4 -> x13, Pallas kernels: 47.9 us -> 28.3 us  [call(): pl.pallas_call(body, out_shape=out, in_specs=[ANY if i < len(after) else...]
    ppermute x23, waiting for transfers between devices: 17.1 us -> 14.7 us  [exchange(): return lax.ppermute(x, 'rows', [(i, i ^ mask) for i in range(count)])]
    add x4 -> x0, other arithmetic: 2.1 us -> none  [all_sum(): parts = [parts[i] + parts[i + 1] for i in range(0, len(parts), 2)]]
    ppermute x23, starting transfers between devices: 28.1 us -> 26.4 us  [exchange(): return lax.ppermute(x, 'rows', [(i, i ^ mask) for i in range(count)])]
    sub x1 -> x0, other arithmetic: 1.46 us -> none  [local(): return (solution + alpha * new, residual - alpha * image, new, inner_new)]
    unnamed x27 -> x22, local copies, waits for them, and re-layouts: 3.77 us -> 3.96 us
  transfers between devices with their start and end apart: 23 -> 23, of which waited for: 8 -> 8; matrix products, arithmetic and copies ran while one was open for 4% -> 0% of each run, Pallas kernels for 27% -> 23%
where the time goes in v2:
time: 75.3 us; the launch traced here: 74.9 us
  Pallas kernels  28.3 us (38%)
  starting transfers between devices  26.4 us (35%)
  waiting for transfers between devices  14.7 us (20%)
  local copies, waits for them, and re-layouts  3.96 us (5%)
  between operations  1.49 us (2%)
    pallas_call x13, Pallas kernels, call(): pl.pallas_call(body, out_shape=out, in_specs=[ANY if i < len(after) else...  28.3 us
    ppermute x23, starting transfers between devices, exchange(): return lax.ppermute(x, 'rows', [(i, i ^ mask) for i in range(count)])  26.4 us
    ppermute x23, waiting for transfers between devices, exchange(): return lax.ppermute(x, 'rows', [(i, i ^ mask) for i in range(count)])  14.7 us
    unnamed x22, local copies, waits for them, and re-layouts  3.96 us
  transfers between devices with their start and end apart: 23, of which 8 were waited for; matrix products, arithmetic and copies ran while one was open for 0% of the time, Pallas kernels for 23%

profile of v2, /device:TPU:0, one launch (start us, length us, event | category | flops | bytes accessed | tf_op | source)
XLA Modules:
  0.0 74.9 jit_solution(2169335154083130826)
XLA Ops:
  0.6 3.1 %collective-permute-start.6 = (bf16[64,1024]{1,0:T(8,128)(2,1)}, bf16[64,1024]{1,0:T(8,128)(2,1)S(1)}, u32[]{:S(2)}, u32[]{:S(2)}) collective-permute-start(bf16[64,1024]{1,0:T(8,128)(2,1)} %own_ref.3), channel_id=1, source_target_pairs={{0,4},{1,5},{2,6},{3,7},{4,0},{5,1},{6,2},{7,3},{8,12},{9,13},{10,... | collective-permute-start | bytes 393224 | tf_op jit(solution)/shard_map/ppermute | solution.py:215
  3.7 2.6 %collective-permute-start.7 = (bf16[64,1024]{1,0:T(8,128)(2,1)}, bf16[64,1024]{1,0:T(8,128)(2,1)S(1)}, u32[]{:S(2)}, u32[]{:S(2)}) collective-permute-start(bf16[64,1024]{1,0:T(8,128)(2,1)} %own_ref.3), channel_id=1, source_target_pairs={{0,8},{1,9},{2,10},{3,11},{4,12},{5,13},{6,14},{7,15},{8,0},{9,1},... | collective-permute-start | bytes 393224 | tf_op jit(solution)/shard_map/ppermute | solution.py:215
  7.1 0.9 %copy-done.5 = bf16[64,1024]{1,0:T(8,128)(2,1)S(1)} copy-done((bf16[64,1024]{1,0:T(8,128)(2,1)S(1)}, bf16[64,1024]{1,0:T(8,128)(2,1)}, u32[]{:S(2)}) %copy-start.5) | copy-done | bytes 131096
  8.0 0.9 %copy-done.10 = bf16[64,1024]{1,0:T(8,128)(2,1)S(1)} copy-done((bf16[64,1024]{1,0:T(8,128)(2,1)S(1)}, bf16[64,1024]{1,0:T(8,128)(2,1)}, u32[]{:S(2)}) %copy-start.10) | copy-done | bytes 131096
  8.9 2.2 %cross.1 = (bf16[1024,1024]{1,0:T(8,128)(2,1)S(1)}, bf16[1024,1024]{1,0:T(8,128)(2,1)S(1)}, bf16[1024,1024]{1,0:T(8,128)(2,1)S(1)}, f32[8,1152]{1,0:T(8,128)S(1)}) custom-call(bf16[64,1024]{1,0:T(8,128)(2,1)S(1)} %copy-done.5, bf16[64,1024]{1,0:T(8,128)(2,1)S(1)} %copy-done.10, f32[8,1024]{1,0:T(8,128)S(1)} %copy-done.1), custom_call_target="tpu_custom_call" | custom-call | flops 2684354560 | tf_op jit(solution)/shard_map/cross/pallas_call | solution.py:272
  11.2 1.8 %collective-permute-start.1 = (f32[8,1152]{1,0:T(8,128)S(1)}, f32[8,1152]{1,0:T(8,128)S(1)}, u32[]{:S(2)}, u32[]{:S(2)}) collective-permute-start(f32[8,1152]{1,0:T(8,128)S(1)} %get-tuple-element.19.refs_0_.refs_1_), channel_id=1, source_target_pairs={{0,2},{1,3},{2,0},{3,1},{4,6},{5,7},{6,4},{7,5},{8,10},{9,11},{10,... | collective-permute-start | bytes 110600 | tf_op jit(solution)/shard_map/ppermute | solution.py:215
  13.0 0.9 %collective-permute-start.2 = (f32[8,1152]{1,0:T(8,128)S(1)}, f32[8,1152]{1,0:T(8,128)S(1)}, u32[]{:S(2)}, u32[]{:S(2)}) collective-permute-start(f32[8,1152]{1,0:T(8,128)S(1)} %get-tuple-element.19.refs_0_.refs_1_), channel_id=1, source_target_pairs={{0,3},{1,2},{2,1},{3,0},{4,7},{5,6},{6,5},{7,4},{8,11},{9,10},{10,... | collective-permute-start | bytes 110600 | tf_op jit(solution)/shard_map/ppermute | solution.py:215
  13.9 5.5 %inverse.1 = (bf16[1024,512]{1,0:T(8,128)(2,1)S(1)}, bf16[1024,512]{1,0:T(8,128)(2,1)S(1)}, bf16[1024,512]{1,0:T(8,128)(2,1)S(1)}) custom-call(f32[8,1152]{1,0:T(8,128)S(1)} %get-tuple-element.19.refs_0_.refs_1_, f32[1024,1024]{1,0:T(8,128)S(1)} %copy-done), custom_call_target="tpu_custom_call" | custom-call | flops 536870912 | tf_op jit(solution)/shard_map/inverse/pallas_call | solution.py:272
  19.6 1.0 %collective-permute-start.9 = (bf16[64,4096]{1,0:T(8,128)(2,1)S(1)}, bf16[64,4096]{1,0:T(8,128)(2,1)S(1)}, u32[]{:S(2)}, u32[]{:S(2)}) collective-permute-start(bf16[64,4096]{1,0:T(8,128)(2,1)S(1)} %join.5.refs_1_.pts_ref), channel_id=1, source_target_pairs={{0,2},{1,3},{2,0},{3,1},{4,6},{5,7},{6,4},{7,5},{8,10},{9,11},{10,... | collective-permute-start | bytes 1572872 | tf_op jit(solution)/shard_map/ppermute | solution.py:215
  21.3 3.5 %collective-permute-start.4 = (f32[8,1152]{1,0:T(8,128)S(1)}, f32[8,1152]{1,0:T(8,128)S(1)}, u32[]{:S(2)}, u32[]{:S(2)}) collective-permute-start(f32[8,1152]{1,0:T(8,128)S(1)} %add.2.refs_0_), channel_id=1, source_target_pairs={{0,8},{1,9},{2,10},{3,11},{4,12},{5,13},{6,14},{7,15},{8,0},{9,1},... | collective-permute-start | bytes 110600 | tf_op jit(solution)/shard_map/ppermute | solution.py:215
  25.6 1.6 %collective-permute-done.4.refs_2_ = f32[8,1152]{1,0:T(8,128)S(1)} collective-permute-done((f32[8,1152]{1,0:T(8,128)S(1)}, f32[8,1152]{1,0:T(8,128)S(1)}, u32[]{:S(2)}, u32[]{:S(2)}) %collective-permute-start.4) | collective-permute-done | bytes 36896 | tf_op jit(solution)/shard_map/ppermute | solution.py:215
  27.3 3.3 %collective-permute-done.5.refs_3_ = f32[8,1152]{1,0:T(8,128)S(1)} collective-permute-done((f32[8,1152]{1,0:T(8,128)S(1)}, f32[8,1152]{1,0:T(8,128)S(1)}, u32[]{:S(2)}, u32[]{:S(2)}) %collective-permute-start.5) | collective-permute-done | bytes 36896 | tf_op jit(solution)/shard_map/ppermute | solution.py:215
  30.5 5.7 %direction.1 = (f32[8,1024]{1,0:T(8,128)}, bf16[8,1024]{1,0:T(8,128)(2,1)S(1)}, f32[8,1]{1,0:T(8,128)S(1)}) custom-call(f32[1]{0:T(128)S(6)} %copy.12.ridge_ref, f32[8]{0:T(128)S(1)} %copy-done.9, f32[8,1152]{1,0:T(8,128)S(1)} %add.2.refs_0_, f32[8,1152]{1,0:T(8,128)S(1)} %collective-permute-done.3.refs_1_, f32[8,1152]{1,0:T(8,128)S(1)} %collective-permute-done.4.refs_2_, ...), custom_call_target="tpu_custom_call" | custom-call | flops 3221225472 | tf_op jit(solution)/shard_map/direction/pallas_call | solution.py:272
  37.2 1.8 %collective-permute-start.12 = (bf16[8,1024]{1,0:T(8,128)(2,1)S(1)}, bf16[8,1024]{1,0:T(8,128)(2,1)S(1)}, u32[]{:S(2)}, u32[]{:S(2)}) collective-permute-start(bf16[8,1024]{1,0:T(8,128)(2,1)S(1)} %get-tuple-element.27.refs_0_), channel_id=1, source_target_pairs={{0,8},{1,9},{2,10},{3,11},{4,12},{5,13},{6,14},{7,15},{8,0},{9,1},... | collective-permute-start | bytes 49160 | tf_op jit(solution)/shard_map/ppermute | solution.py:215
  39.0 2.5 %collective-permute-start.13 = (bf16[8,1024]{1,0:T(8,128)(2,1)S(1)}, bf16[8,1024]{1,0:T(8,128)(2,1)S(1)}, u32[]{:S(2)}, u32[]{:S(2)}) collective-permute-start(bf16[8,1024]{1,0:T(8,128)(2,1)S(1)} %get-tuple-element.27.refs_0_), channel_id=1, source_target_pairs={{0,12},{1,13},{2,14},{3,15},{4,8},{5,9},{6,10},{7,11},{8,4},{9,5},... | collective-permute-start | bytes 49160 | tf_op jit(solution)/shard_map/ppermute | solution.py:215
  41.9 2.7 %collective-permute-done.13.refs_3_ = bf16[8,1024]{1,0:T(8,128)(2,1)S(1)} collective-permute-done((bf16[8,1024]{1,0:T(8,128)(2,1)S(1)}, bf16[8,1024]{1,0:T(8,128)(2,1)S(1)}, u32[]{:S(2)}, u32[]{:S(2)}) %collective-permute-start.13) | collective-permute-done | bytes 16416 | tf_op jit(solution)/shard_map/ppermute | solution.py:215
  44.6 1.0 %collective-permute-start.15 = (bf16[8,4096]{1,0:T(8,128)(2,1)S(1)}, bf16[8,4096]{1,0:T(8,128)(2,1)S(1)}, u32[]{:S(2)}, u32[]{:S(2)}) collective-permute-start(bf16[8,4096]{1,0:T(8,128)(2,1)S(1)} %join.8.low_ref.refs_1_), channel_id=1, source_target_pairs={{0,2},{1,3},{2,0},{3,1},{4,6},{5,7},{6,4},{7,5},{8,10},{9,11},{10,... | collective-permute-start | bytes 196616 | tf_op jit(solution)/shard_map/ppermute | solution.py:215
  46.4 3.7 %near.1.refs_0_.near_ref = f32[8,1024]{1,0:T(8,128)S(1)} custom-call(bf16[64,1024]{1,0:T(8,128)(2,1)S(1)} %copy-done.6, bf16[64,4096]{1,0:T(8,128)(2,1)S(1)} %join.5.refs_1_.pts_ref, bf16[8,4096]{1,0:T(8,128)(2,1)S(1)} %join.8.low_ref.refs_1_), custom_call_target="tpu_custom_call" | custom-call | flops 4294967296 | tf_op jit(solution)/shard_map/near/pallas_call | solution.py:272
  50.9 10.2 %image.1 = (f32[8,1024]{1,0:T(8,128)S(1)}, f32[8,128]{1,0:T(8,128)S(1)}) custom-call(f32[1]{0:T(128)S(6)} %copy.12.ridge_ref, bf16[64,1024]{1,0:T(8,128)(2,1)S(1)} %copy-done.6, bf16[64,16384]{1,0:T(8,128)(2,1)S(1)} %join.7.pts_ref, bf16[8,16384]{1,0:T(8,128)(2,1)S(1)} %join.9.low_ref, f32[8,1024]{1,0:T(8,128)S(1)} %near.1.refs_0_.near_ref, ...), custom_call_target="tpu_custom_call" | custom-call | flops 12884901888 | tf_op jit(solution)/shard_map/image/pallas_call | solution.py:272
  61.5 0.9 %collective-permute-start.18 = (f32[8,128]{1,0:T(8,128)S(1)}, f32[8,128]{1,0:T(8,128)S(1)}, u32[]{:S(2)}, u32[]{:S(2)}) collective-permute-start(f32[8,128]{1,0:T(8,128)S(1)} %get-tuple-element.28.refs_0_), channel_id=1, source_target_pairs={{0,2},{1,3},{2,0},{3,1},{4,6},{5,7},{6,4},{7,5},{8,10},{9,11},{10,... | collective-permute-start | bytes 12296 | tf_op jit(solution)/shard_map/ppermute | solution.py:215
  63.0 2.1 %collective-permute-done.18.refs_2_ = f32[8,128]{1,0:T(8,128)S(1)} collective-permute-done((f32[8,128]{1,0:T(8,128)S(1)}, f32[8,128]{1,0:T(8,128)S(1)}, u32[]{:S(2)}, u32[]{:S(2)}) %collective-permute-start.18) | collective-permute-done | bytes 4128 | tf_op jit(solution)/shard_map/ppermute | solution.py:215
  65.4 3.3 %collective-permute-start.21 = (f32[8,128]{1,0:T(8,128)S(1)}, f32[8,128]{1,0:T(8,128)S(1)}, u32[]{:S(2)}, u32[]{:S(2)}) collective-permute-start(f32[8,128]{1,0:T(8,128)S(1)} %add.3.refs_0_), channel_id=1, source_target_pairs={{0,8},{1,9},{2,10},{3,11},{4,12},{5,13},{6,14},{7,15},{8,0},{9,1},... | collective-permute-start | bytes 12296 | tf_op jit(solution)/shard_map/ppermute | solution.py:215
  68.8 1.1 %collective-permute-start.22 = (f32[8,128]{1,0:T(8,128)S(1)}, f32[8,128]{1,0:T(8,128)S(1)}, u32[]{:S(2)}, u32[]{:S(2)}) collective-permute-start(f32[8,128]{1,0:T(8,128)S(1)} %add.3.refs_0_), channel_id=1, source_target_pairs={{0,12},{1,13},{2,14},{3,15},{4,8},{5,9},{6,10},{7,11},{8,4},{9,5},... | collective-permute-start | bytes 12296 | tf_op jit(solution)/shard_map/ppermute | solution.py:215
  70.4 3.8 %collective-permute-done.22.refs_3_ = f32[8,128]{1,0:T(8,128)S(1)} collective-permute-done((f32[8,128]{1,0:T(8,128)S(1)}, f32[8,128]{1,0:T(8,128)S(1)}, u32[]{:S(2)}, u32[]{:S(2)}) %collective-permute-start.22) | collective-permute-done | bytes 4128 | tf_op jit(solution)/shard_map/ppermute | solution.py:215
  (57 shorter events, 7.4 us)
Async XLA Ops:
  0.6 18.9 %collective-permute-start.6 = (bf16[64,1024]{1,0:T(8,128)(2,1)}, bf16[64,1024]{1,0:T(8,128)(2,1)S(1)}, u32[]{:S(2)}, u32[]{:S(2)}) collective-permute-start(bf16[64,1024]{1,0:T(8,128)(2,1)} %own_ref.3), channel_id=1, source_target_pairs={{0,4},{1,5},{2,6},{3,7},{4,0},{5,1},{6,2},{7,3},{8,12},{9,13},{10,... | collective-permute-start | bytes 393224 | tf_op jit(solution)/shard_map/ppermute | solution.py:215
  3.7 15.8 %collective-permute-start.7 = (bf16[64,1024]{1,0:T(8,128)(2,1)}, bf16[64,1024]{1,0:T(8,128)(2,1)S(1)}, u32[]{:S(2)}, u32[]{:S(2)}) collective-permute-start(bf16[64,1024]{1,0:T(8,128)(2,1)} %own_ref.3), channel_id=1, source_target_pairs={{0,8},{1,9},{2,10},{3,11},{4,12},{5,13},{6,14},{7,15},{8,0},{9,1},... | collective-permute-start | bytes 393224 | tf_op jit(solution)/shard_map/ppermute | solution.py:215
  6.3 13.3 %collective-permute-start.8 = (bf16[64,1024]{1,0:T(8,128)(2,1)}, bf16[64,1024]{1,0:T(8,128)(2,1)S(1)}, u32[]{:S(2)}, u32[]{:S(2)}) collective-permute-start(bf16[64,1024]{1,0:T(8,128)(2,1)} %own_ref.3), channel_id=1, source_target_pairs={{0,12},{1,13},{2,14},{3,15},{4,8},{5,9},{6,10},{7,11},{8,4},{9,5},... | collective-permute-start | bytes 393224 | tf_op jit(solution)/shard_map/ppermute | solution.py:215
  11.1 1.9 %collective-permute-start = (f32[8,1152]{1,0:T(8,128)S(1)}, f32[8,1152]{1,0:T(8,128)S(1)}, u32[]{:S(2)}, u32[]{:S(2)}) collective-permute-start(f32[8,1152]{1,0:T(8,128)S(1)} %get-tuple-element.19.refs_0_.refs_1_), channel_id=1, source_target_pairs={{0,1},{1,0},{2,3},{3,2},{4,5},{5,4},{6,7},{7,6},{8,9},{9,8},{10,11... | collective-permute-start | bytes 110600 | tf_op jit(solution)/shard_map/ppermute | solution.py:215
  11.2 8.3 %collective-permute-start.1 = (f32[8,1152]{1,0:T(8,128)S(1)}, f32[8,1152]{1,0:T(8,128)S(1)}, u32[]{:S(2)}, u32[]{:S(2)}) collective-permute-start(f32[8,1152]{1,0:T(8,128)S(1)} %get-tuple-element.19.refs_0_.refs_1_), channel_id=1, source_target_pairs={{0,2},{1,3},{2,0},{3,1},{4,6},{5,7},{6,4},{7,5},{8,10},{9,11},{10,... | collective-permute-start | bytes 110600 | tf_op jit(solution)/shard_map/ppermute | solution.py:215
  13.0 6.5 %collective-permute-start.2 = (f32[8,1152]{1,0:T(8,128)S(1)}, f32[8,1152]{1,0:T(8,128)S(1)}, u32[]{:S(2)}, u32[]{:S(2)}) collective-permute-start(f32[8,1152]{1,0:T(8,128)S(1)} %get-tuple-element.19.refs_0_.refs_1_), channel_id=1, source_target_pairs={{0,3},{1,2},{2,1},{3,0},{4,7},{5,6},{6,5},{7,4},{8,11},{9,10},{10,... | collective-permute-start | bytes 110600 | tf_op jit(solution)/shard_map/ppermute | solution.py:215
  19.6 16.6 %collective-permute-start.9 = (bf16[64,4096]{1,0:T(8,128)(2,1)S(1)}, bf16[64,4096]{1,0:T(8,128)(2,1)S(1)}, u32[]{:S(2)}, u32[]{:S(2)}) collective-permute-start(bf16[64,4096]{1,0:T(8,128)(2,1)S(1)} %join.5.refs_1_.pts_ref), channel_id=1, source_target_pairs={{0,2},{1,3},{2,0},{3,1},{4,6},{5,7},{6,4},{7,5},{8,10},{9,11},{10,... | collective-permute-start | bytes 1572872 | tf_op jit(solution)/shard_map/ppermute | solution.py:215
  20.6 5.0 %collective-permute-start.3 = (f32[8,1152]{1,0:T(8,128)S(1)}, f32[8,1152]{1,0:T(8,128)S(1)}, u32[]{:S(2)}, u32[]{:S(2)}) collective-permute-start(f32[8,1152]{1,0:T(8,128)S(1)} %add.2.refs_0_), channel_id=1, source_target_pairs={{0,4},{1,5},{2,6},{3,7},{4,0},{5,1},{6,2},{7,3},{8,12},{9,13},{10,... | collective-permute-start | bytes 110600 | tf_op jit(solution)/shard_map/ppermute | solution.py:215
  21.3 6.0 %collective-permute-start.4 = (f32[8,1152]{1,0:T(8,128)S(1)}, f32[8,1152]{1,0:T(8,128)S(1)}, u32[]{:S(2)}, u32[]{:S(2)}) collective-permute-start(f32[8,1152]{1,0:T(8,128)S(1)} %add.2.refs_0_), channel_id=1, source_target_pairs={{0,8},{1,9},{2,10},{3,11},{4,12},{5,13},{6,14},{7,15},{8,0},{9,1},... | collective-permute-start | bytes 110600 | tf_op jit(solution)/shard_map/ppermute | solution.py:215
  24.8 5.8 %collective-permute-start.5 = (f32[8,1152]{1,0:T(8,128)S(1)}, f32[8,1152]{1,0:T(8,128)S(1)}, u32[]{:S(2)}, u32[]{:S(2)}) collective-permute-start(f32[8,1152]{1,0:T(8,128)S(1)} %add.2.refs_0_), channel_id=1, source_target_pairs={{0,12},{1,13},{2,14},{3,15},{4,8},{5,9},{6,10},{7,11},{8,4},{9,5},... | collective-permute-start | bytes 110600 | tf_op jit(solution)/shard_map/ppermute | solution.py:215
  37.0 13.2 %collective-permute-start.10 = (bf16[64,8192]{1,0:T(8,128)(2,1)S(1)}, bf16[64,8192]{1,0:T(8,128)(2,1)S(1)}, u32[]{:S(2)}, u32[]{:S(2)}) collective-permute-start(bf16[64,8192]{1,0:T(8,128)(2,1)S(1)} %join.6.refs_0_), channel_id=1, source_target_pairs={{0,1},{1,0},{2,3},{3,2},{4,5},{5,4},{6,7},{7,6},{8,9},{9,8},{10,11... | collective-permute-start | bytes 3145736 | tf_op jit(solution)/shard_map/ppermute | solution.py:215
  37.1 4.5 %collective-permute-start.11 = (bf16[8,1024]{1,0:T(8,128)(2,1)S(1)}, bf16[8,1024]{1,0:T(8,128)(2,1)S(1)}, u32[]{:S(2)}, u32[]{:S(2)}) collective-permute-start(bf16[8,1024]{1,0:T(8,128)(2,1)S(1)} %get-tuple-element.27.refs_0_), channel_id=1, source_target_pairs={{0,4},{1,5},{2,6},{3,7},{4,0},{5,1},{6,2},{7,3},{8,12},{9,13},{10,... | collective-permute-start | bytes 49160 | tf_op jit(solution)/shard_map/ppermute | solution.py:215
  37.2 4.7 %collective-permute-start.12 = (bf16[8,1024]{1,0:T(8,128)(2,1)S(1)}, bf16[8,1024]{1,0:T(8,128)(2,1)S(1)}, u32[]{:S(2)}, u32[]{:S(2)}) collective-permute-start(bf16[8,1024]{1,0:T(8,128)(2,1)S(1)} %get-tuple-element.27.refs_0_), channel_id=1, source_target_pairs={{0,8},{1,9},{2,10},{3,11},{4,12},{5,13},{6,14},{7,15},{8,0},{9,1},... | collective-permute-start | bytes 49160 | tf_op jit(solution)/shard_map/ppermute | solution.py:215
  39.0 5.5 %collective-permute-start.13 = (bf16[8,1024]{1,0:T(8,128)(2,1)S(1)}, bf16[8,1024]{1,0:T(8,128)(2,1)S(1)}, u32[]{:S(2)}, u32[]{:S(2)}) collective-permute-start(bf16[8,1024]{1,0:T(8,128)(2,1)S(1)} %get-tuple-element.27.refs_0_), channel_id=1, source_target_pairs={{0,12},{1,13},{2,14},{3,15},{4,8},{5,9},{6,10},{7,11},{8,4},{9,5},... | collective-permute-start | bytes 49160 | tf_op jit(solution)/shard_map/ppermute | solution.py:215
  44.6 5.6 %collective-permute-start.14 = (bf16[8,4096]{1,0:T(8,128)(2,1)S(1)}, bf16[8,4096]{1,0:T(8,128)(2,1)S(1)}, u32[]{:S(2)}, u32[]{:S(2)}) collective-permute-start(bf16[8,4096]{1,0:T(8,128)(2,1)S(1)} %join.8.low_ref.refs_1_), channel_id=1, source_target_pairs={{0,1},{1,0},{2,3},{3,2},{4,5},{5,4},{6,7},{7,6},{8,9},{9,8},{10,11... | collective-permute-start | bytes 196616 | tf_op jit(solution)/shard_map/ppermute | solution.py:215
  44.6 5.5 %collective-permute-start.15 = (bf16[8,4096]{1,0:T(8,128)(2,1)S(1)}, bf16[8,4096]{1,0:T(8,128)(2,1)S(1)}, u32[]{:S(2)}, u32[]{:S(2)}) collective-permute-start(bf16[8,4096]{1,0:T(8,128)(2,1)S(1)} %join.8.low_ref.refs_1_), channel_id=1, source_target_pairs={{0,2},{1,3},{2,0},{3,1},{4,6},{5,7},{6,4},{7,5},{8,10},{9,11},{10,... | collective-permute-start | bytes 196616 | tf_op jit(solution)/shard_map/ppermute | solution.py:215
  45.5 4.6 %collective-permute-start.16 = (bf16[8,4096]{1,0:T(8,128)(2,1)S(1)}, bf16[8,4096]{1,0:T(8,128)(2,1)S(1)}, u32[]{:S(2)}, u32[]{:S(2)}) collective-permute-start(bf16[8,4096]{1,0:T(8,128)(2,1)S(1)} %join.8.low_ref.refs_1_), channel_id=1, source_target_pairs={{0,3},{1,2},{2,1},{3,0},{4,7},{5,6},{6,5},{7,4},{8,11},{9,10},{10,... | collective-permute-start | bytes 196616 | tf_op jit(solution)/shard_map/ppermute | solution.py:215
  50.9 23.3 %copy-start.8 = (f32[8,1024]{1,0:T(8,128)S(1)}, f32[8,1024]{1,0:T(8,128)}, u32[]{:S(2)}) copy-start(f32[8,1024]{1,0:T(8,128)} %refs_5_.1) | copy-start | bytes 98308
  61.1 1.9 %collective-permute-start.17 = (f32[8,128]{1,0:T(8,128)S(1)}, f32[8,128]{1,0:T(8,128)S(1)}, u32[]{:S(2)}, u32[]{:S(2)}) collective-permute-start(f32[8,128]{1,0:T(8,128)S(1)} %get-tuple-element.28.refs_0_), channel_id=1, source_target_pairs={{0,1},{1,0},{2,3},{3,2},{4,5},{5,4},{6,7},{7,6},{8,9},{9,8},{10,11... | collective-permute-start | bytes 12296 | tf_op jit(solution)/shard_map/ppermute | solution.py:215
  61.5 3.6 %collective-permute-start.18 = (f32[8,128]{1,0:T(8,128)S(1)}, f32[8,128]{1,0:T(8,128)S(1)}, u32[]{:S(2)}, u32[]{:S(2)}) collective-permute-start(f32[8,128]{1,0:T(8,128)S(1)} %get-tuple-element.28.refs_0_), channel_id=1, source_target_pairs={{0,2},{1,3},{2,0},{3,1},{4,6},{5,7},{6,4},{7,5},{8,10},{9,11},{10,... | collective-permute-start | bytes 12296 | tf_op jit(solution)/shard_map/ppermute | solution.py:215
  62.4 3.0 %collective-permute-start.19 = (f32[8,128]{1,0:T(8,128)S(1)}, f32[8,128]{1,0:T(8,128)S(1)}, u32[]{:S(2)}, u32[]{:S(2)}) collective-permute-start(f32[8,128]{1,0:T(8,128)S(1)} %get-tuple-element.28.refs_0_), channel_id=1, source_target_pairs={{0,3},{1,2},{2,1},{3,0},{4,7},{5,6},{6,5},{7,4},{8,11},{9,10},{10,... | collective-permute-start | bytes 12296 | tf_op jit(solution)/shard_map/ppermute | solution.py:215
  65.4 4.4 %collective-permute-start.20 = (f32[8,128]{1,0:T(8,128)S(1)}, f32[8,128]{1,0:T(8,128)S(1)}, u32[]{:S(2)}, u32[]{:S(2)}) collective-permute-start(f32[8,128]{1,0:T(8,128)S(1)} %add.3.refs_0_), channel_id=1, source_target_pairs={{0,4},{1,5},{2,6},{3,7},{4,0},{5,1},{6,2},{7,3},{8,12},{9,13},{10,... | collective-permute-start | bytes 12296 | tf_op jit(solution)/shard_map/ppermute | solution.py:215
  65.4 4.9 %collective-permute-start.21 = (f32[8,128]{1,0:T(8,128)S(1)}, f32[8,128]{1,0:T(8,128)S(1)}, u32[]{:S(2)}, u32[]{:S(2)}) collective-permute-start(f32[8,128]{1,0:T(8,128)S(1)} %add.3.refs_0_), channel_id=1, source_target_pairs={{0,8},{1,9},{2,10},{3,11},{4,12},{5,13},{6,14},{7,15},{8,0},{9,1},... | collective-permute-start | bytes 12296 | tf_op jit(solution)/shard_map/ppermute | solution.py:215
  68.8 5.4 %collective-permute-start.22 = (f32[8,128]{1,0:T(8,128)S(1)}, f32[8,128]{1,0:T(8,128)S(1)}, u32[]{:S(2)}, u32[]{:S(2)}) collective-permute-start(f32[8,128]{1,0:T(8,128)S(1)} %add.3.refs_0_), channel_id=1, source_target_pairs={{0,12},{1,13},{2,14},{3,15},{4,8},{5,9},{6,10},{7,11},{8,4},{9,5},... | collective-permute-start | bytes 12296 | tf_op jit(solution)/shard_map/ppermute | solution.py:215
  (10 other events, 62.9 us)

commit v3 on v2

--- a/solution.py
+++ b/solution.py
@@ -57,6 +57,19 @@
     return jnp.exp2(exponent * (0.5 * LOG2E / features))
 
 
+def on_diagonal(rows, lanes):
+    shape = (rows, lanes)
+    return lax.broadcasted_iota(jnp.int32, shape, 0) == lax.broadcasted_iota(jnp.int32, shape, 1)
+
+
+def to_lanes(column):
+    return jnp.sum(jnp.where(on_diagonal(column.shape[0], 128), column, 0.0), axis=0, keepdims=True)
+
+
+def to_rows(row, count):
+    return jnp.sum(jnp.where(on_diagonal(count, row.shape[1]), row, 0.0), axis=1, keepdims=True)
+
+
 def stacked(x):
     return jnp.concatenate([piece.astype(F32) for piece in split3(x)], axis=0).astype(B16)
 
@@ -66,7 +79,7 @@
     stack = stacked(x)
     total = None
     for i, piece in enumerate(pieces):
-        count = len(pieces) - i
+        count = 3 - i
         part = dot(stack[: count * rows] if rows % 16 == 0 else stack, piece, 1, axis)
         for k in reversed(range(count)):
             term = part[k * rows : (k + 1) * rows]
@@ -85,11 +98,12 @@
 
 
 def cross_kernel(pts_ref, marks_ref, res_ref, *refs):
-    cross_refs, proj_ref = refs[:-1], refs[-1]
+    cross_refs, refs = refs[:2], refs[2:]
+    proj_ref = refs[0]
     feat = pts_ref.shape[0]
     land = marks_ref.shape[1]
     exponent = dot(rows_side(pts_ref[...]), cols_side(marks_ref[...]), 0, 0)
-    pieces = split3(gauss(exponent, feat))
+    pieces = split3(gauss(exponent, feat))[: len(cross_refs)]
     for ref, piece in zip(cross_refs, pieces):
         ref[...] = piece
     res = res_ref[...]
@@ -98,10 +112,8 @@
     proj_ref[:, land:] = jnp.broadcast_to(squares, (res.shape[0], proj_ref.shape[1] - land))
 
 
-def inverse_kernel(chol_ref, *inv_refs):
-    half = inv_refs[0].shape[1]
-    size = chol_ref.shape[0]
-    base = math.gcd(half, 128)
+def inverse_kernel(chol_ref, inv_ref):
+    size, base = inv_ref.shape
     row = lax.broadcasted_iota(jnp.int32, (base, base), 0)
     col = lax.broadcasted_iota(jnp.int32, (base, base), 1)
     eye = row == col
@@ -123,90 +135,119 @@
         tmp = [fine_dot(jnp.where(mask, blocks[b], 0.0), inverses[b]) for b in range(count)]
         inverses = [inverses[b] - fine_dot(inverses[b], tmp[b]) for b in range(count)]
         step *= 2
-    while step < half:
-        tmp = []
-        for i in range(0, count, 2):
-            lo = i * step
-            tmp.append(fine_dot(chol_ref[lo + step : lo + 2 * step, lo : lo + step], inverses[i]))
+    for b in range(count):
+        inv_ref[b * base : (b + 1) * base, :] = inverses[b]
+
+
+def merge_kernel(chol_ref, part_ref, *inv_refs):
+    size, step = chol_ref.shape[0], part_ref.shape[1]
+    inverses = [part_ref[lo : lo + step, :] for lo in range(0, size, step)]
+    while len(inverses) > 1:
         merged = []
-        for i in range(0, count, 2):
-            low = -fine_dot(inverses[i + 1], tmp[i // 2])
-            top = jnp.concatenate([inverses[i], jnp.zeros((step, step), F32)], axis=1)
+        for i in range(0, len(inverses), 2):
+            lo, zero = i * step, jnp.zeros((step, step), F32)
+            block, cut = chol_ref[lo + step : lo + 2 * step, lo : lo + step], step // 2
+            low = fine_dot(block, inverses[i]) if step < 256 else jnp.concatenate(
+                [fine_dot(block, inverses[i][:, :cut]), fine_dot(block[:, cut:], inverses[i][cut:, cut:])], axis=1
+            )
+            other = inverses[i + 1]
+            low = -(fine_dot(other, low) if step < 256 else jnp.concatenate(
+                [fine_dot(other[:cut, :cut], low[:cut]), fine_dot(other[cut:], low)], axis=0
+            ))
+            if len(inverses) == 2:
+                for ref, c, nw, sw, se in zip(inv_refs, split3(zero), split3(inverses[0]), split3(low), split3(inverses[1])):
+                    ref[:step, :step] = nw
+                    ref[:step, step:] = c
+                    ref[step:, :step] = sw
+                    ref[step:, step:] = se
+                return
+            top = jnp.concatenate([inverses[i], zero], axis=1)
             merged.append(jnp.concatenate([top, jnp.concatenate([low, inverses[i + 1]], axis=1)], axis=0))
         inverses = merged
-        count //= 2
         step *= 2
-    for i in range(count):
-        for ref, piece in zip(inv_refs, split3(inverses[i])):
-            ref[i * half : (i + 1) * half, :] = piece
 
 
 def direction_kernel(ridge_ref, rz_ref, *refs):
     proj_refs, refs = refs[:4], refs[4:]
-    chol_ref, refs = refs[0], refs[1:]
-    inv_refs, cross_refs, refs = refs[:3], refs[3:6], refs[6:]
-    res_ref, dir_ref, new_ref, low_ref, inner_ref = refs
+    inv_refs, cross_refs, refs = refs[:3], refs[3:5], refs[5:]
+    res_ref, dir_ref, new_ref, near_ref, low_ref, inner_ref = refs
     land = cross_refs[0].shape[1]
-    half = inv_refs[0].shape[1]
+    half = land // 2
     ridge = ridge_ref[0]
     lane = lax.broadcasted_iota(jnp.int32, inner_ref.shape, 0)
     rz = sum(jnp.where(lane == i, rz_ref[i], 0.0) for i in range(inner_ref.shape[0]))
     sums = (proj_refs[0][...] + proj_refs[1][...]) + (proj_refs[2][...] + proj_refs[3][...])
     proj = sums[:, :land]
     squares = sums[:, land : land + 1]
-    below = split3(chol_ref[half:, :half])
-    upper = [ref[:half] for ref in inv_refs]
-    lower = [ref[half:] for ref in inv_refs]
-    y0 = wide_dot(proj[:, :half], upper, 1)
-    y1 = wide_dot(proj[:, half:] - wide_dot(y0, below, 1), lower, 1)
-    x1 = wide_dot(y1, lower, 0)
-    x0 = wide_dot(y0 - wide_dot(x1, below, 0), upper, 0)
+    north = [ref[:half, :half] for ref in inv_refs]
+    south = [ref[half:] for ref in inv_refs]
+    y0 = wide_dot(proj[:, :half], north, 1)
+    y1 = wide_dot(proj, south, 1)
+    x0 = wide_dot(jnp.concatenate([y0, y1], axis=1), [ref[:, :half] for ref in inv_refs], 0)
+    x1 = wide_dot(y1, [ref[half:, half:] for ref in inv_refs], 0)
     coeffs = jnp.concatenate([x0, x1], axis=1)
     inner = (squares - jnp.sum(proj * coeffs, axis=1, keepdims=True)) / ridge
     precond = (res_ref[...] - wide_dot(coeffs, [ref[...] for ref in cross_refs], 1)) / ridge
     new = precond + (inner / rz) * dir_ref[...]
     new_ref[...] = new
+    near_ref[...] = new
     low_ref[...] = new.astype(B16)
     inner_ref[...] = inner
 
 
-def products(points_at, first, own_lhs, pts_ref, low_ref, total):
-    feat, width = pts_ref.shape[0], own_lhs.shape[1]
-    group = math.gcd(len(points_at), 4)
-    for i in range(0, len(points_at), group):
-        pts = jnp.concatenate(
-            [pts_ref[:, at * width : (at + 1) * width] for at in points_at[i : i + group]], axis=1
-        )
-        kernel = gauss(dot(rows_side(pts), own_lhs[...], 0, 0), feat).astype(B16)
-        at = (first + i) * width
-        total = total + dot(low_ref[:, at : at + group * width], kernel, 1, 0)
-    return total
-
-
-def near_kernel(points_at, own_ref, pts_ref, low_ref, total_ref, lhs_ref):
+def tile(pts, lhs):
+    return gauss(dot(rows_side(pts), lhs, 0, 0), pts.shape[0]).astype(B16)
+
+
+def tiles_kernel(first, own_ref, pts_ref, tiles_ref):
+    width = own_ref.shape[1]
+    lhs = cols_side(own_ref[...])
+    group = math.gcd(tiles_ref.shape[0] // width, 2)
+    for at in range(0, tiles_ref.shape[0], group * width):
+        pts = pts_ref[:, first * width + at : first * width + at + group * width]
+        tiles_ref[at : at + group * width, :] = tile(pts, lhs)
+
+
+def near_kernel(low_ref, tiles_ref, total_ref):
+    total_ref[...] = dot(low_ref[...], tiles_ref[: low_ref.shape[1], :], 1, 0)
+
+
+def image_kernel(
+    low_at, near, ridge_ref, own_ref, pts_ref, low_ref, near_ref, early_ref, late_ref, new_ref, image_ref, curv_ref, lhs_ref
+):
+    width = own_ref.shape[1]
     lhs_ref[...] = cols_side(own_ref[...])
-    total_ref[...] = products(points_at, 0, lhs_ref, pts_ref, low_ref, jnp.zeros(total_ref.shape, F32))
-
-
-def image_kernel(points_at, first, ridge_ref, own_ref, pts_ref, low_ref, near_ref, new_ref, image_ref, curv_ref, lhs_ref):
-    lhs_ref[...] = cols_side(own_ref[...])
-    total = products(points_at, first, lhs_ref, pts_ref, low_ref, near_ref[...])
+
+    def low(blocks):
+        return jnp.concatenate(
+            [low_ref[:, low_at[b] * width : (low_at[b] + 1) * width].astype(F32) for b in blocks], axis=1
+        ).astype(B16)
+
+    early = early_ref.shape[0] // width
+    held = early + late_ref.shape[0] // width
+    blocks = len(low_at)
+    total = near_ref[...]
+    left = blocks - held
+    group = max(g for g in range(1, 3) if left % g == 0)
+    for b in range(held, blocks, group):
+        pts = pts_ref[:, b * width : (b + group) * width]
+        total = total + dot(low(range(b, b + group)), tile(pts, lhs_ref[...]), 1, 0)
+    total = total + dot(low(range(near, early)), early_ref[near * width :, :], 1, 0)
+    total = total + dot(low(range(early, held)), late_ref[...], 1, 0)
     new = new_ref[...]
     image = total + ridge_ref[0] * new
     image_ref[...] = image
     curv = jnp.sum(new * image, axis=1, keepdims=True)
-    curv_ref[...] = jnp.broadcast_to(curv, curv_ref.shape)
+    curv_ref[...] = jnp.broadcast_to(to_lanes(curv)[None], curv_ref.shape)
 
 
 def update_kernel(*refs):
-    curv_refs, refs = refs[:4], refs[4:]
+    curv_ref, refs = refs[0], refs[1:]
     inner_ref, sol_ref, res_ref, new_ref, image_ref, sol_out, res_out, inner_out = refs
-    curv = (curv_refs[0][...] + curv_refs[1][...]) + (curv_refs[2][...] + curv_refs[3][...])
+    curv = to_rows(jnp.sum(curv_ref[...], axis=0), inner_ref.shape[0])
     inner = inner_ref[...]
-    alpha = inner / curv[:, :1]
-    n = inner.shape[0]
-    eye = lax.broadcasted_iota(jnp.int32, (n, n), 0) == lax.broadcasted_iota(jnp.int32, (n, n), 1)
-    inner_out[...] = jnp.sum(jnp.where(eye, inner, 0.0), axis=0, keepdims=True)
+    alpha = inner / curv
+    inner_out[...] = to_lanes(inner)[:, : inner.shape[0]]
     sol_out[...] = sol_ref[...] + alpha * new_ref[...]
     res_out[...] = res_ref[...] - alpha * image_ref[...]
 
@@ -295,42 +336,58 @@
     far_stages = [[m] for masks in reversed(lower) for m in masks[1::-1]]
     *cross, partial = call(
         cross_kernel,
-        (shape((width, land), B16),) * 3 + (shape((outs, land + 128), F32),),
+        (shape((width, land), B16),) * 2 + (shape((outs, land + 128), F32),),
         points, landmarks, residual, name="cross", room=24, work=5 * width * land * depth,
     )
+    *quick, last = levels[0][:2]
+    if quick:
+        partial = add_up([partial, exchange(partial, quick[0], count)])
+    base = math.gcd(land, 128)
     inverse = call(
-        inverse_kernel, (shape((land, land // 2), B16),) * 3, chol,
-        name="inverse", work=width * land * depth, after=(partial,),
-    )
-    partial = add_up(all_sum(partial, levels[:1], count), inverse[:1])
+        inverse_kernel, shape((land, base), F32), chol, name="inverse", work=width * land * depth, after=(partial,)
+    )
+    partial = add_up([partial, exchange(partial, last, count)], (inverse,))
     near_points, near_order = gather(points, [0], [top], count, [(partial,)])
+    merged = call(
+        merge_kernel, (shape((land, land), B16),) * 3, chol, inverse,
+        name="merge", work=2 * width * land * depth, room=24, after=(partial,),
+    )
     proj = all_sum(partial, levels[1:], count)
-    new, low, inner = call(
+    new, new_kept, low, inner = call(
         direction_kernel,
-        (shape((outs, width), F32), shape((outs, width), B16), shape((outs, 1), F32)),
-        ridge, rz_prev, *proj, chol, *inverse, *cross, residual, direction,
+        (shape((outs, width), F32),) * 2 + (shape((outs, width), B16), shape((outs, 1), F32)),
+        ridge, rz_prev, *proj, *merged, *cross, residual, direction,
         smem=(0, 1), name="direction", room=24, work=6 * width * land * depth,
     )
-    all_points, point_order = gather(near_points, near_order, far_stages, count, [(new,)])
-    near_low, low_order = gather(low, [0], [top], count)
-    near = call(
-        functools.partial(near_kernel, [near_order.index(m) for m in low_order]),
-        shape((outs, width), F32),
-        points, near_points, near_low, scratch=(side,), name="near", room=32,
-        work=2 * len(low_order) * width * width * depth,
-    )
-    first = len(low_order)
-    all_low, low_order = gather(near_low, low_order, lower[::-1], count, [(near,)])
+    early_points, early_order = gather(near_points, near_order, far_stages[:1], count, [(inner,)])
+    early = len(early_order)
+    early_tiles = call(
+        functools.partial(tiles_kernel, 0), shape((early * width, width), B16), points, early_points,
+        name="tiles", room=14, work=early * width * width * depth, after=(inner,),
+    )
+    near_low, low_order = gather(low, [0], [top], count, [(early_tiles,)])
+    near = len(low_order)
+    near_sum = call(
+        near_kernel, shape((outs, width), F32), near_low, early_tiles, name="near", room=2,
+        work=near * width * width * depth // 2,
+    )
+    all_points, point_order = gather(early_points, early_order, far_stages[1:], count)
+    late = 3
+    late_tiles = call(
+        functools.partial(tiles_kernel, early), shape((late * width, width), B16), points, all_points,
+        name="tiles", room=14, work=late * width * width * depth, after=(near_sum,),
+    )
+    all_low, low_order = gather(near_low, low_order, lower[::-1], count, [(late_tiles,)])
     image, curv = call(
-        functools.partial(image_kernel, [point_order.index(m) for m in low_order[first:]], first),
-        (shape((outs, width), F32), shape((outs, 128), F32)),
-        ridge, points, all_points, all_low, near, new, smem=(0,),
-        scratch=(side,), name="image", room=32, work=2 * (count - first) * width * width * depth,
+        functools.partial(image_kernel, [low_order.index(m) for m in point_order], near),
+        (shape((outs, width), F32), shape((count, 1, 128), F32)),
+        ridge, points, all_points, all_low, near_sum, early_tiles, late_tiles, new_kept, smem=(0,),
+        scratch=(side,), name="image", room=14, work=2 * (count - early - late) * width * width * depth,
     )
     sol_new, res_new, inner_row = call(
         update_kernel,
         (shape((outs, width), F32),) * 2 + (shape((1, outs), F32),),
-        *all_sum(curv, levels, count), inner, solution, residual, new, image, name="update",
+        lax.all_to_all(curv, "rows", 0, 0, tiled=True), inner, solution, residual, new_kept, image, name="update",
     )
     return (sol_new, res_new, new, inner_row.reshape(outs))
 

time: 75.3 us -> 68.6 us (0.911)
  waiting for transfers between devices: 14.7 us -> 1.54 us
  blocking collectives: 0 us -> 11.8 us
  starting transfers between devices: 26.4 us -> 19.3 us
  Pallas kernels: 28.3 us -> 31.5 us
  local copies, waits for them, and re-layouts: 3.96 us -> 2.63 us
    ppermute x23 -> x16, waiting for transfers between devices: 14.7 us -> 1.54 us  [exchange(): return lax.ppermute(x, 'rows', [(i, i ^ mask) for i in range(count)])]
    all_to_all x0 -> x1, blocking collectives: none -> 11.8 us  [local(): lax.all_to_all(curv, 'rows', 0, 0, tiled=True)]
    ppermute x23 -> x16, starting transfers between devices: 26.4 us -> 19.3 us  [exchange(): return lax.ppermute(x, 'rows', [(i, i ^ mask) for i in range(count)])]
    pallas_call x13 -> x16, Pallas kernels: 28.3 us -> 31.5 us  [call(): pl.pallas_call(body, out_shape=out, in_specs=[ANY if i < len(after) else...]
    unnamed x22 -> x18, local copies, waits for them, and re-layouts: 3.96 us -> 2.63 us
  transfers between devices with their start and end apart: 23 -> 16, of which waited for: 8 -> 2; matrix products, arithmetic and copies ran while one was open for 0% -> 0% of each run, Pallas kernels for 23% -> 35%
where the time goes in v3:
time: 68.6 us; the launch traced here: 68.3 us
  Pallas kernels  31.5 us (46%)
  starting transfers between devices  19.3 us (28%)
  blocking collectives  11.8 us (17%)
  local copies, waits for them, and re-layouts  2.63 us (4%)
  between operations  1.55 us (2%)
  waiting for transfers between devices  1.54 us (2%)
    pallas_call x16, Pallas kernels, call(): pl.pallas_call(body, out_shape=out, in_specs=[ANY if i < len(after) else...  31.5 us
    ppermute x16, starting transfers between devices, exchange(): return lax.ppermute(x, 'rows', [(i, i ^ mask) for i in range(count)])  19.3 us
    all_to_all x1, blocking collectives, local(): lax.all_to_all(curv, 'rows', 0, 0, tiled=True)  11.8 us
    unnamed x18, local copies, waits for them, and re-layouts  2.63 us
    ppermute x16, waiting for transfers between devices, exchange(): return lax.ppermute(x, 'rows', [(i, i ^ mask) for i in range(count)])  1.54 us
  transfers between devices with their start and end apart: 16, of which 2 were waited for; matrix products, arithmetic and copies ran while one was open for 0% of the time, Pallas kernels for 35%

profile of v3, /device:TPU:0, one launch (start us, length us, event | category | flops | bytes accessed | tf_op | source)
XLA Modules:
  0.0 68.3 jit_solution(2283115015813741996)
XLA Ops:
  0.6 5.1 %collective-permute-start.7 = (bf16[64,1024]{1,0:T(8,128)(2,1)}, bf16[64,1024]{1,0:T(8,128)(2,1)S(1)}, u32[]{:S(2)}, u32[]{:S(2)}) collective-permute-start(bf16[64,1024]{1,0:T(8,128)(2,1)} %own_ref.1), channel_id=1, source_target_pairs={{0,12},{1,13},{2,14},{3,15},{4,8},{5,9},{6,10},{7,11},{8,4},{9,5},... | collective-permute-start | bytes 393224 | tf_op jit(solution)/shard_map/ppermute | solution.py:256
  5.7 0.6 collective-permute-start.5
  6.4 0.9 %copy-done.1 = bf16[64,1024]{1,0:T(8,128)(2,1)S(1)} copy-done((bf16[64,1024]{1,0:T(8,128)(2,1)S(1)}, bf16[64,1024]{1,0:T(8,128)(2,1)}, u32[]{:S(2)}) %copy-start.1) | copy-done | bytes 131096
  7.3 0.8 %copy-done.3 = f32[8,1024]{1,0:T(8,128)S(1)} copy-done((f32[8,1024]{1,0:T(8,128)S(1)}, f32[8,1024]{1,0:T(8,128)}, u32[]{:S(2)}) %copy-start.3) | copy-done | bytes 32792
  8.1 0.9 %copy-done.6 = bf16[64,1024]{1,0:T(8,128)(2,1)S(1)} copy-done((bf16[64,1024]{1,0:T(8,128)(2,1)S(1)}, bf16[64,1024]{1,0:T(8,128)(2,1)}, u32[]{:S(2)}) %copy-start.6) | copy-done | bytes 131096
  9.0 1.6 %cross.1 = (bf16[1024,1024]{1,0:T(8,128)(2,1)S(1)}, bf16[1024,1024]{1,0:T(8,128)(2,1)S(1)}, f32[8,1152]{1,0:T(8,128)S(1)}) custom-call(bf16[64,1024]{1,0:T(8,128)(2,1)S(1)} %copy-done.1, bf16[64,1024]{1,0:T(8,128)(2,1)S(1)} %copy-done.6, f32[8,1024]{1,0:T(8,128)S(1)} %copy-done.3), custom_call_target="tpu_custom_call" | custom-call | flops 2684354560 | tf_op jit(solution)/shard_map/cross/pallas_call | solution.py:313
  10.7 1.2 %collective-permute-done.refs_1_ = f32[8,1152]{1,0:T(8,128)S(1)} collective-permute-done((f32[8,1152]{1,0:T(8,128)S(1)}, f32[8,1152]{1,0:T(8,128)S(1)}, u32[]{:S(2)}, u32[]{:S(2)}) %collective-permute-start) | collective-permute-done | bytes 36896 | tf_op jit(solution)/shard_map/ppermute | solution.py:256
  11.9 1.7 %collective-permute-start.1 = (f32[8,1152]{1,0:T(8,128)S(1)}, f32[8,1152]{1,0:T(8,128)S(1)}, u32[]{:S(2)}, u32[]{:S(2)}) collective-permute-start(f32[8,1152]{1,0:T(8,128)S(1)} %add.2.refs_0_.refs_1_), channel_id=1, source_target_pairs={{0,2},{1,3},{2,0},{3,1},{4,6},{5,7},{6,4},{7,5},{8,10},{9,11},{10,... | collective-permute-start | bytes 110600 | tf_op jit(solution)/shard_map/ppermute | solution.py:256
  13.7 4.0 %inverse.1.refs_0_.refs_2_ = f32[1024,128]{1,0:T(8,128)S(1)} custom-call(f32[8,1152]{1,0:T(8,128)S(1)} %add.2.refs_0_.refs_1_, f32[1024,1024]{1,0:T(8,128)S(1)} %copy-done), custom_call_target="tpu_custom_call" | custom-call | flops 536870912 | tf_op jit(solution)/shard_map/inverse/pallas_call | solution.py:313
  17.8 0.9 %collective-permute-start.8 = (bf16[64,4096]{1,0:T(8,128)(2,1)S(1)}, bf16[64,4096]{1,0:T(8,128)(2,1)S(1)}, u32[]{:S(2)}, u32[]{:S(2)}) collective-permute-start(bf16[64,4096]{1,0:T(8,128)(2,1)S(1)} %join.5.refs_1_), channel_id=1, source_target_pairs={{0,2},{1,3},{2,0},{3,1},{4,6},{5,7},{6,4},{7,5},{8,10},{9,11},{10,... | collective-permute-start | bytes 1572872 | tf_op jit(solution)/shard_map/ppermute | solution.py:256
  19.4 3.4 %collective-permute-start.4 = (f32[8,1152]{1,0:T(8,128)S(1)}, f32[8,1152]{1,0:T(8,128)S(1)}, u32[]{:S(2)}, u32[]{:S(2)}) collective-permute-start(f32[8,1152]{1,0:T(8,128)S(1)} %add.3.refs_0_), channel_id=1, source_target_pairs={{0,12},{1,13},{2,14},{3,15},{4,8},{5,9},{6,10},{7,11},{8,4},{9,5},... | collective-permute-start | bytes 110600 | tf_op jit(solution)/shard_map/ppermute | solution.py:256
  22.7 1.1 %collective-permute-start.2 = (f32[8,1152]{1,0:T(8,128)S(1)}, f32[8,1152]{1,0:T(8,128)S(1)}, u32[]{:S(2)}, u32[]{:S(2)}) collective-permute-start(f32[8,1152]{1,0:T(8,128)S(1)} %add.3.refs_0_), channel_id=1, source_target_pairs={{0,4},{1,5},{2,6},{3,7},{4,0},{5,1},{6,2},{7,3},{8,12},{9,13},{10,... | collective-permute-start | bytes 110600 | tf_op jit(solution)/shard_map/ppermute | solution.py:256
  23.8 5.4 %merge.1 = (bf16[1024,1024]{1,0:T(8,128)(2,1)S(1)}, bf16[1024,1024]{1,0:T(8,128)(2,1)S(1)}, bf16[1024,1024]{1,0:T(8,128)(2,1)S(1)}) custom-call(f32[8,1152]{1,0:T(8,128)S(1)} %add.3.refs_0_, f32[1024,1024]{1,0:T(8,128)S(1)} %copy-done, f32[1024,128]{1,0:T(8,128)S(1)} %inverse.1.refs_0_.refs_2_), custom_call_target="tpu_custom_call" | custom-call | flops 1073741824 | tf_op jit(solution)/shard_map/merge/pallas_call | solution.py:313
  29.3 4.9 %direction.1 = (f32[8,1024]{1,0:T(8,128)}, f32[8,1024]{1,0:T(8,128)S(1)}, bf16[8,1024]{1,0:T(8,128)(2,1)S(1)}, f32[8,1]{1,0:T(8,128)S(1)}) custom-call(f32[1]{0:T(128)S(6)} %copy.12.ridge_ref, f32[8]{0:T(128)S(1)} %copy-done.8, f32[8,1152]{1,0:T(8,128)S(1)} %add.3.refs_0_, f32[8,1152]{1,0:T(8,128)S(1)} %collective-permute-done.2.refs_1_, ...), custom_call_target="tpu_custom_call" | custom-call | flops 3221225472 | tf_op jit(solution)/shard_map/direction/pallas_call | solution.py:313
  34.3 3.4 %collective-permute-start.12 = (bf16[8,1024]{1,0:T(8,128)(2,1)S(1)}, bf16[8,1024]{1,0:T(8,128)(2,1)S(1)}, u32[]{:S(2)}, u32[]{:S(2)}) collective-permute-start(bf16[8,1024]{1,0:T(8,128)(2,1)S(1)} %get-tuple-element.26.refs_1_), channel_id=1, source_target_pairs={{0,12},{1,13},{2,14},{3,15},{4,8},{5,9},{6,10},{7,11},{8,4},{9,5},... | collective-permute-start | bytes 49160 | tf_op jit(solution)/shard_map/ppermute | solution.py:256
  37.7 1.1 %collective-permute-start.10 = (bf16[8,1024]{1,0:T(8,128)(2,1)S(1)}, bf16[8,1024]{1,0:T(8,128)(2,1)S(1)}, u32[]{:S(2)}, u32[]{:S(2)}) collective-permute-start(bf16[8,1024]{1,0:T(8,128)(2,1)S(1)} %get-tuple-element.26.refs_1_), channel_id=1, source_target_pairs={{0,4},{1,5},{2,6},{3,7},{4,0},{5,1},{6,2},{7,3},{8,12},{9,13},{10,... | collective-permute-start | bytes 49160 | tf_op jit(solution)/shard_map/ppermute | solution.py:256
  38.8 4.9 %tiles.2.refs_0_.tiles_ref.early_ref = bf16[8192,1024]{1,0:T(8,128)(2,1)S(1)} custom-call(f32[8,1]{1,0:T(8,128)S(1)} %get-tuple-element.25.refs_0_.refs_1_, bf16[64,1024]{1,0:T(8,128)(2,1)S(1)} %copy-done.2, bf16[64,8192]{1,0:T(8,128)(2,1)S(1)} %join.6.refs_0_.refs_2_), custom_call_target="tpu_custom_call" | custom-call | flops 4294967296 | tf_op jit(solution)/shard_map/tiles/pallas_call | solution.py:313
  43.7 0.6 collective-permute-start.15
  44.2 0.8 %collective-permute-start.14 = (bf16[8,4096]{1,0:T(8,128)(2,1)S(1)}, bf16[8,4096]{1,0:T(8,128)(2,1)S(1)}, u32[]{:S(2)}, u32[]{:S(2)}) collective-permute-start(bf16[8,4096]{1,0:T(8,128)(2,1)S(1)} %join.8.low_ref.refs_1_), channel_id=1, source_target_pairs={{0,2},{1,3},{2,0},{3,1},{4,6},{5,7},{6,4},{7,5},{8,10},{9,11},{10,... | collective-permute-start | bytes 196616 | tf_op jit(solution)/shard_map/ppermute | solution.py:256
  45.6 1.2 %near.1.refs_0_.near_ref = f32[8,1024]{1,0:T(8,128)S(1)} custom-call(bf16[8,4096]{1,0:T(8,128)(2,1)S(1)} %join.8.low_ref.refs_1_, bf16[8192,1024]{1,0:T(8,128)(2,1)S(1)} %tiles.2.refs_0_.tiles_ref.early_ref), custom_call_target="tpu_custom_call" | custom-call | flops 1073741824 | tf_op jit(solution)/shard_map/near/pallas_call | solution.py:313
  46.9 1.9 %tiles.3.refs_0_.late_ref = bf16[3072,1024]{1,0:T(8,128)(2,1)S(1)} custom-call(f32[8,1024]{1,0:T(8,128)S(1)} %near.1.refs_0_.near_ref, bf16[64,1024]{1,0:T(8,128)(2,1)S(1)} %copy-done.2, bf16[64,16384]{1,0:T(8,128)(2,1)S(1)} %join.7.refs_2_.pts_ref), custom_call_target="tpu_custom_call" | custom-call | flops 1610612736 | tf_op jit(solution)/shard_map/tiles/pallas_call | solution.py:313
  49.2 6.5 %image.1 = (f32[8,1024]{1,0:T(8,128)S(1)}, f32[16,1,128]{2,1,0:T(1,128)S(1)}) custom-call(f32[1]{0:T(128)S(6)} %copy.12.ridge_ref, bf16[64,1024]{1,0:T(8,128)(2,1)S(1)} %copy-done.2, bf16[64,16384]{1,0:T(8,128)(2,1)S(1)} %join.7.refs_2_.pts_ref, bf16[8,16384]{1,0:T(8,128)(2,1)S(1)} %join.9.low_ref, f32[8,1024]{1,0:T(8,128)S(1)} %near.1.refs_0_.near_ref, ...), custom_call_target="tpu_custom_call" | custom-call | flops 5368709120 | tf_op jit(solution)/shard_map/image/pallas_call | solution.py:313
  55.7 11.8 %all_to_all.5.refs_0_ = f32[16,1,128]{2,1,0:T(1,128)S(1)} all-to-all(f32[16,1,128]{2,1,0:T(1,128)S(1)} %get-tuple-element.28), channel_id=1, replica_groups=mesh['groups'=2,'rows'=16] {'rows'}, dimensions={0} | all-to-all | bytes 16384 | tf_op jit(solution)/shard_map/all_to_all | solution.py:390
  67.5 0.8 %update.1 = (f32[8,1024]{1,0:T(8,128)}, f32[8,1024]{1,0:T(8,128)}, f32[1,8]{1,0:T(1,128)}) custom-call(f32[16,1,128]{2,1,0:T(1,128)S(1)} %all_to_all.5.refs_0_, f32[8,1]{1,0:T(8,128)S(1)} %get-tuple-element.25.refs_0_.refs_1_, f32[8,1024]{1,0:T(8,128)S(1)} %copy-done.5, f32[8,1024]{1,0:T(8,128)S(1)} %copy-done.4, ...), custom_call_target="tpu_custom_call" | custom-call | tf_op jit(solution)/shard_map/update/pallas_call | solution.py:313
  (43 shorter events, 1.4 us)
Async XLA Ops:
  0.6 17.1 %collective-permute-start.7 = (bf16[64,1024]{1,0:T(8,128)(2,1)}, bf16[64,1024]{1,0:T(8,128)(2,1)S(1)}, u32[]{:S(2)}, u32[]{:S(2)}) collective-permute-start(bf16[64,1024]{1,0:T(8,128)(2,1)} %own_ref.1), channel_id=1, source_target_pairs={{0,12},{1,13},{2,14},{3,15},{4,8},{5,9},{6,10},{7,11},{8,4},{9,5},... | collective-permute-start | bytes 393224 | tf_op jit(solution)/shard_map/ppermute | solution.py:256
  5.7 12.0 %collective-permute-start.6 = (bf16[64,1024]{1,0:T(8,128)(2,1)}, bf16[64,1024]{1,0:T(8,128)(2,1)S(1)}, u32[]{:S(2)}, u32[]{:S(2)}) collective-permute-start(bf16[64,1024]{1,0:T(8,128)(2,1)} %own_ref.1), channel_id=1, source_target_pairs={{0,8},{1,9},{2,10},{3,11},{4,12},{5,13},{6,14},{7,15},{8,0},{9,1},... | collective-permute-start | bytes 393224 | tf_op jit(solution)/shard_map/ppermute | solution.py:256
  5.7 12.0 %collective-permute-start.5 = (bf16[64,1024]{1,0:T(8,128)(2,1)}, bf16[64,1024]{1,0:T(8,128)(2,1)S(1)}, u32[]{:S(2)}, u32[]{:S(2)}) collective-permute-start(bf16[64,1024]{1,0:T(8,128)(2,1)} %own_ref.1), channel_id=1, source_target_pairs={{0,4},{1,5},{2,6},{3,7},{4,0},{5,1},{6,2},{7,3},{8,12},{9,13},{10,... | collective-permute-start | bytes 393224 | tf_op jit(solution)/shard_map/ppermute | solution.py:256
  6.4 0.9 %copy-start.1 = (bf16[64,1024]{1,0:T(8,128)(2,1)S(1)}, bf16[64,1024]{1,0:T(8,128)(2,1)}, u32[]{:S(2)}) copy-start(bf16[64,1024]{1,0:T(8,128)(2,1)} %own_ref.1) | copy-start | bytes 393220
  8.1 0.9 %copy-start.6 = (bf16[64,1024]{1,0:T(8,128)(2,1)S(1)}, bf16[64,1024]{1,0:T(8,128)(2,1)}, u32[]{:S(2)}) copy-start(bf16[64,1024]{1,0:T(8,128)(2,1)} %marks_ref.1) | copy-start | bytes 393220
  9.0 4.7 %copy-start = (f32[1024,1024]{1,0:T(8,128)S(1)}, f32[1024,1024]{1,0:T(8,128)}, u32[]{:S(2)}) copy-start(f32[1024,1024]{1,0:T(8,128)} %refs_1_.6) | copy-start | bytes 12582916
  10.6 1.3 %collective-permute-start = (f32[8,1152]{1,0:T(8,128)S(1)}, f32[8,1152]{1,0:T(8,128)S(1)}, u32[]{:S(2)}, u32[]{:S(2)}) collective-permute-start(f32[8,1152]{1,0:T(8,128)S(1)} %get-tuple-element.19.refs_0_), channel_id=1, source_target_pairs={{0,1},{1,0},{2,3},{3,2},{4,5},{5,4},{6,7},{7,6},{8,9},{9,8},{10,11... | collective-permute-start | bytes 110600 | tf_op jit(solution)/shard_map/ppermute | solution.py:256
  11.9 5.8 %copy-start.2 = (bf16[64,1024]{1,0:T(8,128)(2,1)S(1)}, bf16[64,1024]{1,0:T(8,128)(2,1)}, u32[]{:S(2)}) copy-start(bf16[64,1024]{1,0:T(8,128)(2,1)} %own_ref.1) | copy-start | bytes 393220
  11.9 5.8 %collective-permute-start.1 = (f32[8,1152]{1,0:T(8,128)S(1)}, f32[8,1152]{1,0:T(8,128)S(1)}, u32[]{:S(2)}, u32[]{:S(2)}) collective-permute-start(f32[8,1152]{1,0:T(8,128)S(1)} %add.2.refs_0_.refs_1_), channel_id=1, source_target_pairs={{0,2},{1,3},{2,0},{3,1},{4,6},{5,7},{6,4},{7,5},{8,10},{9,11},{10,... | collective-permute-start | bytes 110600 | tf_op jit(solution)/shard_map/ppermute | solution.py:256
  17.8 16.4 %collective-permute-start.8 = (bf16[64,4096]{1,0:T(8,128)(2,1)S(1)}, bf16[64,4096]{1,0:T(8,128)(2,1)S(1)}, u32[]{:S(2)}, u32[]{:S(2)}) collective-permute-start(bf16[64,4096]{1,0:T(8,128)(2,1)S(1)} %join.5.refs_1_), channel_id=1, source_target_pairs={{0,2},{1,3},{2,0},{3,1},{4,6},{5,7},{6,4},{7,5},{8,10},{9,11},{10,... | collective-permute-start | bytes 1572872 | tf_op jit(solution)/shard_map/ppermute | solution.py:256
  19.3 9.9 %copy-start.4 = (f32[8,1024]{1,0:T(8,128)S(1)}, f32[8,1024]{1,0:T(8,128)}, u32[]{:S(2)}) copy-start(f32[8,1024]{1,0:T(8,128)} %refs_3_.1) | copy-start | bytes 98308
  19.3 9.9 %copy-start.7 = (f32[8,1024]{1,0:T(8,128)S(1)}, f32[8,1024]{1,0:T(8,128)}, u32[]{:S(2)}) copy-start(f32[8,1024]{1,0:T(8,128)} %refs_10_.1) | copy-start | bytes 98308
  19.3 9.9 %copy-start.8 = (f32[8]{0:T(128)S(1)}, f32[8]{0:T(128)}, u32[]{:S(2)}) copy-start(f32[8]{0:T(128)} %rz_ref.1) | copy-start | bytes 100
  19.4 9.8 %collective-permute-start.4 = (f32[8,1152]{1,0:T(8,128)S(1)}, f32[8,1152]{1,0:T(8,128)S(1)}, u32[]{:S(2)}, u32[]{:S(2)}) collective-permute-start(f32[8,1152]{1,0:T(8,128)S(1)} %add.3.refs_0_), channel_id=1, source_target_pairs={{0,12},{1,13},{2,14},{3,15},{4,8},{5,9},{6,10},{7,11},{8,4},{9,5},... | collective-permute-start | bytes 110600 | tf_op jit(solution)/shard_map/ppermute | solution.py:256
  22.7 6.5 %collective-permute-start.3 = (f32[8,1152]{1,0:T(8,128)S(1)}, f32[8,1152]{1,0:T(8,128)S(1)}, u32[]{:S(2)}, u32[]{:S(2)}) collective-permute-start(f32[8,1152]{1,0:T(8,128)S(1)} %add.3.refs_0_), channel_id=1, source_target_pairs={{0,8},{1,9},{2,10},{3,11},{4,12},{5,13},{6,14},{7,15},{8,0},{9,1},... | collective-permute-start | bytes 110600 | tf_op jit(solution)/shard_map/ppermute | solution.py:256
  22.7 6.5 %collective-permute-start.2 = (f32[8,1152]{1,0:T(8,128)S(1)}, f32[8,1152]{1,0:T(8,128)S(1)}, u32[]{:S(2)}, u32[]{:S(2)}) collective-permute-start(f32[8,1152]{1,0:T(8,128)S(1)} %add.3.refs_0_), channel_id=1, source_target_pairs={{0,4},{1,5},{2,6},{3,7},{4,0},{5,1},{6,2},{7,3},{8,12},{9,13},{10,... | collective-permute-start | bytes 110600 | tf_op jit(solution)/shard_map/ppermute | solution.py:256
  34.2 12.6 %collective-permute-start.9 = (bf16[64,8192]{1,0:T(8,128)(2,1)S(1)}, bf16[64,8192]{1,0:T(8,128)(2,1)S(1)}, u32[]{:S(2)}, u32[]{:S(2)}) collective-permute-start(bf16[64,8192]{1,0:T(8,128)(2,1)S(1)} %join.6.refs_0_.refs_2_), channel_id=1, source_target_pairs={{0,1},{1,0},{2,3},{3,2},{4,5},{5,4},{6,7},{7,6},{8,9},{9,8},{10,11... | collective-permute-start | bytes 3145736 | tf_op jit(solution)/shard_map/ppermute | solution.py:256
  34.3 9.3 %collective-permute-start.12 = (bf16[8,1024]{1,0:T(8,128)(2,1)S(1)}, bf16[8,1024]{1,0:T(8,128)(2,1)S(1)}, u32[]{:S(2)}, u32[]{:S(2)}) collective-permute-start(bf16[8,1024]{1,0:T(8,128)(2,1)S(1)} %get-tuple-element.26.refs_1_), channel_id=1, source_target_pairs={{0,12},{1,13},{2,14},{3,15},{4,8},{5,9},{6,10},{7,11},{8,4},{9,5},... | collective-permute-start | bytes 49160 | tf_op jit(solution)/shard_map/ppermute | solution.py:256
  37.7 6.0 %collective-permute-start.11 = (bf16[8,1024]{1,0:T(8,128)(2,1)S(1)}, bf16[8,1024]{1,0:T(8,128)(2,1)S(1)}, u32[]{:S(2)}, u32[]{:S(2)}) collective-permute-start(bf16[8,1024]{1,0:T(8,128)(2,1)S(1)} %get-tuple-element.26.refs_1_), channel_id=1, source_target_pairs={{0,8},{1,9},{2,10},{3,11},{4,12},{5,13},{6,14},{7,15},{8,0},{9,1},... | collective-permute-start | bytes 49160 | tf_op jit(solution)/shard_map/ppermute | solution.py:256
  37.7 6.0 %collective-permute-start.10 = (bf16[8,1024]{1,0:T(8,128)(2,1)S(1)}, bf16[8,1024]{1,0:T(8,128)(2,1)S(1)}, u32[]{:S(2)}, u32[]{:S(2)}) collective-permute-start(bf16[8,1024]{1,0:T(8,128)(2,1)S(1)} %get-tuple-element.26.refs_1_), channel_id=1, source_target_pairs={{0,4},{1,5},{2,6},{3,7},{4,0},{5,1},{6,2},{7,3},{8,12},{9,13},{10,... | collective-permute-start | bytes 49160 | tf_op jit(solution)/shard_map/ppermute | solution.py:256
  43.7 5.2 %collective-permute-start.15 = (bf16[8,4096]{1,0:T(8,128)(2,1)S(1)}, bf16[8,4096]{1,0:T(8,128)(2,1)S(1)}, u32[]{:S(2)}, u32[]{:S(2)}) collective-permute-start(bf16[8,4096]{1,0:T(8,128)(2,1)S(1)} %join.8.low_ref.refs_1_), channel_id=1, source_target_pairs={{0,3},{1,2},{2,1},{3,0},{4,7},{5,6},{6,5},{7,4},{8,11},{9,10},{10,... | collective-permute-start | bytes 196616 | tf_op jit(solution)/shard_map/ppermute | solution.py:256
  44.2 5.0 %collective-permute-start.14 = (bf16[8,4096]{1,0:T(8,128)(2,1)S(1)}, bf16[8,4096]{1,0:T(8,128)(2,1)S(1)}, u32[]{:S(2)}, u32[]{:S(2)}) collective-permute-start(bf16[8,4096]{1,0:T(8,128)(2,1)S(1)} %join.8.low_ref.refs_1_), channel_id=1, source_target_pairs={{0,2},{1,3},{2,0},{3,1},{4,6},{5,7},{6,4},{7,5},{8,10},{9,11},{10,... | collective-permute-start | bytes 196616 | tf_op jit(solution)/shard_map/ppermute | solution.py:256
  45.1 4.2 %collective-permute-start.13 = (bf16[8,4096]{1,0:T(8,128)(2,1)S(1)}, bf16[8,4096]{1,0:T(8,128)(2,1)S(1)}, u32[]{:S(2)}, u32[]{:S(2)}) collective-permute-start(bf16[8,4096]{1,0:T(8,128)(2,1)S(1)} %join.8.low_ref.refs_1_), channel_id=1, source_target_pairs={{0,1},{1,0},{2,3},{3,2},{4,5},{5,4},{6,7},{7,6},{8,9},{9,8},{10,11... | collective-permute-start | bytes 196616 | tf_op jit(solution)/shard_map/ppermute | solution.py:256
  49.2 18.3 %copy-start.5 = (f32[8,1024]{1,0:T(8,128)S(1)}, f32[8,1024]{1,0:T(8,128)}, u32[]{:S(2)}) copy-start(f32[8,1024]{1,0:T(8,128)} %refs_2_.1) | copy-start | bytes 98308
  (1 other events, 0.8 us)

commit v4 on v3

--- a/solution.py
+++ b/solution.py
@@ -139,52 +139,60 @@
         inv_ref[b * base : (b + 1) * base, :] = inverses[b]
 
 
-def merge_kernel(chol_ref, part_ref, *inv_refs):
+def merge_kernel(chol_ref, part_ref, *refs):
+    inv_refs, below_refs = refs[:3], refs[3:]
     size, step = chol_ref.shape[0], part_ref.shape[1]
+    half = inv_refs[0].shape[1]
     inverses = [part_ref[lo : lo + step, :] for lo in range(0, size, step)]
-    while len(inverses) > 1:
+    while step < half:
         merged = []
         for i in range(0, len(inverses), 2):
             lo, zero = i * step, jnp.zeros((step, step), F32)
             block, cut = chol_ref[lo + step : lo + 2 * step, lo : lo + step], step // 2
-            low = fine_dot(block, inverses[i]) if step < 256 else jnp.concatenate(
-                [fine_dot(block, inverses[i][:, :cut]), fine_dot(block[:, cut:], inverses[i][cut:, cut:])], axis=1
-            )
             other = inverses[i + 1]
-            low = -(fine_dot(other, low) if step < 256 else jnp.concatenate(
-                [fine_dot(other[:cut, :cut], low[:cut]), fine_dot(other[cut:], low)], axis=0
-            ))
-            if len(inverses) == 2:
-                for ref, c, nw, sw, se in zip(inv_refs, split3(zero), split3(inverses[0]), split3(low), split3(inverses[1])):
-                    ref[:step, :step] = nw
-                    ref[:step, step:] = c
-                    ref[step:, :step] = sw
-                    ref[step:, step:] = se
-                return
+            if step < 256:
+                low = -fine_dot(other, fine_dot(block, inverses[i]))
+            else:
+                low = jnp.concatenate(
+                    [fine_dot(block, inverses[i][:, :cut]), fine_dot(block[:, cut:], inverses[i][cut:, cut:])], axis=1
+                )
+                low = -jnp.concatenate([fine_dot(other[:cut, :cut], low[:cut]), fine_dot(other[cut:], low)], axis=0)
             top = jnp.concatenate([inverses[i], zero], axis=1)
-            merged.append(jnp.concatenate([top, jnp.concatenate([low, inverses[i + 1]], axis=1)], axis=0))
+            merged.append(jnp.concatenate([top, jnp.concatenate([low, other], axis=1)], axis=0))
         inverses = merged
         step *= 2
-
-
-def direction_kernel(ridge_ref, rz_ref, *refs):
-    proj_refs, refs = refs[:4], refs[4:]
-    inv_refs, cross_refs, refs = refs[:3], refs[3:5], refs[5:]
+    for i, inverse in enumerate(inverses):
+        for ref, piece in zip(inv_refs, split3(inverse)):
+            ref[i * half : (i + 1) * half, :] = piece
+    for ref, piece in zip(below_refs, split3(chol_ref[half:, :half])):
+        ref[...] = piece
+
+
+def add_pairs(parts):
+    while len(parts) > 1:
+        parts = [parts[i] + parts[i + 1] for i in range(0, len(parts), 2)]
+    return parts[0]
+
+
+def direction_kernel(parts, ridge_ref, rz_ref, *refs):
+    proj_refs, refs = refs[:parts], refs[parts:]
+    inv_refs, below_refs, cross_refs, refs = refs[:3], refs[3:6], refs[6:8], refs[8:]
     res_ref, dir_ref, new_ref, near_ref, low_ref, inner_ref = refs
     land = cross_refs[0].shape[1]
     half = land // 2
     ridge = ridge_ref[0]
     lane = lax.broadcasted_iota(jnp.int32, inner_ref.shape, 0)
     rz = sum(jnp.where(lane == i, rz_ref[i], 0.0) for i in range(inner_ref.shape[0]))
-    sums = (proj_refs[0][...] + proj_refs[1][...]) + (proj_refs[2][...] + proj_refs[3][...])
+    sums = add_pairs([ref[...] for ref in proj_refs])
     proj = sums[:, :land]
     squares = sums[:, land : land + 1]
-    north = [ref[:half, :half] for ref in inv_refs]
-    south = [ref[half:] for ref in inv_refs]
-    y0 = wide_dot(proj[:, :half], north, 1)
-    y1 = wide_dot(proj, south, 1)
-    x0 = wide_dot(jnp.concatenate([y0, y1], axis=1), [ref[:, :half] for ref in inv_refs], 0)
-    x1 = wide_dot(y1, [ref[half:, half:] for ref in inv_refs], 0)
+    below = [ref[...] for ref in below_refs]
+    upper = [ref[:half] for ref in inv_refs]
+    lower = [ref[half:] for ref in inv_refs]
+    y0 = wide_dot(proj[:, :half], upper, 1)
+    y1 = wide_dot(proj[:, half:] - wide_dot(y0, below, 1), lower, 1)
+    x1 = wide_dot(y1, lower, 0)
+    x0 = wide_dot(y0 - wide_dot(x1, below, 0), upper, 0)
     coeffs = jnp.concatenate([x0, x1], axis=1)
     inner = (squares - jnp.sum(proj * coeffs, axis=1, keepdims=True)) / ridge
     precond = (res_ref[...] - wide_dot(coeffs, [ref[...] for ref in cross_refs], 1)) / ridge
@@ -208,13 +216,13 @@
         tiles_ref[at : at + group * width, :] = tile(pts, lhs)
 
 
-def near_kernel(low_ref, tiles_ref, total_ref):
-    total_ref[...] = dot(low_ref[...], tiles_ref[: low_ref.shape[1], :], 1, 0)
-
-
-def image_kernel(
-    low_at, near, ridge_ref, own_ref, pts_ref, low_ref, near_ref, early_ref, late_ref, new_ref, image_ref, curv_ref, lhs_ref
-):
+def near_kernel(first, own_ref, pts_ref, low_ref, held_ref, total_ref, tiles_ref):
+    total_ref[...] = dot(low_ref[...], held_ref[: low_ref.shape[1], :], 1, 0)
+    tiles_kernel(first, own_ref, pts_ref, tiles_ref)
+
+
+def image_kernel(low_at, near, tile_count, ridge_ref, own_ref, pts_ref, low_ref, near_ref, *refs):
+    tile_refs, (new_ref, image_ref, curv_ref, lhs_ref) = refs[:tile_count], refs[tile_count:]
     width = own_ref.shape[1]
     lhs_ref[...] = cols_side(own_ref[...])
 
@@ -223,17 +231,16 @@
             [low_ref[:, low_at[b] * width : (low_at[b] + 1) * width].astype(F32) for b in blocks], axis=1
         ).astype(B16)
 
-    early = early_ref.shape[0] // width
-    held = early + late_ref.shape[0] // width
+    at, total = near, near_ref[...]
+    for ref in tile_refs:
+        end = at + ref.shape[0] // width
+        total = total + dot(low(range(at, end)), ref[...], 1, 0)
+        at = end
     blocks = len(low_at)
-    total = near_ref[...]
-    left = blocks - held
-    group = max(g for g in range(1, 3) if left % g == 0)
-    for b in range(held, blocks, group):
+    group = max(g for g in range(1, 3) if (blocks - at) % g == 0)
+    for b in range(at, blocks, group):
         pts = pts_ref[:, b * width : (b + group) * width]
         total = total + dot(low(range(b, b + group)), tile(pts, lhs_ref[...]), 1, 0)
-    total = total + dot(low(range(near, early)), early_ref[near * width :, :], 1, 0)
-    total = total + dot(low(range(early, held)), late_ref[...], 1, 0)
     new = new_ref[...]
     image = total + ridge_ref[0] * new
     image_ref[...] = image
@@ -269,10 +276,7 @@
 
 
 def add_kernel(*refs):
-    parts = [ref[...] for ref in refs[:-1]]
-    while len(parts) > 1:
-        parts = [parts[i] + parts[i + 1] for i in range(0, len(parts), 2)]
-    refs[-1][...] = parts[0]
+    refs[-1][...] = add_pairs([ref[...] for ref in refs[:-1]])
 
 
 def join_kernel(*refs):
@@ -349,40 +353,48 @@
     partial = add_up([partial, exchange(partial, last, count)], (inverse,))
     near_points, near_order = gather(points, [0], [top], count, [(partial,)])
     merged = call(
-        merge_kernel, (shape((land, land), B16),) * 3, chol, inverse,
+        merge_kernel, (shape((land, land // 2), B16),) * 3 + (shape((land // 2, land // 2), B16),) * 3, chol, inverse,
         name="merge", work=2 * width * land * depth, room=24, after=(partial,),
     )
-    proj = all_sum(partial, levels[1:], count)
+    bits = [m for masks in levels[1:] for m in masks[:2]]
+    for i, bit in enumerate(bits):
+        proj = [partial, exchange(partial, bit, count)]
+        if i < len(bits) - 1:
+            partial = add_up(proj, (merged[0],))
+
+    def tiles(first, blocks, pts, *after):
+        return call(
+            functools.partial(tiles_kernel, first), shape((blocks * width, width), B16), points, pts,
+            name="tiles", room=14, work=blocks // 2 * width * width * depth, after=after,
+        )
+
+    near = len(near_order)
+    held = [tiles(0, near, near_points, partial, merged[0])]
     new, new_kept, low, inner = call(
-        direction_kernel,
+        functools.partial(direction_kernel, len(proj)),
         (shape((outs, width), F32),) * 2 + (shape((outs, width), B16), shape((outs, 1), F32)),
         ridge, rz_prev, *proj, *merged, *cross, residual, direction,
-        smem=(0, 1), name="direction", room=24, work=6 * width * land * depth,
+        smem=(0, 1), name="direction", room=24, after=held[:1], work=6 * width * land * depth,
     )
     early_points, early_order = gather(near_points, near_order, far_stages[:1], count, [(inner,)])
-    early = len(early_order)
-    early_tiles = call(
-        functools.partial(tiles_kernel, 0), shape((early * width, width), B16), points, early_points,
-        name="tiles", room=14, work=early * width * width * depth, after=(inner,),
-    )
-    near_low, low_order = gather(low, [0], [top], count, [(early_tiles,)])
-    near = len(low_order)
-    near_sum = call(
-        near_kernel, shape((outs, width), F32), near_low, early_tiles, name="near", room=2,
-        work=near * width * width * depth // 2,
-    )
     all_points, point_order = gather(early_points, early_order, far_stages[1:], count)
-    late = 3
-    late_tiles = call(
-        functools.partial(tiles_kernel, early), shape((late * width, width), B16), points, all_points,
-        name="tiles", room=14, work=late * width * width * depth, after=(near_sum,),
-    )
-    all_low, low_order = gather(near_low, low_order, lower[::-1], count, [(late_tiles,)])
+    held.append(tiles(near, len(early_order) - near, early_points, inner))
+    first_low, low_order = gather(low, [0], [[m] for m in top[:1]], count, [held[-1:]])
+    held.append(tiles(len(early_order), near, all_points, first_low))
+    near_low, low_order = gather(first_low, low_order, [[m] for m in top[1:2]], count, [held[-1:]])
+    late = near - 1
+    near_sum, late_tiles = call(
+        functools.partial(near_kernel, len(early_order) + near),
+        (shape((outs, width), F32), shape((late * width, width), B16)),
+        points, all_points, near_low, held[0], name="near", room=14, work=(late + 1) * width * width * depth,
+    )
+    held.append(late_tiles)
+    all_low, low_order = gather(near_low, low_order, lower[::-1], count, [held[-1:]])
     image, curv = call(
-        functools.partial(image_kernel, [low_order.index(m) for m in point_order], near),
+        functools.partial(image_kernel, [low_order.index(m) for m in point_order], near, len(held) - 1),
         (shape((outs, width), F32), shape((count, 1, 128), F32)),
-        ridge, points, all_points, all_low, near_sum, early_tiles, late_tiles, new_kept, smem=(0,),
-        scratch=(side,), name="image", room=14, work=2 * (count - early - late) * width * width * depth,
+        ridge, points, all_points, all_low, near_sum, *held[1:], new_kept, smem=(0,),
+        scratch=(side,), name="image", room=14, work=(count - near) * width * width * depth,
     )
     sol_new, res_new, inner_row = call(
         update_kernel,

time: 68.6 us -> 64.5 us (0.940)
  Pallas kernels: 31.5 us -> 29.1 us
  blocking collectives: 11.8 us -> 10.4 us
  starting transfers between devices: 19.3 us -> 18 us
  waiting for transfers between devices: 1.54 us -> 2.67 us
    pallas_call x16 -> x19, Pallas kernels: 31.5 us -> 29.1 us  [call(): pl.pallas_call(body, out_shape=out, in_specs=[ANY if i < len(after) else...]
    all_to_all x1, blocking collectives: 11.8 us -> 10.4 us  [local(): lax.all_to_all(curv, 'rows', 0, 0, tiled=True)]
    ppermute x16 -> x14, starting transfers between devices: 19.3 us -> 18 us  [exchange(): return lax.ppermute(x, 'rows', [(i, i ^ mask) for i in range(count)])]
    ppermute x16 -> x14, waiting for transfers between devices: 1.54 us -> 2.67 us  [exchange(): return lax.ppermute(x, 'rows', [(i, i ^ mask) for i in range(count)])]
  transfers between devices with their start and end apart: 16 -> 14, of which waited for: 2 -> 3; matrix products, arithmetic and copies ran while one was open for 0% -> 0% of each run, Pallas kernels for 35% -> 37%
where the time goes in v4:
time: 64.5 us; the launch traced here: 64.3 us
  Pallas kernels  29.1 us (45%)
  starting transfers between devices  18 us (28%)
  blocking collectives  10.4 us (16%)
  waiting for transfers between devices  2.67 us (4%)
  local copies, waits for them, and re-layouts  2.63 us (4%)
  between operations  1.54 us (2%)
    pallas_call x19, Pallas kernels, call(): pl.pallas_call(body, out_shape=out, in_specs=[ANY if i < len(after) else...  29.1 us
    ppermute x14, starting transfers between devices, exchange(): return lax.ppermute(x, 'rows', [(i, i ^ mask) for i in range(count)])  18 us
    all_to_all x1, blocking collectives, local(): lax.all_to_all(curv, 'rows', 0, 0, tiled=True)  10.4 us
    ppermute x14, waiting for transfers between devices, exchange(): return lax.ppermute(x, 'rows', [(i, i ^ mask) for i in range(count)])  2.67 us
    unnamed x18, local copies, waits for them, and re-layouts  2.63 us
  transfers between devices with their start and end apart: 14, of which 3 were waited for; matrix products, arithmetic and copies ran while one was open for 0% of the time, Pallas kernels for 37%

profile of v4, /device:TPU:0, one launch (start us, length us, event | category | flops | bytes accessed | tf_op | source)
XLA Modules:
  0.0 64.3 jit_solution(14975035571748676569)
XLA Ops:
  0.6 5.1 %collective-permute-start.5 = (bf16[64,1024]{1,0:T(8,128)(2,1)}, bf16[64,1024]{1,0:T(8,128)(2,1)S(1)}, u32[]{:S(2)}, u32[]{:S(2)}) collective-permute-start(bf16[64,1024]{1,0:T(8,128)(2,1)} %own_ref.3), channel_id=1, source_target_pairs={{0,12},{1,13},{2,14},{3,15},{4,8},{5,9},{6,10},{7,11},{8,4},{9,5},... | collective-permute-start | bytes 393224 | tf_op jit(solution)/shard_map/ppermute | solution.py:263
  6.4 0.9 %copy-done.1 = bf16[64,1024]{1,0:T(8,128)(2,1)S(1)} copy-done((bf16[64,1024]{1,0:T(8,128)(2,1)S(1)}, bf16[64,1024]{1,0:T(8,128)(2,1)}, u32[]{:S(2)}) %copy-start.1) | copy-done | bytes 131096
  7.3 0.8 %copy-done.3 = f32[8,1024]{1,0:T(8,128)S(1)} copy-done((f32[8,1024]{1,0:T(8,128)S(1)}, f32[8,1024]{1,0:T(8,128)}, u32[]{:S(2)}) %copy-start.3) | copy-done | bytes 32792
  8.1 0.9 %copy-done.8 = bf16[64,1024]{1,0:T(8,128)(2,1)S(1)} copy-done((bf16[64,1024]{1,0:T(8,128)(2,1)S(1)}, bf16[64,1024]{1,0:T(8,128)(2,1)}, u32[]{:S(2)}) %copy-start.8) | copy-done | bytes 131096
  9.0 1.6 %cross.1 = (bf16[1024,1024]{1,0:T(8,128)(2,1)S(1)}, bf16[1024,1024]{1,0:T(8,128)(2,1)S(1)}, f32[8,1152]{1,0:T(8,128)S(1)}) custom-call(bf16[64,1024]{1,0:T(8,128)(2,1)S(1)} %copy-done.1, bf16[64,1024]{1,0:T(8,128)(2,1)S(1)} %copy-done.8, f32[8,1024]{1,0:T(8,128)S(1)} %copy-done.3), custom_call_target="tpu_custom_call" | custom-call | flops 2684354560 | tf_op jit(solution)/shard_map/cross/pallas_call | solution.py:317
  10.7 1.2 %collective-permute-done.refs_1_ = f32[8,1152]{1,0:T(8,128)S(1)} collective-permute-done((f32[8,1152]{1,0:T(8,128)S(1)}, f32[8,1152]{1,0:T(8,128)S(1)}, u32[]{:S(2)}, u32[]{:S(2)}) %collective-permute-start) | collective-permute-done | bytes 36896 | tf_op jit(solution)/shard_map/ppermute | solution.py:263
  11.9 1.7 %collective-permute-start.1 = (f32[8,1152]{1,0:T(8,128)S(1)}, f32[8,1152]{1,0:T(8,128)S(1)}, u32[]{:S(2)}, u32[]{:S(2)}) collective-permute-start(f32[8,1152]{1,0:T(8,128)S(1)} %add.3.refs_0_.refs_1_), channel_id=1, source_target_pairs={{0,2},{1,3},{2,0},{3,1},{4,6},{5,7},{6,4},{7,5},{8,10},{9,11},{10,... | collective-permute-start | bytes 110600 | tf_op jit(solution)/shard_map/ppermute | solution.py:263
  13.6 4.0 %inverse.1.refs_0_.refs_2_ = f32[1024,128]{1,0:T(8,128)S(1)} custom-call(f32[8,1152]{1,0:T(8,128)S(1)} %add.3.refs_0_.refs_1_, f32[1024,1024]{1,0:T(8,128)S(1)} %copy-done), custom_call_target="tpu_custom_call" | custom-call | flops 536870912 | tf_op jit(solution)/shard_map/inverse/pallas_call | solution.py:317
  17.7 0.9 %collective-permute-start.7 = (bf16[64,4096]{1,0:T(8,128)(2,1)S(1)}, bf16[64,4096]{1,0:T(8,128)(2,1)S(1)}, u32[]{:S(2)}, u32[]{:S(2)}) collective-permute-start(bf16[64,4096]{1,0:T(8,128)(2,1)S(1)} %join.6.refs_3_.refs_1_), channel_id=1, source_target_pairs={{0,2},{1,3},{2,0},{3,1},{4,6},{5,7},{6,4},{7,5},{8,10},{9,11},{10,... | collective-permute-start | bytes 1572872 | tf_op jit(solution)/shard_map/ppermute | solution.py:263
  19.3 0.9 %collective-permute-start.2 = (f32[8,1152]{1,0:T(8,128)S(1)}, f32[8,1152]{1,0:T(8,128)S(1)}, u32[]{:S(2)}, u32[]{:S(2)}) collective-permute-start(f32[8,1152]{1,0:T(8,128)S(1)} %add.4.refs_0_.refs_1_), channel_id=1, source_target_pairs={{0,4},{1,5},{2,6},{3,7},{4,0},{5,1},{6,2},{7,3},{8,12},{9,13},{10,... | collective-permute-start | bytes 110600 | tf_op jit(solution)/shard_map/ppermute | solution.py:263
  20.3 2.6 %merge.1 = (bf16[1024,512]{1,0:T(8,128)(2,1)S(1)}, bf16[1024,512]{1,0:T(8,128)(2,1)S(1)}, bf16[1024,512]{1,0:T(8,128)(2,1)S(1)}, bf16[512,512]{1,0:T(8,128)(2,1)...) custom-call(f32[8,1152]{1,0:T(8,128)S(1)} %add.4.refs_0_.refs_1_, f32[1024,1024]{1,0:T(8,128)S(1)} %copy-done, ...), custom_call_target="tpu_custom_call" | custom-call | flops 1073741824 | tf_op jit(solution)/shard_map/merge/pallas_call | solution.py:317
  23.4 2.5 %collective-permute-start.6 = (f32[8,1152]{1,0:T(8,128)S(1)}, f32[8,1152]{1,0:T(8,128)S(1)}, u32[]{:S(2)}, u32[]{:S(2)}) collective-permute-start(f32[8,1152]{1,0:T(8,128)S(1)} %add.5.refs_0_.refs_3_), channel_id=1, source_target_pairs={{0,8},{1,9},{2,10},{3,11},{4,12},{5,13},{6,14},{7,15},{8,0},{9,1},... | collective-permute-start | bytes 110600 | tf_op jit(solution)/shard_map/ppermute | solution.py:263
  25.9 2.5 %tiles.3.refs_0_.held_ref = bf16[4096,1024]{1,0:T(8,128)(2,1)S(1)} custom-call(f32[8,1152]{1,0:T(8,128)S(1)} %add.5.refs_0_.refs_3_, bf16[1024,512]{1,0:T(8,128)(2,1)S(1)} %get-tuple-element.25.refs_0_.refs_1_.refs_5_, bf16[64,1024]{1,0:T(8,128)(2,1)S(1)} %copy-done.1, bf16[64,4096]{1,0:T(8,128)(2,1)S(1)} %join.6.refs_3_.refs_1_), custom_call_target="tpu_custom_call" | custom-call | flops 1073741824 | tf_op jit(solution)/shard_map/tiles/pallas_call | solution.py:317
  28.5 5.2 %direction.1 = (f32[8,1024]{1,0:T(8,128)}, f32[8,1024]{1,0:T(8,128)S(1)}, bf16[8,1024]{1,0:T(8,128)(2,1)S(1)}, f32[8,1]{1,0:T(8,128)S(1)}) custom-call(bf16[4096,1024]{1,0:T(8,128)(2,1)S(1)} %tiles.3.refs_0_.held_ref, f32[1]{0:T(128)S(6)} %copy.12.refs_1_.ridge_ref, f32[8]{0:T(128)S(1)} %copy-done.7, f32[8,1152]{1,0:T(8,128)S(1)} %add.5.refs_0_.refs_3_, ...), custom_call_target="tpu_custom_call" | custom-call | flops 3221225472 | tf_op jit(solution)/shard_map/direction/pallas_call | solution.py:317
  33.8 1.3 %collective-permute-start.9 = (bf16[8,1024]{1,0:T(8,128)(2,1)S(1)}, bf16[8,1024]{1,0:T(8,128)(2,1)S(1)}, u32[]{:S(2)}, u32[]{:S(2)}) collective-permute-start(bf16[8,1024]{1,0:T(8,128)(2,1)S(1)} %get-tuple-element.34.refs_1_), channel_id=1, source_target_pairs={{0,4},{1,5},{2,6},{3,7},{4,0},{5,1},{6,2},{7,3},{8,12},{9,13},{10,... | collective-permute-start | bytes 49160 | tf_op jit(solution)/shard_map/ppermute | solution.py:263
  35.1 2.5 %tiles.4.refs_0_ = bf16[4096,1024]{1,0:T(8,128)(2,1)S(1)} custom-call(f32[8,1]{1,0:T(8,128)S(1)} %get-tuple-element.33.refs_0_.refs_1_, bf16[64,1024]{1,0:T(8,128)(2,1)S(1)} %copy-done.2, bf16[64,8192]{1,0:T(8,128)(2,1)S(1)} %join.7.refs_0_.refs_2_), custom_call_target="tpu_custom_call" | custom-call | flops 1073741824 | tf_op jit(solution)/shard_map/tiles/pallas_call | solution.py:317
  37.7 2.7 %collective-permute-start.10 = (bf16[8,2048]{1,0:T(8,128)(2,1)S(1)}, bf16[8,2048]{1,0:T(8,128)(2,1)S(1)}, u32[]{:S(2)}, u32[]{:S(2)}) collective-permute-start(bf16[8,2048]{1,0:T(8,128)(2,1)S(1)} %join.9.refs_0_.refs_1_), channel_id=1, source_target_pairs={{0,8},{1,9},{2,10},{3,11},{4,12},{5,13},{6,14},{7,15},{8,0},{9,1},... | collective-permute-start | bytes 98312 | tf_op jit(solution)/shard_map/ppermute | solution.py:263
  40.6 2.5 %tiles.5.refs_0_.refs_1_ = bf16[4096,1024]{1,0:T(8,128)(2,1)S(1)} custom-call(bf16[8,2048]{1,0:T(8,128)(2,1)S(1)} %join.9.refs_0_.refs_1_, bf16[64,1024]{1,0:T(8,128)(2,1)S(1)} %copy-done.2, bf16[64,16384]{1,0:T(8,128)(2,1)S(1)} %join.8.refs_2_.pts_ref), custom_call_target="tpu_custom_call" | custom-call | flops 1073741824 | tf_op jit(solution)/shard_map/tiles/pallas_call | solution.py:317
  43.1 1.1 %collective-permute-start.13 = (bf16[8,4096]{1,0:T(8,128)(2,1)S(1)}, bf16[8,4096]{1,0:T(8,128)(2,1)S(1)}, u32[]{:S(2)}, u32[]{:S(2)}) collective-permute-start(bf16[8,4096]{1,0:T(8,128)(2,1)S(1)} %join.10.low_ref.refs_1_), channel_id=1, source_target_pairs={{0,3},{1,2},{2,1},{3,0},{4,7},{5,6},{6,5},{7,4},{8,11},{9,10},{10,... | collective-permute-start | bytes 196616 | tf_op jit(solution)/shard_map/ppermute | solution.py:263
  45.1 2.9 %near.1 = (f32[8,1024]{1,0:T(8,128)S(1)}, bf16[3072,1024]{1,0:T(8,128)(2,1)S(1)}) custom-call(bf16[64,1024]{1,0:T(8,128)(2,1)S(1)} %copy-done.2, bf16[64,16384]{1,0:T(8,128)(2,1)S(1)} %join.8.refs_2_.pts_ref, bf16[8,4096]{1,0:T(8,128)(2,1)S(1)} %join.10.low_ref.refs_1_, bf16[4096,1024]{1,0:T(8,128)(2,1)S(1)} %tiles.3.refs_0_.held_ref), custom_call_target="tpu_custom_call" | custom-call | flops 2147483648 | tf_op jit(solution)/shard_map/near/pallas_call | solution.py:317
  48.0 1.0 %collective-permute-done.12.refs_3_ = bf16[8,4096]{1,0:T(8,128)(2,1)S(1)} collective-permute-done((bf16[8,4096]{1,0:T(8,128)(2,1)S(1)}, bf16[8,4096]{1,0:T(8,128)(2,1)S(1)}, u32[]{:S(2)}, u32[]{:S(2)}) %collective-permute-start.12) | collective-permute-done | bytes 65568 | tf_op jit(solution)/shard_map/ppermute | solution.py:263
  49.0 4.0 %image.1 = (f32[8,1024]{1,0:T(8,128)S(1)}, f32[16,1,128]{2,1,0:T(1,128)S(1)}) custom-call(f32[1]{0:T(128)S(6)} %copy.12.refs_1_.ridge_ref, bf16[64,1024]{1,0:T(8,128)(2,1)S(1)} %copy-done.2, bf16[64,16384]{1,0:T(8,128)(2,1)S(1)} %join.8.refs_2_.pts_ref, bf16[8,16384]{1,0:T(8,128)(2,1)S(1)} %join.11.low_ref, f32[8,1024]{1,0:T(8,128)S(1)} %get-tuple-element.36.near_ref, ...), custom_call_target="tpu_custom_call" | custom-call | flops 6442450944 | tf_op jit(solution)/shard_map/image/pallas_call | solution.py:317
  53.1 10.4 %all_to_all.5.refs_0_ = f32[16,1,128]{2,1,0:T(1,128)S(1)} all-to-all(f32[16,1,128]{2,1,0:T(1,128)S(1)} %get-tuple-element.38), channel_id=1, replica_groups=mesh['groups'=2,'rows'=16] {'rows'}, dimensions={0} | all-to-all | bytes 16384 | tf_op jit(solution)/shard_map/all_to_all | solution.py:402
  63.5 0.8 %update.1 = (f32[8,1024]{1,0:T(8,128)}, f32[8,1024]{1,0:T(8,128)}, f32[1,8]{1,0:T(1,128)}) custom-call(f32[16,1,128]{2,1,0:T(1,128)S(1)} %all_to_all.5.refs_0_, f32[8,1]{1,0:T(8,128)S(1)} %get-tuple-element.33.refs_0_.refs_1_, f32[8,1024]{1,0:T(8,128)S(1)} %copy-done.6, f32[8,1024]{1,0:T(8,128)S(1)} %copy-done.4, ...), custom_call_target="tpu_custom_call" | custom-call | tf_op jit(solution)/shard_map/update/pallas_call | solution.py:317
  (42 shorter events, 2.5 us)
Async XLA Ops:
  0.6 13.0 %copy-start = (f32[1024,1024]{1,0:T(8,128)S(1)}, f32[1024,1024]{1,0:T(8,128)}, u32[]{:S(2)}) copy-start(f32[1024,1024]{1,0:T(8,128)} %refs_1_.7) | copy-start | bytes 12582916
  0.6 17.0 %collective-permute-start.5 = (bf16[64,1024]{1,0:T(8,128)(2,1)}, bf16[64,1024]{1,0:T(8,128)(2,1)S(1)}, u32[]{:S(2)}, u32[]{:S(2)}) collective-permute-start(bf16[64,1024]{1,0:T(8,128)(2,1)} %own_ref.3), channel_id=1, source_target_pairs={{0,12},{1,13},{2,14},{3,15},{4,8},{5,9},{6,10},{7,11},{8,4},{9,5},... | collective-permute-start | bytes 393224 | tf_op jit(solution)/shard_map/ppermute | solution.py:263
  5.8 11.9 %collective-permute-start.4 = (bf16[64,1024]{1,0:T(8,128)(2,1)}, bf16[64,1024]{1,0:T(8,128)(2,1)S(1)}, u32[]{:S(2)}, u32[]{:S(2)}) collective-permute-start(bf16[64,1024]{1,0:T(8,128)(2,1)} %own_ref.3), channel_id=1, source_target_pairs={{0,8},{1,9},{2,10},{3,11},{4,12},{5,13},{6,14},{7,15},{8,0},{9,1},... | collective-permute-start | bytes 393224 | tf_op jit(solution)/shard_map/ppermute | solution.py:263
  5.8 11.9 %collective-permute-start.3 = (bf16[64,1024]{1,0:T(8,128)(2,1)}, bf16[64,1024]{1,0:T(8,128)(2,1)S(1)}, u32[]{:S(2)}, u32[]{:S(2)}) collective-permute-start(bf16[64,1024]{1,0:T(8,128)(2,1)} %own_ref.3), channel_id=1, source_target_pairs={{0,4},{1,5},{2,6},{3,7},{4,0},{5,1},{6,2},{7,3},{8,12},{9,13},{10,... | collective-permute-start | bytes 393224 | tf_op jit(solution)/shard_map/ppermute | solution.py:263
  6.4 0.9 %copy-start.1 = (bf16[64,1024]{1,0:T(8,128)(2,1)S(1)}, bf16[64,1024]{1,0:T(8,128)(2,1)}, u32[]{:S(2)}) copy-start(bf16[64,1024]{1,0:T(8,128)(2,1)} %own_ref.3) | copy-start | bytes 393220
  7.3 0.8 %copy-start.3 = (f32[8,1024]{1,0:T(8,128)S(1)}, f32[8,1024]{1,0:T(8,128)}, u32[]{:S(2)}) copy-start(f32[8,1024]{1,0:T(8,128)} %refs_3_.1) | copy-start | bytes 98308
  8.1 0.9 %copy-start.8 = (bf16[64,1024]{1,0:T(8,128)(2,1)S(1)}, bf16[64,1024]{1,0:T(8,128)(2,1)}, u32[]{:S(2)}) copy-start(bf16[64,1024]{1,0:T(8,128)(2,1)} %marks_ref.1) | copy-start | bytes 393220
  10.6 1.3 %collective-permute-start = (f32[8,1152]{1,0:T(8,128)S(1)}, f32[8,1152]{1,0:T(8,128)S(1)}, u32[]{:S(2)}, u32[]{:S(2)}) collective-permute-start(f32[8,1152]{1,0:T(8,128)S(1)} %get-tuple-element.24.refs_0_), channel_id=1, source_target_pairs={{0,1},{1,0},{2,3},{3,2},{4,5},{5,4},{6,7},{7,6},{8,9},{9,8},{10,11... | collective-permute-start | bytes 110600 | tf_op jit(solution)/shard_map/ppermute | solution.py:263
  11.9 5.7 %collective-permute-start.1 = (f32[8,1152]{1,0:T(8,128)S(1)}, f32[8,1152]{1,0:T(8,128)S(1)}, u32[]{:S(2)}, u32[]{:S(2)}) collective-permute-start(f32[8,1152]{1,0:T(8,128)S(1)} %add.3.refs_0_.refs_1_), channel_id=1, source_target_pairs={{0,2},{1,3},{2,0},{3,1},{4,6},{5,7},{6,4},{7,5},{8,10},{9,11},{10,... | collective-permute-start | bytes 110600 | tf_op jit(solution)/shard_map/ppermute | solution.py:263
  17.7 15.9 %collective-permute-start.7 = (bf16[64,4096]{1,0:T(8,128)(2,1)S(1)}, bf16[64,4096]{1,0:T(8,128)(2,1)S(1)}, u32[]{:S(2)}, u32[]{:S(2)}) collective-permute-start(bf16[64,4096]{1,0:T(8,128)(2,1)S(1)} %join.6.refs_3_.refs_1_), channel_id=1, source_target_pairs={{0,2},{1,3},{2,0},{3,1},{4,6},{5,7},{6,4},{7,5},{8,10},{9,11},{10,... | collective-permute-start | bytes 1572872 | tf_op jit(solution)/shard_map/ppermute | solution.py:263
  19.3 4.0 %collective-permute-start.2 = (f32[8,1152]{1,0:T(8,128)S(1)}, f32[8,1152]{1,0:T(8,128)S(1)}, u32[]{:S(2)}, u32[]{:S(2)}) collective-permute-start(f32[8,1152]{1,0:T(8,128)S(1)} %add.4.refs_0_.refs_1_), channel_id=1, source_target_pairs={{0,4},{1,5},{2,6},{3,7},{4,0},{5,1},{6,2},{7,3},{8,12},{9,13},{10,... | collective-permute-start | bytes 110600 | tf_op jit(solution)/shard_map/ppermute | solution.py:263
  22.9 5.6 %copy-start.5 = (f32[8,1024]{1,0:T(8,128)S(1)}, f32[8,1024]{1,0:T(8,128)}, u32[]{:S(2)}) copy-start(f32[8,1024]{1,0:T(8,128)} %refs_14_.1) | copy-start | bytes 98308
  22.9 5.6 %copy-start.7 = (f32[8]{0:T(128)S(1)}, f32[8]{0:T(128)}, u32[]{:S(2)}) copy-start(f32[8]{0:T(128)} %refs_2_.4) | copy-start | bytes 100
  23.4 5.1 %collective-permute-start.6 = (f32[8,1152]{1,0:T(8,128)S(1)}, f32[8,1152]{1,0:T(8,128)S(1)}, u32[]{:S(2)}, u32[]{:S(2)}) collective-permute-start(f32[8,1152]{1,0:T(8,128)S(1)} %add.5.refs_0_.refs_3_), channel_id=1, source_target_pairs={{0,8},{1,9},{2,10},{3,11},{4,12},{5,13},{6,14},{7,15},{8,0},{9,1},... | collective-permute-start | bytes 110600 | tf_op jit(solution)/shard_map/ppermute | solution.py:263
  28.5 6.7 %copy-start.2 = (bf16[64,1024]{1,0:T(8,128)(2,1)S(1)}, bf16[64,1024]{1,0:T(8,128)(2,1)}, u32[]{:S(2)}) copy-start(bf16[64,1024]{1,0:T(8,128)(2,1)} %own_ref.3) | copy-start | bytes 393220
  33.7 6.7 %collective-permute-start.8 = (bf16[64,8192]{1,0:T(8,128)(2,1)S(1)}, bf16[64,8192]{1,0:T(8,128)(2,1)S(1)}, u32[]{:S(2)}, u32[]{:S(2)}) collective-permute-start(bf16[64,8192]{1,0:T(8,128)(2,1)S(1)} %join.7.refs_0_.refs_2_), channel_id=1, source_target_pairs={{0,1},{1,0},{2,3},{3,2},{4,5},{5,4},{6,7},{7,6},{8,9},{9,8},{10,11... | collective-permute-start | bytes 3145736 | tf_op jit(solution)/shard_map/ppermute | solution.py:263
  33.8 3.8 %collective-permute-start.9 = (bf16[8,1024]{1,0:T(8,128)(2,1)S(1)}, bf16[8,1024]{1,0:T(8,128)(2,1)S(1)}, u32[]{:S(2)}, u32[]{:S(2)}) collective-permute-start(bf16[8,1024]{1,0:T(8,128)(2,1)S(1)} %get-tuple-element.34.refs_1_), channel_id=1, source_target_pairs={{0,4},{1,5},{2,6},{3,7},{4,0},{5,1},{6,2},{7,3},{8,12},{9,13},{10,... | collective-permute-start | bytes 49160 | tf_op jit(solution)/shard_map/ppermute | solution.py:263
  37.7 5.4 %collective-permute-start.10 = (bf16[8,2048]{1,0:T(8,128)(2,1)S(1)}, bf16[8,2048]{1,0:T(8,128)(2,1)S(1)}, u32[]{:S(2)}, u32[]{:S(2)}) collective-permute-start(bf16[8,2048]{1,0:T(8,128)(2,1)S(1)} %join.9.refs_0_.refs_1_), channel_id=1, source_target_pairs={{0,8},{1,9},{2,10},{3,11},{4,12},{5,13},{6,14},{7,15},{8,0},{9,1},... | collective-permute-start | bytes 98312 | tf_op jit(solution)/shard_map/ppermute | solution.py:263
  43.1 4.9 %collective-permute-start.13 = (bf16[8,4096]{1,0:T(8,128)(2,1)S(1)}, bf16[8,4096]{1,0:T(8,128)(2,1)S(1)}, u32[]{:S(2)}, u32[]{:S(2)}) collective-permute-start(bf16[8,4096]{1,0:T(8,128)(2,1)S(1)} %join.10.low_ref.refs_1_), channel_id=1, source_target_pairs={{0,3},{1,2},{2,1},{3,0},{4,7},{5,6},{6,5},{7,4},{8,11},{9,10},{10,... | collective-permute-start | bytes 196616 | tf_op jit(solution)/shard_map/ppermute | solution.py:263
  44.2 4.8 %collective-permute-start.12 = (bf16[8,4096]{1,0:T(8,128)(2,1)S(1)}, bf16[8,4096]{1,0:T(8,128)(2,1)S(1)}, u32[]{:S(2)}, u32[]{:S(2)}) collective-permute-start(bf16[8,4096]{1,0:T(8,128)(2,1)S(1)} %join.10.low_ref.refs_1_), channel_id=1, source_target_pairs={{0,2},{1,3},{2,0},{3,1},{4,6},{5,7},{6,4},{7,5},{8,10},{9,11},{10,... | collective-permute-start | bytes 196616 | tf_op jit(solution)/shard_map/ppermute | solution.py:263
  44.8 4.2 %collective-permute-start.11 = (bf16[8,4096]{1,0:T(8,128)(2,1)S(1)}, bf16[8,4096]{1,0:T(8,128)(2,1)S(1)}, u32[]{:S(2)}, u32[]{:S(2)}) collective-permute-start(bf16[8,4096]{1,0:T(8,128)(2,1)S(1)} %join.10.low_ref.refs_1_), channel_id=1, source_target_pairs={{0,1},{1,0},{2,3},{3,2},{4,5},{5,4},{6,7},{7,6},{8,9},{9,8},{10,11... | collective-permute-start | bytes 196616 | tf_op jit(solution)/shard_map/ppermute | solution.py:263
  49.0 14.4 %copy-start.4 = (f32[8,1024]{1,0:T(8,128)S(1)}, f32[8,1024]{1,0:T(8,128)}, u32[]{:S(2)}) copy-start(f32[8,1024]{1,0:T(8,128)} %refs_3_.1) | copy-start | bytes 98308
  49.0 14.4 %copy-start.6 = (f32[8,1024]{1,0:T(8,128)S(1)}, f32[8,1024]{1,0:T(8,128)}, u32[]{:S(2)}) copy-start(f32[8,1024]{1,0:T(8,128)} %refs_2_.5) | copy-start | bytes 98308

commit v5 on v4

--- a/solution.py
+++ b/solution.py
@@ -180,9 +180,9 @@
     res_ref, dir_ref, new_ref, near_ref, low_ref, inner_ref = refs
     land = cross_refs[0].shape[1]
     half = land // 2
-    ridge = ridge_ref[0]
-    lane = lax.broadcasted_iota(jnp.int32, inner_ref.shape, 0)
-    rz = sum(jnp.where(lane == i, rz_ref[i], 0.0) for i in range(inner_ref.shape[0]))
+    ridge = ridge_ref[...].reshape(1, 1)
+    outs = inner_ref.shape[0]
+    rz = to_rows(rz_ref[...].reshape(1, outs), outs)
     sums = add_pairs([ref[...] for ref in proj_refs])
     proj = sums[:, :land]
     squares = sums[:, land : land + 1]
@@ -242,7 +242,7 @@
         pts = pts_ref[:, b * width : (b + group) * width]
         total = total + dot(low(range(b, b + group)), tile(pts, lhs_ref[...]), 1, 0)
     new = new_ref[...]
-    image = total + ridge_ref[0] * new
+    image = total + ridge_ref[...].reshape(1, 1) * new
     image_ref[...] = image
     curv = jnp.sum(new * image, axis=1, keepdims=True)
     curv_ref[...] = jnp.broadcast_to(to_lanes(curv)[None], curv_ref.shape)
@@ -374,7 +374,7 @@
         functools.partial(direction_kernel, len(proj)),
         (shape((outs, width), F32),) * 2 + (shape((outs, width), B16), shape((outs, 1), F32)),
         ridge, rz_prev, *proj, *merged, *cross, residual, direction,
-        smem=(0, 1), name="direction", room=24, after=held[:1], work=6 * width * land * depth,
+        name="direction", room=24, after=held[:1], work=6 * width * land * depth,
     )
     early_points, early_order = gather(near_points, near_order, far_stages[:1], count, [(inner,)])
     all_points, point_order = gather(early_points, early_order, far_stages[1:], count)
@@ -393,7 +393,7 @@
     image, curv = call(
         functools.partial(image_kernel, [low_order.index(m) for m in point_order], near, len(held) - 1),
         (shape((outs, width), F32), shape((count, 1, 128), F32)),
-        ridge, points, all_points, all_low, near_sum, *held[1:], new_kept, smem=(0,),
+        ridge, points, all_points, all_low, near_sum, *held[1:], new_kept,
         scratch=(side,), name="image", room=14, work=(count - near) * width * width * depth,
     )
     sol_new, res_new, inner_row = call(

time: 64.5 us -> 64 us (level)
  no operation moved by 1% of the time
where the time goes in v5:
time: 64 us; the launch traced here: 63.7 us
  Pallas kernels  28.5 us (45%)
  starting transfers between devices  18 us (28%)
  blocking collectives  10.4 us (16%)
  waiting for transfers between devices  2.67 us (4%)
  local copies, waits for them, and re-layouts  2.63 us (4%)
  between operations  1.54 us (2%)
    pallas_call x19, Pallas kernels, call(): pl.pallas_call(body, out_shape=out, in_specs=[ANY if i < len(after) else...  28.5 us
    ppermute x14, starting transfers between devices, exchange(): return lax.ppermute(x, 'rows', [(i, i ^ mask) for i in range(count)])  18 us
    all_to_all x1, blocking collectives, local(): lax.all_to_all(curv, 'rows', 0, 0, tiled=True)  10.4 us
    ppermute x14, waiting for transfers between devices, exchange(): return lax.ppermute(x, 'rows', [(i, i ^ mask) for i in range(count)])  2.67 us
    unnamed x18, local copies, waits for them, and re-layouts  2.63 us
  transfers between devices with their start and end apart: 14, of which 3 were waited for; matrix products, arithmetic and copies ran while one was open for 0% of the time, Pallas kernels for 37%

profile of v5, /device:TPU:0, one launch (start us, length us, event | category | flops | bytes accessed | tf_op | source)
XLA Modules:
  0.0 63.7 jit_solution(3800350771631786725)
XLA Ops:
  0.6 5.1 %collective-permute-start.5 = (bf16[64,1024]{1,0:T(8,128)(2,1)}, bf16[64,1024]{1,0:T(8,128)(2,1)S(1)}, u32[]{:S(2)}, u32[]{:S(2)}) collective-permute-start(bf16[64,1024]{1,0:T(8,128)(2,1)} %own_ref.3), channel_id=1, source_target_pairs={{0,12},{1,13},{2,14},{3,15},{4,8},{5,9},{6,10},{7,11},{8,4},{9,5},... | collective-permute-start | bytes 393224 | tf_op jit(solution)/shard_map/ppermute | solution.py:263
  6.4 0.9 %copy-done.1 = bf16[64,1024]{1,0:T(8,128)(2,1)S(1)} copy-done((bf16[64,1024]{1,0:T(8,128)(2,1)S(1)}, bf16[64,1024]{1,0:T(8,128)(2,1)}, u32[]{:S(2)}) %copy-start.1) | copy-done | bytes 131096
  7.3 0.8 %copy-done.3 = f32[8,1024]{1,0:T(8,128)S(1)} copy-done((f32[8,1024]{1,0:T(8,128)S(1)}, f32[8,1024]{1,0:T(8,128)}, u32[]{:S(2)}) %copy-start.3) | copy-done | bytes 32792
  8.1 0.9 %copy-done.8 = bf16[64,1024]{1,0:T(8,128)(2,1)S(1)} copy-done((bf16[64,1024]{1,0:T(8,128)(2,1)S(1)}, bf16[64,1024]{1,0:T(8,128)(2,1)}, u32[]{:S(2)}) %copy-start.8) | copy-done | bytes 131096
  9.0 1.6 %cross.1 = (bf16[1024,1024]{1,0:T(8,128)(2,1)S(1)}, bf16[1024,1024]{1,0:T(8,128)(2,1)S(1)}, f32[8,1152]{1,0:T(8,128)S(1)}) custom-call(bf16[64,1024]{1,0:T(8,128)(2,1)S(1)} %copy-done.1, bf16[64,1024]{1,0:T(8,128)(2,1)S(1)} %copy-done.8, f32[8,1024]{1,0:T(8,128)S(1)} %copy-done.3), custom_call_target="tpu_custom_call" | custom-call | flops 2684354560 | tf_op jit(solution)/shard_map/cross/pallas_call | solution.py:317
  10.7 1.2 %collective-permute-done.refs_1_ = f32[8,1152]{1,0:T(8,128)S(1)} collective-permute-done((f32[8,1152]{1,0:T(8,128)S(1)}, f32[8,1152]{1,0:T(8,128)S(1)}, u32[]{:S(2)}, u32[]{:S(2)}) %collective-permute-start) | collective-permute-done | bytes 36896 | tf_op jit(solution)/shard_map/ppermute | solution.py:263
  11.9 1.7 %collective-permute-start.1 = (f32[8,1152]{1,0:T(8,128)S(1)}, f32[8,1152]{1,0:T(8,128)S(1)}, u32[]{:S(2)}, u32[]{:S(2)}) collective-permute-start(f32[8,1152]{1,0:T(8,128)S(1)} %add.3.refs_0_.refs_1_), channel_id=1, source_target_pairs={{0,2},{1,3},{2,0},{3,1},{4,6},{5,7},{6,4},{7,5},{8,10},{9,11},{10,... | collective-permute-start | bytes 110600 | tf_op jit(solution)/shard_map/ppermute | solution.py:263
  13.6 4.0 %inverse.1.refs_0_.refs_2_ = f32[1024,128]{1,0:T(8,128)S(1)} custom-call(f32[8,1152]{1,0:T(8,128)S(1)} %add.3.refs_0_.refs_1_, f32[1024,1024]{1,0:T(8,128)S(1)} %copy-done), custom_call_target="tpu_custom_call" | custom-call | flops 536870912 | tf_op jit(solution)/shard_map/inverse/pallas_call | solution.py:317
  17.7 0.9 %collective-permute-start.7 = (bf16[64,4096]{1,0:T(8,128)(2,1)S(1)}, bf16[64,4096]{1,0:T(8,128)(2,1)S(1)}, u32[]{:S(2)}, u32[]{:S(2)}) collective-permute-start(bf16[64,4096]{1,0:T(8,128)(2,1)S(1)} %join.6.refs_3_.refs_1_), channel_id=1, source_target_pairs={{0,2},{1,3},{2,0},{3,1},{4,6},{5,7},{6,4},{7,5},{8,10},{9,11},{10,... | collective-permute-start | bytes 1572872 | tf_op jit(solution)/shard_map/ppermute | solution.py:263
  19.3 0.9 %collective-permute-start.2 = (f32[8,1152]{1,0:T(8,128)S(1)}, f32[8,1152]{1,0:T(8,128)S(1)}, u32[]{:S(2)}, u32[]{:S(2)}) collective-permute-start(f32[8,1152]{1,0:T(8,128)S(1)} %add.4.refs_0_.refs_1_), channel_id=1, source_target_pairs={{0,4},{1,5},{2,6},{3,7},{4,0},{5,1},{6,2},{7,3},{8,12},{9,13},{10,... | collective-permute-start | bytes 110600 | tf_op jit(solution)/shard_map/ppermute | solution.py:263
  20.3 2.6 %merge.1 = (bf16[1024,512]{1,0:T(8,128)(2,1)S(1)}, bf16[1024,512]{1,0:T(8,128)(2,1)S(1)}, bf16[1024,512]{1,0:T(8,128)(2,1)S(1)}, bf16[512,512]{1,0:T(8,128)(2,1)...) custom-call(f32[8,1152]{1,0:T(8,128)S(1)} %add.4.refs_0_.refs_1_, f32[1024,1024]{1,0:T(8,128)S(1)} %copy-done, ...), custom_call_target="tpu_custom_call" | custom-call | flops 1073741824 | tf_op jit(solution)/shard_map/merge/pallas_call | solution.py:317
  23.4 2.5 %collective-permute-start.6 = (f32[8,1152]{1,0:T(8,128)S(1)}, f32[8,1152]{1,0:T(8,128)S(1)}, u32[]{:S(2)}, u32[]{:S(2)}) collective-permute-start(f32[8,1152]{1,0:T(8,128)S(1)} %add.5.refs_0_.refs_3_), channel_id=1, source_target_pairs={{0,8},{1,9},{2,10},{3,11},{4,12},{5,13},{6,14},{7,15},{8,0},{9,1},... | collective-permute-start | bytes 110600 | tf_op jit(solution)/shard_map/ppermute | solution.py:263
  25.9 2.5 %tiles.3.refs_0_.held_ref = bf16[4096,1024]{1,0:T(8,128)(2,1)S(1)} custom-call(f32[8,1152]{1,0:T(8,128)S(1)} %add.5.refs_0_.refs_3_, bf16[1024,512]{1,0:T(8,128)(2,1)S(1)} %get-tuple-element.25.refs_0_.refs_1_.refs_5_, bf16[64,1024]{1,0:T(8,128)(2,1)S(1)} %copy-done.1, bf16[64,4096]{1,0:T(8,128)(2,1)S(1)} %join.6.refs_3_.refs_1_), custom_call_target="tpu_custom_call" | custom-call | flops 1073741824 | tf_op jit(solution)/shard_map/tiles/pallas_call | solution.py:317
  28.5 4.7 %direction.1 = (f32[8,1024]{1,0:T(8,128)}, f32[8,1024]{1,0:T(8,128)S(1)}, bf16[8,1024]{1,0:T(8,128)(2,1)S(1)}, f32[8,1]{1,0:T(8,128)S(1)}) custom-call(bf16[4096,1024]{1,0:T(8,128)(2,1)S(1)} %tiles.3.refs_0_.held_ref, f32[1]{0:T(128)S(6)} %copy.12.refs_1_.ridge_ref, f32[8]{0:T(128)S(1)} %copy-done.7, f32[8,1152]{1,0:T(8,128)S(1)} %add.5.refs_0_.refs_3_, ...), custom_call_target="tpu_custom_call" | custom-call | flops 3221225472 | tf_op jit(solution)/shard_map/direction/pallas_call | solution.py:317
  33.3 1.3 %collective-permute-start.9 = (bf16[8,1024]{1,0:T(8,128)(2,1)S(1)}, bf16[8,1024]{1,0:T(8,128)(2,1)S(1)}, u32[]{:S(2)}, u32[]{:S(2)}) collective-permute-start(bf16[8,1024]{1,0:T(8,128)(2,1)S(1)} %get-tuple-element.34.refs_1_), channel_id=1, source_target_pairs={{0,4},{1,5},{2,6},{3,7},{4,0},{5,1},{6,2},{7,3},{8,12},{9,13},{10,... | collective-permute-start | bytes 49160 | tf_op jit(solution)/shard_map/ppermute | solution.py:263
  34.6 2.5 %tiles.4.refs_0_ = bf16[4096,1024]{1,0:T(8,128)(2,1)S(1)} custom-call(f32[8,1]{1,0:T(8,128)S(1)} %get-tuple-element.33.refs_0_.refs_1_, bf16[64,1024]{1,0:T(8,128)(2,1)S(1)} %copy-done.2, bf16[64,8192]{1,0:T(8,128)(2,1)S(1)} %join.7.refs_0_.refs_2_), custom_call_target="tpu_custom_call" | custom-call | flops 1073741824 | tf_op jit(solution)/shard_map/tiles/pallas_call | solution.py:317
  37.2 2.7 %collective-permute-start.10 = (bf16[8,2048]{1,0:T(8,128)(2,1)S(1)}, bf16[8,2048]{1,0:T(8,128)(2,1)S(1)}, u32[]{:S(2)}, u32[]{:S(2)}) collective-permute-start(bf16[8,2048]{1,0:T(8,128)(2,1)S(1)} %join.9.refs_0_.refs_1_), channel_id=1, source_target_pairs={{0,8},{1,9},{2,10},{3,11},{4,12},{5,13},{6,14},{7,15},{8,0},{9,1},... | collective-permute-start | bytes 98312 | tf_op jit(solution)/shard_map/ppermute | solution.py:263
  40.0 2.5 %tiles.5.refs_0_.refs_1_ = bf16[4096,1024]{1,0:T(8,128)(2,1)S(1)} custom-call(bf16[8,2048]{1,0:T(8,128)(2,1)S(1)} %join.9.refs_0_.refs_1_, bf16[64,1024]{1,0:T(8,128)(2,1)S(1)} %copy-done.2, bf16[64,16384]{1,0:T(8,128)(2,1)S(1)} %join.8.refs_2_.pts_ref), custom_call_target="tpu_custom_call" | custom-call | flops 1073741824 | tf_op jit(solution)/shard_map/tiles/pallas_call | solution.py:317
  42.6 1.1 %collective-permute-start.13 = (bf16[8,4096]{1,0:T(8,128)(2,1)S(1)}, bf16[8,4096]{1,0:T(8,128)(2,1)S(1)}, u32[]{:S(2)}, u32[]{:S(2)}) collective-permute-start(bf16[8,4096]{1,0:T(8,128)(2,1)S(1)} %join.10.low_ref.refs_1_), channel_id=1, source_target_pairs={{0,3},{1,2},{2,1},{3,0},{4,7},{5,6},{6,5},{7,4},{8,11},{9,10},{10,... | collective-permute-start | bytes 196616 | tf_op jit(solution)/shard_map/ppermute | solution.py:263
  44.5 2.9 %near.1 = (f32[8,1024]{1,0:T(8,128)S(1)}, bf16[3072,1024]{1,0:T(8,128)(2,1)S(1)}) custom-call(bf16[64,1024]{1,0:T(8,128)(2,1)S(1)} %copy-done.2, bf16[64,16384]{1,0:T(8,128)(2,1)S(1)} %join.8.refs_2_.pts_ref, bf16[8,4096]{1,0:T(8,128)(2,1)S(1)} %join.10.low_ref.refs_1_, bf16[4096,1024]{1,0:T(8,128)(2,1)S(1)} %tiles.3.refs_0_.held_ref), custom_call_target="tpu_custom_call" | custom-call | flops 2147483648 | tf_op jit(solution)/shard_map/near/pallas_call | solution.py:317
  47.5 1.0 %collective-permute-done.12.refs_3_ = bf16[8,4096]{1,0:T(8,128)(2,1)S(1)} collective-permute-done((bf16[8,4096]{1,0:T(8,128)(2,1)S(1)}, bf16[8,4096]{1,0:T(8,128)(2,1)S(1)}, u32[]{:S(2)}, u32[]{:S(2)}) %collective-permute-start.12) | collective-permute-done | bytes 65568 | tf_op jit(solution)/shard_map/ppermute | solution.py:263
  48.5 4.0 %image.1 = (f32[8,1024]{1,0:T(8,128)S(1)}, f32[16,1,128]{2,1,0:T(1,128)S(1)}) custom-call(f32[1]{0:T(128)S(6)} %copy.12.refs_1_.ridge_ref, bf16[64,1024]{1,0:T(8,128)(2,1)S(1)} %copy-done.2, bf16[64,16384]{1,0:T(8,128)(2,1)S(1)} %join.8.refs_2_.pts_ref, bf16[8,16384]{1,0:T(8,128)(2,1)S(1)} %join.11.low_ref, f32[8,1024]{1,0:T(8,128)S(1)} %get-tuple-element.36.near_ref, ...), custom_call_target="tpu_custom_call" | custom-call | flops 6442450944 | tf_op jit(solution)/shard_map/image/pallas_call | solution.py:317
  52.6 10.4 %all_to_all.5.refs_0_ = f32[16,1,128]{2,1,0:T(1,128)S(1)} all-to-all(f32[16,1,128]{2,1,0:T(1,128)S(1)} %get-tuple-element.38), channel_id=1, replica_groups=mesh['groups'=2,'rows'=16] {'rows'}, dimensions={0} | all-to-all | bytes 16384 | tf_op jit(solution)/shard_map/all_to_all | solution.py:402
  62.9 0.8 %update.1 = (f32[8,1024]{1,0:T(8,128)}, f32[8,1024]{1,0:T(8,128)}, f32[1,8]{1,0:T(1,128)}) custom-call(f32[16,1,128]{2,1,0:T(1,128)S(1)} %all_to_all.5.refs_0_, f32[8,1]{1,0:T(8,128)S(1)} %get-tuple-element.33.refs_0_.refs_1_, f32[8,1024]{1,0:T(8,128)S(1)} %copy-done.6, f32[8,1024]{1,0:T(8,128)S(1)} %copy-done.4, ...), custom_call_target="tpu_custom_call" | custom-call | tf_op jit(solution)/shard_map/update/pallas_call | solution.py:317
  (42 shorter events, 2.4 us)
Async XLA Ops:
  0.6 13.0 %copy-start = (f32[1024,1024]{1,0:T(8,128)S(1)}, f32[1024,1024]{1,0:T(8,128)}, u32[]{:S(2)}) copy-start(f32[1024,1024]{1,0:T(8,128)} %refs_1_.7) | copy-start | bytes 12582916
  0.6 17.0 %collective-permute-start.5 = (bf16[64,1024]{1,0:T(8,128)(2,1)}, bf16[64,1024]{1,0:T(8,128)(2,1)S(1)}, u32[]{:S(2)}, u32[]{:S(2)}) collective-permute-start(bf16[64,1024]{1,0:T(8,128)(2,1)} %own_ref.3), channel_id=1, source_target_pairs={{0,12},{1,13},{2,14},{3,15},{4,8},{5,9},{6,10},{7,11},{8,4},{9,5},... | collective-permute-start | bytes 393224 | tf_op jit(solution)/shard_map/ppermute | solution.py:263
  5.8 11.9 %collective-permute-start.4 = (bf16[64,1024]{1,0:T(8,128)(2,1)}, bf16[64,1024]{1,0:T(8,128)(2,1)S(1)}, u32[]{:S(2)}, u32[]{:S(2)}) collective-permute-start(bf16[64,1024]{1,0:T(8,128)(2,1)} %own_ref.3), channel_id=1, source_target_pairs={{0,8},{1,9},{2,10},{3,11},{4,12},{5,13},{6,14},{7,15},{8,0},{9,1},... | collective-permute-start | bytes 393224 | tf_op jit(solution)/shard_map/ppermute | solution.py:263
  5.8 11.9 %collective-permute-start.3 = (bf16[64,1024]{1,0:T(8,128)(2,1)}, bf16[64,1024]{1,0:T(8,128)(2,1)S(1)}, u32[]{:S(2)}, u32[]{:S(2)}) collective-permute-start(bf16[64,1024]{1,0:T(8,128)(2,1)} %own_ref.3), channel_id=1, source_target_pairs={{0,4},{1,5},{2,6},{3,7},{4,0},{5,1},{6,2},{7,3},{8,12},{9,13},{10,... | collective-permute-start | bytes 393224 | tf_op jit(solution)/shard_map/ppermute | solution.py:263
  6.4 0.9 %copy-start.1 = (bf16[64,1024]{1,0:T(8,128)(2,1)S(1)}, bf16[64,1024]{1,0:T(8,128)(2,1)}, u32[]{:S(2)}) copy-start(bf16[64,1024]{1,0:T(8,128)(2,1)} %own_ref.3) | copy-start | bytes 393220
  7.3 0.8 %copy-start.3 = (f32[8,1024]{1,0:T(8,128)S(1)}, f32[8,1024]{1,0:T(8,128)}, u32[]{:S(2)}) copy-start(f32[8,1024]{1,0:T(8,128)} %refs_3_.1) | copy-start | bytes 98308
  8.1 0.9 %copy-start.8 = (bf16[64,1024]{1,0:T(8,128)(2,1)S(1)}, bf16[64,1024]{1,0:T(8,128)(2,1)}, u32[]{:S(2)}) copy-start(bf16[64,1024]{1,0:T(8,128)(2,1)} %marks_ref.1) | copy-start | bytes 393220
  10.6 1.3 %collective-permute-start = (f32[8,1152]{1,0:T(8,128)S(1)}, f32[8,1152]{1,0:T(8,128)S(1)}, u32[]{:S(2)}, u32[]{:S(2)}) collective-permute-start(f32[8,1152]{1,0:T(8,128)S(1)} %get-tuple-element.24.refs_0_), channel_id=1, source_target_pairs={{0,1},{1,0},{2,3},{3,2},{4,5},{5,4},{6,7},{7,6},{8,9},{9,8},{10,11... | collective-permute-start | bytes 110600 | tf_op jit(solution)/shard_map/ppermute | solution.py:263
  11.9 5.7 %collective-permute-start.1 = (f32[8,1152]{1,0:T(8,128)S(1)}, f32[8,1152]{1,0:T(8,128)S(1)}, u32[]{:S(2)}, u32[]{:S(2)}) collective-permute-start(f32[8,1152]{1,0:T(8,128)S(1)} %add.3.refs_0_.refs_1_), channel_id=1, source_target_pairs={{0,2},{1,3},{2,0},{3,1},{4,6},{5,7},{6,4},{7,5},{8,10},{9,11},{10,... | collective-permute-start | bytes 110600 | tf_op jit(solution)/shard_map/ppermute | solution.py:263
  17.7 15.4 %collective-permute-start.7 = (bf16[64,4096]{1,0:T(8,128)(2,1)S(1)}, bf16[64,4096]{1,0:T(8,128)(2,1)S(1)}, u32[]{:S(2)}, u32[]{:S(2)}) collective-permute-start(bf16[64,4096]{1,0:T(8,128)(2,1)S(1)} %join.6.refs_3_.refs_1_), channel_id=1, source_target_pairs={{0,2},{1,3},{2,0},{3,1},{4,6},{5,7},{6,4},{7,5},{8,10},{9,11},{10,... | collective-permute-start | bytes 1572872 | tf_op jit(solution)/shard_map/ppermute | solution.py:263
  19.3 4.0 %collective-permute-start.2 = (f32[8,1152]{1,0:T(8,128)S(1)}, f32[8,1152]{1,0:T(8,128)S(1)}, u32[]{:S(2)}, u32[]{:S(2)}) collective-permute-start(f32[8,1152]{1,0:T(8,128)S(1)} %add.4.refs_0_.refs_1_), channel_id=1, source_target_pairs={{0,4},{1,5},{2,6},{3,7},{4,0},{5,1},{6,2},{7,3},{8,12},{9,13},{10,... | collective-permute-start | bytes 110600 | tf_op jit(solution)/shard_map/ppermute | solution.py:263
  22.9 5.6 %copy-start.5 = (f32[8,1024]{1,0:T(8,128)S(1)}, f32[8,1024]{1,0:T(8,128)}, u32[]{:S(2)}) copy-start(f32[8,1024]{1,0:T(8,128)} %refs_14_.1) | copy-start | bytes 98308
  22.9 5.6 %copy-start.7 = (f32[8]{0:T(128)S(1)}, f32[8]{0:T(128)}, u32[]{:S(2)}) copy-start(f32[8]{0:T(128)} %refs_2_.4) | copy-start | bytes 100
  23.4 5.1 %collective-permute-start.6 = (f32[8,1152]{1,0:T(8,128)S(1)}, f32[8,1152]{1,0:T(8,128)S(1)}, u32[]{:S(2)}, u32[]{:S(2)}) collective-permute-start(f32[8,1152]{1,0:T(8,128)S(1)} %add.5.refs_0_.refs_3_), channel_id=1, source_target_pairs={{0,8},{1,9},{2,10},{3,11},{4,12},{5,13},{6,14},{7,15},{8,0},{9,1},... | collective-permute-start | bytes 110600 | tf_op jit(solution)/shard_map/ppermute | solution.py:263
  28.5 6.1 %copy-start.2 = (bf16[64,1024]{1,0:T(8,128)(2,1)S(1)}, bf16[64,1024]{1,0:T(8,128)(2,1)}, u32[]{:S(2)}) copy-start(bf16[64,1024]{1,0:T(8,128)(2,1)} %own_ref.3) | copy-start | bytes 393220
  33.2 6.7 %collective-permute-start.8 = (bf16[64,8192]{1,0:T(8,128)(2,1)S(1)}, bf16[64,8192]{1,0:T(8,128)(2,1)S(1)}, u32[]{:S(2)}, u32[]{:S(2)}) collective-permute-start(bf16[64,8192]{1,0:T(8,128)(2,1)S(1)} %join.7.refs_0_.refs_2_), channel_id=1, source_target_pairs={{0,1},{1,0},{2,3},{3,2},{4,5},{5,4},{6,7},{7,6},{8,9},{9,8},{10,11... | collective-permute-start | bytes 3145736 | tf_op jit(solution)/shard_map/ppermute | solution.py:263
  33.3 3.8 %collective-permute-start.9 = (bf16[8,1024]{1,0:T(8,128)(2,1)S(1)}, bf16[8,1024]{1,0:T(8,128)(2,1)S(1)}, u32[]{:S(2)}, u32[]{:S(2)}) collective-permute-start(bf16[8,1024]{1,0:T(8,128)(2,1)S(1)} %get-tuple-element.34.refs_1_), channel_id=1, source_target_pairs={{0,4},{1,5},{2,6},{3,7},{4,0},{5,1},{6,2},{7,3},{8,12},{9,13},{10,... | collective-permute-start | bytes 49160 | tf_op jit(solution)/shard_map/ppermute | solution.py:263
  37.2 5.4 %collective-permute-start.10 = (bf16[8,2048]{1,0:T(8,128)(2,1)S(1)}, bf16[8,2048]{1,0:T(8,128)(2,1)S(1)}, u32[]{:S(2)}, u32[]{:S(2)}) collective-permute-start(bf16[8,2048]{1,0:T(8,128)(2,1)S(1)} %join.9.refs_0_.refs_1_), channel_id=1, source_target_pairs={{0,8},{1,9},{2,10},{3,11},{4,12},{5,13},{6,14},{7,15},{8,0},{9,1},... | collective-permute-start | bytes 98312 | tf_op jit(solution)/shard_map/ppermute | solution.py:263
  42.6 4.9 %collective-permute-start.13 = (bf16[8,4096]{1,0:T(8,128)(2,1)S(1)}, bf16[8,4096]{1,0:T(8,128)(2,1)S(1)}, u32[]{:S(2)}, u32[]{:S(2)}) collective-permute-start(bf16[8,4096]{1,0:T(8,128)(2,1)S(1)} %join.10.low_ref.refs_1_), channel_id=1, source_target_pairs={{0,3},{1,2},{2,1},{3,0},{4,7},{5,6},{6,5},{7,4},{8,11},{9,10},{10,... | collective-permute-start | bytes 196616 | tf_op jit(solution)/shard_map/ppermute | solution.py:263
  43.7 4.8 %collective-permute-start.12 = (bf16[8,4096]{1,0:T(8,128)(2,1)S(1)}, bf16[8,4096]{1,0:T(8,128)(2,1)S(1)}, u32[]{:S(2)}, u32[]{:S(2)}) collective-permute-start(bf16[8,4096]{1,0:T(8,128)(2,1)S(1)} %join.10.low_ref.refs_1_), channel_id=1, source_target_pairs={{0,2},{1,3},{2,0},{3,1},{4,6},{5,7},{6,4},{7,5},{8,10},{9,11},{10,... | collective-permute-start | bytes 196616 | tf_op jit(solution)/shard_map/ppermute | solution.py:263
  44.3 4.2 %collective-permute-start.11 = (bf16[8,4096]{1,0:T(8,128)(2,1)S(1)}, bf16[8,4096]{1,0:T(8,128)(2,1)S(1)}, u32[]{:S(2)}, u32[]{:S(2)}) collective-permute-start(bf16[8,4096]{1,0:T(8,128)(2,1)S(1)} %join.10.low_ref.refs_1_), channel_id=1, source_target_pairs={{0,1},{1,0},{2,3},{3,2},{4,5},{5,4},{6,7},{7,6},{8,9},{9,8},{10,11... | collective-permute-start | bytes 196616 | tf_op jit(solution)/shard_map/ppermute | solution.py:263
  48.5 14.4 %copy-start.4 = (f32[8,1024]{1,0:T(8,128)S(1)}, f32[8,1024]{1,0:T(8,128)}, u32[]{:S(2)}) copy-start(f32[8,1024]{1,0:T(8,128)} %refs_3_.1) | copy-start | bytes 98308
  48.5 14.4 %copy-start.6 = (f32[8,1024]{1,0:T(8,128)S(1)}, f32[8,1024]{1,0:T(8,128)}, u32[]{:S(2)}) copy-start(f32[8,1024]{1,0:T(8,128)} %refs_2_.5) | copy-start | bytes 98308
